TPU v7x, 32 devices: a whole 2x2x4 slice. The times are simulated.
32 devices in a mesh: gx: 8 (over y, x, core), col: 4 (over z).
Axes of the slice: x: 2, y: 2, z: 4, core: 2. Of those that a mesh axis runs over, the one named last changes fastest.
Arguments:
- field: bfloat16 [32, 16, 128, 256], P('col', 'gx'), may hold values from -6 to 6
- kernel: bfloat16 [64, 32, 3, 3, 3], replicated, may hold values from -0.21875 to 0.21875
- bias: float32 [64], P('col'), may hold values from -3 to 3
- cotangent: bfloat16 [64, 8, 64, 128], P('col', 'gx'), may hold values from -6 to 6
Outputs:
- out_act: bfloat16 [64, 8, 64, 128], P('col', 'gx')
- in_grad: bfloat16 [32, 16, 128, 256], P('col', 'gx')
All inputs are finite; a program needn't handle non-finite values.
Results may differ from a plain program's by a relative error of at most 0.014.
Values may be sent and summed in bfloat16 or wider, within the bound.
No kernel may reach another device: no remote copies, remote signals or barrier semaphores. Data moves between devices by JAX's collectives and lax.ppermute only.
A program may use at most 128 MiB of HBM per device.

v0:
```python
import jax
import jax.numpy as jnp
from jax import lax
from jax.sharding import PartitionSpec as P


def from_behind(block, axis, distance):
    devices = range(lax.axis_size(axis))
    route = [((i - distance) % len(devices), i) for i in devices]
    return lax.ppermute(block, axis, route)


def parity_views(values):
    chans, planes, span_y, span_z = values.shape
    half_z = span_z // 2
    source_idx = lax.broadcasted_iota(jnp.int32, (span_z, span_z), 0)
    target_idx = lax.broadcasted_iota(jnp.int32, (span_z, span_z), 1)
    select = (source_idx == 2 * (target_idx % half_z) + target_idx // half_z).astype(values.dtype)
    split_z = jnp.einsum(
        "cpyz,zm->cpym", values, select, preferred_element_type=jnp.float32
    ).astype(values.dtype)
    split_y = split_z.reshape(chans, planes, span_y // 2, 2, span_z)
    y_parts = [jnp.roll(split_y[:, :, :, 1], 1, axis=2), split_y[:, :, :, 0], split_y[:, :, :, 1]]
    views = []
    for part in y_parts:
        even_z = part[..., :half_z]
        odd_z = part[..., half_z:]
        views.append([jnp.roll(odd_z, 1, axis=3), even_z, odd_z])
    return views


def conv_taps(extended, weights, planes):
    views = parity_views(extended)
    span_y = extended.shape[2]
    span_z = extended.shape[3]
    summed = jnp.zeros((weights.shape[0], planes, span_y // 2, span_z // 2), jnp.float32)
    for tap_x in range(3):
        for tap_y in range(3):
            for tap_z in range(3):
                window = views[tap_y][tap_z][:, tap_x : tap_x + 2 * planes - 1 : 2]
                summed = summed + jnp.einsum(
                    "oc,cpyz->opyz",
                    weights[:, :, tap_x, tap_y, tap_z],
                    window,
                    preferred_element_type=jnp.float32,
                )
    return summed


def transpose_taps(grad_ext, weights):
    half_planes = grad_ext.shape[1] - 1
    half_z = grad_ext.shape[3]
    sources = []
    for offset_y in range(2):
        row_list = []
        for offset_z in range(2):
            moved = grad_ext
            if offset_y == 1:
                moved = jnp.roll(moved, -1, axis=2)
            if offset_z == 1:
                moved = jnp.roll(moved, -1, axis=3)
            row_list.append(moved)
        sources.append(row_list)
    tap_lists = (((1, 0),), ((0, 1), (2, 0)))
    out_shape = (weights.shape[1], half_planes, grad_ext.shape[2], half_z)
    source_idx = lax.broadcasted_iota(jnp.int32, (2 * half_z, 2 * half_z), 0)
    target_idx = lax.broadcasted_iota(jnp.int32, (2 * half_z, 2 * half_z), 1)
    weave = (source_idx == target_idx % 2 * half_z + target_idx // 2).astype(jnp.float32)
    layers_x = []
    for parity_x in range(2):
        layers_y = []
        for parity_y in range(2):
            layers_z = []
            for parity_z in range(2):
                summed = jnp.zeros(out_shape, jnp.float32)
                for tap_x, offset_x in tap_lists[parity_x]:
                    for tap_y, offset_y in tap_lists[parity_y]:
                        for tap_z, offset_z in tap_lists[parity_z]:
                            source = sources[offset_y][offset_z][
                                :, offset_x : offset_x + half_planes
                            ]
                            summed = summed + jnp.einsum(
                                "oc,opyz->cpyz",
                                weights[:, :, tap_x, tap_y, tap_z],
                                source,
                                preferred_element_type=jnp.float32,
                            )
                layers_z.append(summed)
            joined = jnp.concatenate(layers_z, axis=3)
            layers_y.append(
                jnp.einsum(
                    "cpym,mz->cpyz",
                    joined,
                    weave,
                    precision=lax.Precision.HIGHEST,
                    preferred_element_type=jnp.float32,
                )
            )
        layers_x.append(jnp.stack(layers_y, axis=3))
    woven = jnp.stack(layers_x, axis=2)
    return woven.reshape(out_shape[0], 2 * half_planes, 2 * out_shape[2], 2 * half_z)


def on_device(field, kernel, bias, cotangent):
    ci_dev = field.shape[0]
    co_dev = bias.shape[0]
    half_planes = field.shape[1] // 2
    group = lax.axis_index("col")
    below_plane = from_behind(field[:, -1:], "gx", 1)
    extended = jnp.concatenate([below_plane, field], axis=1)
    own_out = lax.dynamic_slice_in_dim(kernel, group * co_dev, co_dev, 0)
    own_in = lax.dynamic_slice_in_dim(kernel, group * ci_dev, ci_dev, 1)
    gathered = lax.all_gather(extended, "col", axis=0, tiled=True)
    sums = conv_taps(gathered, own_out, half_planes)
    pre = sums + bias[:, None, None, None]
    out_act = (0.3 * pre + 0.7 * jax.nn.softplus(pre)).astype(jnp.bfloat16)
    masked = (cotangent.astype(jnp.float32) * (0.3 + 0.7 * jax.nn.sigmoid(pre))).astype(
        jnp.bfloat16
    )
    above_plane = from_behind(masked, "gx", -1)
    grad_ext = jnp.concatenate([masked, above_plane], axis=1)
    all_grad = lax.all_gather(grad_ext, "col", axis=0, tiled=True)
    grad_sums = transpose_taps(all_grad, own_in)
    return (out_act, grad_sums.astype(jnp.bfloat16))


def solution(mesh):
    in_specs = (P("col", "gx", None, None), P(), P("col"), P("col", "gx", None, None))
    out_specs = (P("col", "gx", None, None), P("col", "gx", None, None))
    return jax.shard_map(
        on_device, mesh=mesh, in_specs=in_specs, out_specs=out_specs, check_vma=False
    )
```

profile of v0, /device:TPU:11, one launch (start us, length us, event | category | flops | bytes accessed | tf_op | source)
XLA Modules:
  0.0 261.9 jit_solution(14912959925093196991)
XLA Ops:
  7.2 1.1 slice.406
  8.4 1.8 collective-permute-start
  10.2 6.1 %collective-permute-done = bf16[8,1,128,256]{3,2,1,0:T(8,128)(2,1)S(1)} collective-permute-done((bf16[8,1,128,256]{3,2,1,0:T(8,128)(2,1)S(1)}, bf16[8,1,128,256]{3,2,1,0:T(8,128)(2,1)S(1)}, u32[]{:S(2)}, u32[]{:S(2)}) %collective-permute-start) | collective-permute-done | bytes 524320 | tf_op jit(solution)/shard_map/ppermute | solution.py:10
  16.3 2.5 pad_maximum_fusion
  18.9 114.5 %all-gather.3.cloned.1.call-done = bf16[32,3,128,256]{3,2,1,0:T(8,128)(2,1)} async-done(((bf16[8,3,128,256]{3,2,1,0:T(8,128)(2,1)}), bf16[32,3,128,256]{3,2,1,0:T(8,128)(2,1)}) %all-gather.3.cloned.1.call-update) | async-done | bytes 6291472 | tf_op jit(solution)/shard_map/all_gather | solution.py:113
  133.4 7.2 %convolution_convert_fusion = bf16[32,3,128,256]{3,2,1,0:T(8,128)(2,1)} fusion(bf16[32,3,128,256]{3,2,1,0:T(8,128)(2,1)} %all-gather.3.cloned.1.call-done, s32[256]{0:T(256)S(1)} %get-tuple-element.18, s32[256]{0:T(256)S(1)} %get-tuple-element.21, s32[256]{0:T(256)S(1)} %get-tuple-element.19, s32[256]{0:T(256)S(1)} %get-tuple-element.20, ...), kind=kOutput, calls=%fused_computation.10 | convolution fusion | flops 1614086144 | bytes 12587520 | tf_op jit(solution)/shard_map/cpyz,zm->cpym/dot_general | solution.py:19
  140.7 10.1 %reshape.279 = bf16[32,3,64,2,256]{4,3,2,1,0:T(2,128)(2,1)} reshape(bf16[32,3,128,256]{3,2,1,0:T(8,128)(2,1)} %convolution_convert_fusion) | data formatting | bytes 12582912 | tf_op jit(solution)/shard_map/reshape | solution.py:22
  150.8 14.7 %fusion.241 = (bf16[32,3,64,1,256]{4,3,2,1,0:T(2,128)(2,1)S(1)}, bf16[32,3,64,1,256]{4,3,2,1,0:T(2,128)(2,1)S(1)}) fusion(bf16[32,3,64,2,256]{4,3,2,1,0:T(2,128)(2,1)} %reshape.279), kind=kLoop, calls=%fused_computation.344 | loop fusion | bytes 12582912 | tf_op jit(solution)/shard_map/slice | solution.py:23
  165.5 3.4 %copy.82 = bf16[32,3,64,1,256]{4,0,2,1,3:T(8,128)(2,1)S(1)} copy(bf16[32,3,64,1,256]{4,3,2,1,0:T(2,128)(2,1)S(1)} %get-tuple-element.9) | data formatting | bytes 6291456
  168.9 0.4 slice.513
  169.5 0.5 fusion.2
  170.0 3.4 %copy.81 = bf16[32,3,64,1,256]{4,0,2,1,3:T(8,128)(2,1)S(1)} copy(bf16[32,3,64,1,256]{4,3,2,1,0:T(2,128)(2,1)S(1)} %get-tuple-element.8) | data formatting | bytes 6291456
  173.4 0.5 slice.525
  174.0 0.4 slice.526
  174.3 0.5 slice.531
  174.8 0.4 slice.532
  175.2 0.4 fusion.61
  176.3 0.4 convolution_add_fusion.23
  177.4 0.4 convolution_add_fusion.20
  177.8 0.3 convolution_add_fusion.19
  178.2 0.5 convolution_add_fusion.18
  178.7 0.4 convolution_add_fusion.17
  179.9 0.4 convolution_add_fusion.14
  181.0 0.4 convolution_add_fusion.11
  182.1 0.4 convolution_add_fusion.8
  183.2 0.4 convolution_add_fusion.5
  183.9 0.3 convolution_add_fusion.3
  184.3 0.4 convolution_add_fusion.2
  184.7 0.3 convolution_add_fusion.1
  185.2 0.5 fusion.78
  185.8 0.7 collective-permute-start.1
  186.5 6.0 %collective-permute-done.1 = bf16[16,1,64,128]{3,0,2,1:T(8,128)(2,1)S(1)} collective-permute-done((bf16[16,1,64,128]{3,0,2,1:T(8,128)(2,1)S(1)}, bf16[16,1,64,128]{3,0,2,1:T(8,128)(2,1)S(1)}, u32[]{:S(2)}, u32[]{:S(2)}) %collective-permute-start.1) | collective-permute-done | bytes 262176 | tf_op jit(solution)/shard_map/ppermute | solution.py:10
  192.5 0.8 pad_maximum_fusion.9
  193.4 0.3 fusion.83
  193.8 0.8 copy.37
  194.6 43.1 %all-gather.5.cloned.1.call-done = bf16[64,2,64,128]{3,0,2,1:T(8,128)(2,1)} async-done(((bf16[16,2,64,128]{3,0,2,1:T(8,128)(2,1)}), bf16[64,2,64,128]{3,0,2,1:T(8,128)(2,1)}) %all-gather.5.cloned.1.call-update) | async-done | bytes 2097168 | tf_op jit(solution)/shard_map/all_gather | solution.py:122
  237.7 1.9 slice.562
  240.0 0.7 fusion.1
  241.1 0.7 fusion.154
  241.8 0.7 fusion.23
  242.4 0.7 slice.558
  243.1 1.2 fusion.21
  246.4 0.5 fusion.5
  246.9 0.5 fusion.6
  249.3 0.5 fusion.7
  251.1 0.7 convolution_add_fusion.29
  252.9 0.5 fusion.8
  253.8 1.2 copy.38
  (69 shorter events, 12.5 us)
Async XLA Ops:
  7.2 168.1 %copy-start = (bf16[64,32,3,3,3]{0,1,4,3,2:T(8,128)(2,1)S(1)}, bf16[64,32,3,3,3]{0,1,4,3,2:T(8,128)(2,1)}, u32[]{:S(2)}) copy-start(bf16[64,32,3,3,3]{0,1,4,3,2:T(8,128)(2,1)} %param.5) | copy-start | bytes 331780
  7.2 126.3 %all-gather.3.cloned.1.call-start = ((), (), s32[]{:S(2)}) async-start(), calls=%async_computation | async-start | bytes 7864320 | tf_op jit(solution)/shard_map/all_gather | solution.py:113
  8.4 8.0 %collective-permute-start = (bf16[8,1,128,256]{3,2,1,0:T(8,128)(2,1)S(1)}, bf16[8,1,128,256]{3,2,1,0:T(8,128)(2,1)S(1)}, u32[]{:S(2)}, u32[]{:S(2)}) collective-permute-start(bf16[8,1,128,256]{3,2,1,0:T(8,128)(2,1)S(1)} %slice.406), channel_id=1, source_target_pairs={{28,0},{0,4},{4,8},{8,12},{12,16},{16,20},{20,24},{24,28},{29,1},{... | collective-permute-start | bytes 1572872 | tf_op jit(solution)/shard_map/ppermute | solution.py:10
  18.8 218.8 %all-gather.5.cloned.1.call-start = ((), (), s32[]{:S(2)}) async-start(), calls=%async_computation.1 | async-start | bytes 2621440 | tf_op jit(solution)/shard_map/all_gather | solution.py:122
  184.3 1.0 copy-start.2
  184.3 0.9 copy-start.3
  185.8 6.7 %collective-permute-start.1 = (bf16[16,1,64,128]{3,0,2,1:T(8,128)(2,1)S(1)}, bf16[16,1,64,128]{3,0,2,1:T(8,128)(2,1)S(1)}, u32[]{:S(2)}, u32[]{:S(2)}) collective-permute-start(bf16[16,1,64,128]{3,0,2,1:T(8,128)(2,1)S(1)} %get-tuple-element.12), channel_id=1, source_target_pairs={{4,0},{8,4},{12,8},{16,12},{20,16},{24,20},{28,24},{0,28},{5,1},{9... | collective-permute-start | bytes 786440 | tf_op jit(solution)/shard_map/ppermute | solution.py:10
  237.7 2.2 copy-start.1
Sparse Core Ops, SparseCore 0:
  19.0 114.4 all-gather.2
  193.5 44.1 all-gather.4
where the time goes:
time: 267 us; the launch traced here: 262 us
  waiting for transfers between devices  170 us (64%)
  local copies, waits for them, and re-layouts  40.5 us (15%)
  matrix products  27.5 us (10%)
  between operations  14.5 us (5%)
  other arithmetic  6.93 us (3%)
    all_gather x1, waiting for transfers between devices, on_device(): gathered = lax.all_gather(extended, 'col', axis=0, tiled=True)  115 us
    all_gather x1, waiting for transfers between devices, on_device(): all_grad = lax.all_gather(grad_ext, 'col', axis=0, tiled=True)  43.1 us
    slice x1, local copies, waits for them, and re-layouts, parity_views(): split_y[:, :, :, 0]  14.7 us
    ppermute x2, waiting for transfers between devices, from_behind(): return lax.ppermute(block, axis, route)  12.1 us
    dot_general x27, matrix products, conv_taps(): jnp.einsum('oc,cpyz->opyz', weights[:, :, tap_x, tap_y, tap_z], window, p...  10.2 us
    reshape x1, local copies, waits for them, and re-layouts, parity_views(): split_y = split_z.reshape(chans, planes, span_y // 2, 2, span_z)  10.1 us
    unnamed x12, local copies, waits for them, and re-layouts  9.26 us
    dot_general x27, matrix products, transpose_taps(): jnp.einsum('oc,opyz->cpyz', weights[:, :, tap_x, tap_y, tap_z], source, p...  8.01 us
  transfers between devices with their start and end apart: 4, of which 4 were waited for; matrix products, arithmetic and copies ran while one was open for 0% of the time, Pallas kernels for 0%

commit v1 on v0

v1 whole, which is shorter than its diff:
```python
import functools

import jax
import jax.numpy as jnp
from jax import lax
from jax.experimental import pallas as pl
from jax.experimental.pallas import tpu as pltpu
from jax.sharding import PartitionSpec as P

F32 = jnp.float32
BF16 = jnp.bfloat16
LANES = 128
ROWS = 16
PARAMS = pltpu.CompilerParams(vmem_limit_bytes=24 * 1024 * 1024)


def shifted(block, axis, distance):
    count = lax.axis_size(axis)
    return lax.ppermute(block, axis, [(i, (i + distance) % count) for i in range(count)])


def one_hot(shape, rule):
    rows = lax.broadcasted_iota(jnp.int32, shape, 0)
    cols = lax.broadcasted_iota(jnp.int32, shape, 1)
    return jnp.where(rule(rows, cols), 1.0, 0.0).astype(BF16)


def dot(left, right):
    return jnp.dot(left, right, preferred_element_type=F32)


def fill_taps(plane_of, chans, span_y, span_z, taps_ref, first_row):
    half_z = span_z // 2
    size = chans * ROWS
    swap = one_hot((size, size), lambda r, c: c == (r % chans) * ROWS + r // chans)
    split = one_hot(
        (span_z, 3 * half_z),
        lambda z, m: z == (2 * (m % half_z) + m // half_z + span_z - 1) % span_z,
    )
    pair = 2 * chans
    for block in range(span_y // ROWS):
        swapped = dot(swap, plane_of(block)).astype(BF16)
        tapped = dot(swapped, split).astype(BF16)
        for j in range(ROWS // 2):
            half_y = block * (ROWS // 2) + j
            for tap in range(3):
                tile = tapped[j * pair : (j + 1) * pair, tap * half_z : (tap + 1) * half_z]
                row = first_row + tap * pair
                lane = (1 + half_y) * half_z
                taps_ref[row : row + pair, lane : lane + half_z] = tile
                if half_y == span_y // 2 - 1:
                    taps_ref[row : row + pair, 0:half_z] = tile


def tap_sums(weights, taps_ref, lane, width, half_z):
    before = taps_ref[:, lane : lane + width]
    here = taps_ref[:, lane + half_z : lane + half_z + width]
    return dot(weights, jnp.concatenate([before, here], axis=0))


def local_kernel(field_ref, weight_ref, acc_ref, taps_ref):
    chans, planes, span_y, span_z = field_ref.shape
    half_z = span_z // 2
    for plane in range(planes):
        def plane_of(block, plane=plane):
            rows = field_ref[:, plane, block * ROWS : (block + 1) * ROWS, :]
            return rows.reshape(chans * ROWS, span_z)

        fill_taps(plane_of, chans, span_y, span_z, taps_ref, plane * 6 * chans)
    weights = weight_ref[...]
    width = 8 * half_z
    for step in range(span_y // 16):
        lane = step * width
        acc_ref[:, lane : lane + width] = tap_sums(weights, taps_ref, lane, width, half_z)


def halo_kernel(halo_ref, weight_ref, acc_ref, parts_ref, taps_ref):
    chans, span_y, span_z = halo_ref.shape
    half_z = span_z // 2

    def plane_of(block):
        return halo_ref[:, block * ROWS : (block + 1) * ROWS, :].reshape(chans * ROWS, span_z)

    fill_taps(plane_of, chans, span_y, span_z, taps_ref, 0)
    weights = weight_ref[...]
    peers, _, rows, _ = parts_ref.shape
    width = 8 * half_z
    for step in range(span_y // 16):
        lane = step * width
        sums = acc_ref[:, lane : lane + width] + tap_sums(weights, taps_ref, lane, width, half_z)
        sums = sums.astype(BF16)
        for j in range(8):
            for peer in range(peers):
                parts_ref[peer, step * 8 + j] = sums[
                    peer * rows : (peer + 1) * rows, j * half_z : (j + 1) * half_z
                ]


def act_kernel(*refs):
    *part_refs, bias_ref, cot_ref, out_ref, masked_ref = refs
    pre = bias_ref[...] + functools.reduce(
        lambda a, b: a + b, [ref[...].astype(F32) for ref in part_refs]
    )
    small = jnp.exp(-jnp.abs(pre))
    soft = jnp.maximum(pre, 0.0) + jnp.log(1.0 + small)
    out_ref[...] = (0.3 * pre + 0.7 * soft).astype(BF16)
    gate = jnp.where(pre >= 0.0, 1.0, small) / (1.0 + small)
    masked_ref[...] = (cot_ref[...].astype(F32) * (0.3 + 0.7 * gate)).astype(BF16)


def grad_kernel(*refs):
    *piece_refs, weight_ref, grad_ref, held_ref = refs
    chans, _, span_y, span_z = grad_ref.shape
    half_y, half_z = span_y // 2, span_z // 2
    for index, ref in enumerate(piece_refs):
        row = index * ROWS
        for j in range(half_y):
            tile = ref[j]
            held_ref[row : row + ROWS, j * half_z : (j + 1) * half_z] = tile
            if j == 0:
                held_ref[row : row + ROWS, half_y * half_z :] = tile
    size = chans * ROWS
    swap = one_hot((size, size), lambda r, c: c == (r % ROWS) * chans + r // ROWS)
    weave = one_hot((span_z, span_z), lambda m, z: z == 2 * (m % half_z) + m // half_z)
    weights = weight_ref[...]
    pair = 2 * chans
    width = 8 * half_z
    for step in range(half_y // 8):
        lane = step * width
        here = held_ref[:, lane : lane + width]
        after = held_ref[:, lane + half_z : lane + half_z + width]
        sums = dot(weights, jnp.concatenate([here, after], axis=0))
        for parity_x in range(2):
            base = parity_x * 3 * pair
            rows = []
            for j in range(8):
                tile = sums[base : base + 3 * pair, j * half_z : (j + 1) * half_z]
                even = tile[:pair]
                odd = tile[pair : 2 * pair] + pltpu.roll(tile[2 * pair :], half_z - 1, 1)
                rows.append(jnp.concatenate([even.astype(BF16), odd.astype(BF16)], axis=1))
            swapped = dot(swap, jnp.concatenate(rows, axis=0)).astype(BF16)
            woven = dot(swapped, weave).astype(BF16)
            for chan in range(chans):
                grad_ref[chan, parity_x, step * ROWS : (step + 1) * ROWS, :] = woven[
                    chan * ROWS : (chan + 1) * ROWS
                ]


def forward_weights(own):
    peers, rows, cin = own.shape[:3]
    lead = jnp.pad(own, ((0, 0),) * 4 + ((1, 0), (0, 0)))
    lead = lead.reshape(*lead.shape[:4], 2, 2, 3)
    cols = jnp.transpose(lead, (0, 1, 4, 3, 6, 5, 2))
    local = cols[:, :, :, 1:].reshape(peers * rows, 2 * 2 * 3 * 2 * cin)
    halo = cols[:, :, :, :1].reshape(peers * rows, 2 * 1 * 3 * 2 * cin)
    return local, halo


def backward_weights(own):
    peers, rows, cin = own.shape[:3]
    none = jnp.zeros_like(own[:, :, :, 0])
    by_x = jnp.stack(
        [
            jnp.stack([own[:, :, :, 1], none]),
            jnp.stack([own[:, :, :, 2], own[:, :, :, 0]]),
        ]
    )
    none = jnp.zeros_like(by_x[..., 0, :])
    by_y = jnp.stack(
        [
            jnp.stack([by_x[..., 1, :], none]),
            jnp.stack([by_x[..., 2, :], by_x[..., 0, :]]),
        ]
    )
    by_z = jnp.stack([by_y[..., 1], by_y[..., 2], by_y[..., 0]])
    turned = jnp.transpose(by_z, (3, 0, 1, 7, 2, 4, 5, 6))
    return turned.reshape(2 * 3 * 2 * cin, 2 * 2 * peers * rows)


def on_device(field, kernel, bias, cotangent):
    peers = lax.axis_size("col")
    me = lax.axis_index("col")
    cin, planes, span_y, span_z = field.shape
    cout = bias.shape[0]
    half_y, half_z = span_y // 2, span_z // 2
    halo = shifted(field[:, planes - 1], "gx", 1)

    chans = -(-cin // 8) * 8
    rows = -(-cout // ROWS) * ROWS
    own = lax.dynamic_slice_in_dim(kernel, me * cin, cin, 1)
    own = own.reshape(peers, cout, cin, 3, 3, 3)
    twice = jnp.concatenate([own, own], axis=0)
    ahead = lax.dynamic_slice_in_dim(twice, me, peers, 0)
    behind = lax.dynamic_slice_in_dim(twice[::-1], peers - 1 - me, peers, 0)
    fill_w = ((0, 0), (0, rows - cout), (0, chans - cin), (0, 0), (0, 0), (0, 0))
    ahead, behind = jnp.pad(ahead, fill_w), jnp.pad(behind, fill_w)
    fill_c = (0, chans - cin)
    field_p = jnp.pad(field, (fill_c, (0, 0), (0, 0), (0, 0)))
    halo_p = jnp.pad(halo, (fill_c, (0, 0), (0, 0)))
    weights_local, weights_halo = forward_weights(ahead)

    total = peers * rows
    acc = pl.pallas_call(
        local_kernel,
        out_shape=jax.ShapeDtypeStruct((total, half_y * half_z), F32),
        scratch_shapes=[pltpu.VMEM((planes * 6 * chans, (1 + half_y) * half_z), BF16)],
        compiler_params=PARAMS,
        cost_estimate=pl.CostEstimate(
            flops=2 * total * 24 * chans * half_y * half_z, bytes_accessed=1 << 22, transcendentals=0
        ),
        name="local_planes",
    )(field_p, weights_local)
    parts = pl.pallas_call(
        halo_kernel,
        out_shape=jax.ShapeDtypeStruct((peers, half_y, rows, half_z), BF16),
        scratch_shapes=[pltpu.VMEM((6 * chans, (1 + half_y) * half_z), BF16)],
        compiler_params=PARAMS,
        cost_estimate=pl.CostEstimate(
            flops=2 * total * 12 * chans * half_y * half_z, bytes_accessed=1 << 22, transcendentals=0
        ),
        name="halo_plane",
    )(halo_p, weights_halo, acc)

    arrived = [parts[0]] + [shifted(parts[r], "col", r) for r in range(1, peers)]
    fill_o = (0, rows - cout)
    bias_p = jnp.broadcast_to(jnp.pad(bias, fill_o)[None, :, None], (1, rows, half_z))
    cot_p = jnp.pad(jnp.transpose(cotangent[:, 0], (1, 0, 2)), ((0, 0), fill_o, (0, 0)))
    shape = jax.ShapeDtypeStruct((half_y, rows, half_z), BF16)
    out, masked = pl.pallas_call(
        act_kernel,
        out_shape=(shape, shape),
        compiler_params=PARAMS,
        cost_estimate=pl.CostEstimate(
            flops=20 * half_y * rows * half_z, bytes_accessed=1 << 21, transcendentals=3 * half_y * rows * half_z
        ),
        name="activation",
    )(*arrived, bias_p, cot_p)
    out_act = jnp.transpose(out[:, :cout], (1, 0, 2))[:, None]

    gathered = [masked] + [shifted(masked, "col", r) for r in range(1, peers)]
    above = [shifted(piece, "gx", -1) for piece in gathered]
    weights_back = backward_weights(behind)
    in_grad = pl.pallas_call(
        grad_kernel,
        out_shape=jax.ShapeDtypeStruct((chans, planes, span_y, span_z), BF16),
        scratch_shapes=[pltpu.VMEM((2 * total, (1 + half_y) * half_z), BF16)],
        compiler_params=PARAMS,
        cost_estimate=pl.CostEstimate(
            flops=2 * 4 * total * 12 * chans * half_y * half_z, bytes_accessed=1 << 22, transcendentals=0
        ),
        name="transposed_taps",
    )(*gathered, *above, weights_back)
    return out_act, in_grad[:cin]


def solution(mesh):
    in_specs = (P("col", "gx", None, None), P(), P("col"), P("col", "gx", None, None))
    out_specs = (P("col", "gx", None, None), P("col", "gx", None, None))
    return jax.shard_map(
        on_device, mesh=mesh, in_specs=in_specs, out_specs=out_specs, check_vma=False
    )
```

time: 267 us -> 76.7 us (0.29); the launches traced: 262 us -> 75.6 us
  waiting for transfers between devices: 170 us -> 33.3 us
  local copies, waits for them, and re-layouts: 40.5 us -> 4.94 us
  matrix products: 27.5 us -> 0 us
  starting transfers between devices: 2.65 us -> 24 us
  between operations: 14.5 us -> 0.88 us
  Pallas kernels: 0 us -> 10.5 us
  other arithmetic: 6.93 us -> 2.07 us
    all_gather x2 -> x0, waiting for transfers between devices: 158 us -> none  [the longest x1 115 us: on_device(): gathered = lax.all_gather(extended, 'col', axis=0, tiled=True)]
    dot_general x59 -> x0, matrix products: 27.5 us -> none  [the longest x27 10.2 us: conv_taps(): jnp.einsum('oc,cpyz->opyz', weights[:, :, tap_x, tap_y, tap_z], window, p...]
    ppermute x2 -> x11, starting transfers between devices: 2.57 us -> 24 us  [shifted(): lax.ppermute(block, axis, [(i, (i + distance) % count) for i in range(cou...]
    ppermute x2 -> x11, waiting for transfers between devices: 12.1 us -> 33.3 us  [shifted(): lax.ppermute(block, axis, [(i, (i + distance) % count) for i in range(cou...]
    slice x11 -> x4, local copies, waits for them, and re-layouts: 20.5 us -> 0.24 us  [the longest x2 0.18 us: forward_weights(): local = cols[:, :, :, 1:].reshape(peers * rows, 2 * 2 * 3 * 2 * cin)]
    pallas_call x0 -> x4, Pallas kernels: none -> 10.5 us  [the longest x1 4.57 us: on_device(): pl.pallas_call(grad_kernel, out_shape=jax.ShapeDtypeStruct((chans, planes...]
    reshape x1 -> x6, local copies, waits for them, and re-layouts: 10.1 us -> 0.92 us  [the longest x1 0.34 us: backward_weights(): return turned.reshape(2 * 3 * 2 * cin, 2 * 2 * peers * rows)]
    unnamed x12 -> x11, local copies, waits for them, and re-layouts: 9.26 us -> 1.01 us
  transfers between devices with their start and end apart: 4 -> 11, of which waited for: 4 -> 8; matrix products, arithmetic and copies ran while one was open for 0% -> 6% of each run, Pallas kernels for 0% -> 5%
where the time goes in v1:
time: 76.7 us; the launch traced here: 75.6 us
  waiting for transfers between devices  33.3 us (43%)
  starting transfers between devices  24 us (31%)
  Pallas kernels  10.5 us (14%)
  local copies, waits for them, and re-layouts  4.94 us (6%)
  other arithmetic  2.07 us (3%)
  between operations  0.88 us (1%)
    ppermute x11, waiting for transfers between devices, shifted(): lax.ppermute(block, axis, [(i, (i + distance) % count) for i in range(cou...  33.3 us
    ppermute x11, starting transfers between devices, shifted(): lax.ppermute(block, axis, [(i, (i + distance) % count) for i in range(cou...  24 us
    pallas_call x1, Pallas kernels, on_device(): pl.pallas_call(grad_kernel, out_shape=jax.ShapeDtypeStruct((chans, planes...  4.57 us
    pallas_call x1, Pallas kernels, on_device(): pl.pallas_call(local_kernel, out_shape=jax.ShapeDtypeStruct((total, half_...  3.48 us
    pallas_call x1, Pallas kernels, on_device(): pl.pallas_call(halo_kernel, out_shape=jax.ShapeDtypeStruct((peers, half_y...  1.9 us
  transfers between devices with their start and end apart: 11, of which 8 were waited for; matrix products, arithmetic and copies ran while one was open for 6% of the time, Pallas kernels for 5%

profile of v1, /device:TPU:11, one launch (start us, length us, event | category | flops | bytes accessed | tf_op | source)
XLA Modules:
  0.0 75.6 jit_solution(11305680485398303720)
XLA Ops:
  0.6 0.0 copy-start
  0.7 1.2 %slice_bitcast_fusion = bf16[8,128,256]{2,1,0:T(8,128)(2,1)S(1)} fusion(bf16[8,2,128,256]{3,2,1,0:T(8,128)(2,1)} %field_ref.1), kind=kLoop, calls=%fused_computation | loop fusion | bytes 1048576 | tf_op jit(solution)/shard_map/squeeze | solution.py:186
  1.8 1.8 %collective-permute-start = (bf16[8,128,256]{2,1,0:T(8,128)(2,1)S(1)}, bf16[8,128,256]{2,1,0:T(8,128)(2,1)S(1)}, u32[]{:S(2)}, u32[]{:S(2)}) collective-permute-start(bf16[8,128,256]{2,1,0:T(8,128)(2,1)S(1)} %slice_bitcast_fusion), channel_id=1, source_target_pairs={{0,4},{4,8},{8,12},{12,16},{16,20},{20,24},{24,28},{28,0},{1,5},{5... | collective-permute-start | bytes 1572872 | tf_op jit(solution)/shard_map/ppermute | solution.py:19
  3.7 0.1 reshape.22
  3.8 0.5 fusion
  4.5 0.2 copy.45
  4.6 0.1 reshape.25
  4.8 0.1 copy.46.weight_ref
  4.9 0.1 copy.44
  5.0 0.1 reshape.24
  5.1 0.1 copy.47.weight_ref
  5.2 3.5 %local_planes.1.acc_ref = f32[64,8192]{1,0:T(8,128)S(1)} custom-call(bf16[8,2,128,256]{3,2,1,0:T(8,128)(2,1)S(1)} %copy-done.1, bf16[64,192]{1,0:T(8,128)(2,1)S(1)} %copy.46.weight_ref), custom_call_target="tpu_custom_call" | custom-call | flops 201326592 | bytes 4194304 | tf_op jit(solution)/shard_map/local_planes/pallas_call | solution.py:203
  8.7 1.1 %collective-permute-done.halo_ref = bf16[8,128,256]{2,1,0:T(8,128)(2,1)S(1)} collective-permute-done((bf16[8,128,256]{2,1,0:T(8,128)(2,1)S(1)}, bf16[8,128,256]{2,1,0:T(8,128)(2,1)S(1)}, u32[]{:S(2)}, u32[]{:S(2)}) %collective-permute-start) | collective-permute-done | bytes 524320 | tf_op jit(solution)/shard_map/ppermute | solution.py:19
  9.8 1.9 %halo_plane.1 = bf16[4,64,16,128]{3,2,1,0:T(8,128)(2,1)S(1)} custom-call(bf16[8,128,256]{2,1,0:T(8,128)(2,1)S(1)} %collective-permute-done.halo_ref, bf16[64,96]{1,0:T(8,128)(2,1)S(1)} %copy.47.weight_ref, f32[64,8192]{1,0:T(8,128)S(1)} %local_planes.1.acc_ref), custom_call_target="tpu_custom_call" | custom-call | flops 100663296 | bytes 4194304 | tf_op jit(solution)/shard_map/halo_plane/pallas_call | solution.py:213
  11.7 0.9 %slice_bitcast_fusion.1 = (bf16[64,16,128]{2,1,0:T(8,128)(2,1)S(1)}, bf16[64,16,128]{2,1,0:T(8,128)(2,1)S(1)}, bf16[64,16,128]{2,1,0:T(8,128)(2,1)}, bf16[64,16,128]{2,1,0:T(8,128)(2,1)S(1)}) fusion(bf16[4,64,16,128]{3,2,1,0:T(8,128)(2,1)S(1)} %halo_plane.1), kind=kLoop, calls=%fused_computation.13 | loop fusion | bytes 2097152 | tf_op jit(solution)/shard_map/squeeze | solution.py:224
  12.6 1.3 %collective-permute-start.1 = (bf16[64,16,128]{2,1,0:T(8,128)(2,1)}, bf16[64,16,128]{2,1,0:T(8,128)(2,1)S(1)}, u32[]{:S(2)}, u32[]{:S(2)}) collective-permute-start(bf16[64,16,128]{2,1,0:T(8,128)(2,1)} %get-tuple-element.16), channel_id=1, source_target_pairs={{0,1},{1,2},{2,3},{3,0},{4,5},{5,6},{6,7},{7,4},{8,9},{9,10},{10,1... | collective-permute-start | bytes 786440 | tf_op jit(solution)/shard_map/ppermute | solution.py:19
  13.9 1.0 %collective-permute-start.2 = (bf16[64,16,128]{2,1,0:T(8,128)(2,1)S(1)}, bf16[64,16,128]{2,1,0:T(8,128)(2,1)S(1)}, u32[]{:S(2)}, u32[]{:S(2)}) collective-permute-start(bf16[64,16,128]{2,1,0:T(8,128)(2,1)S(1)} %get-tuple-element.15), channel_id=1, source_target_pairs={{0,2},{1,3},{2,0},{3,1},{4,6},{5,7},{6,4},{7,5},{8,10},{9,11},{10,... | collective-permute-start | bytes 786440 | tf_op jit(solution)/shard_map/ppermute | solution.py:19
  14.9 1.5 %collective-permute-start.3 = (bf16[64,16,128]{2,1,0:T(8,128)(2,1)S(1)}, bf16[64,16,128]{2,1,0:T(8,128)(2,1)S(1)}, u32[]{:S(2)}, u32[]{:S(2)}) collective-permute-start(bf16[64,16,128]{2,1,0:T(8,128)(2,1)S(1)} %get-tuple-element.14), channel_id=1, source_target_pairs={{0,3},{1,0},{2,1},{3,2},{4,7},{5,4},{6,5},{7,6},{8,11},{9,8},{10,9... | collective-permute-start | bytes 786440 | tf_op jit(solution)/shard_map/ppermute | solution.py:19
  16.4 0.3 pad_maximum_fusion
  16.6 0.2 rev.3
  16.9 0.2 copy.62
  17.1 0.1 dynamic-slice_bitcast_fusion.2
  17.2 2.0 %collective-permute-done.1.refs_1_ = bf16[64,16,128]{2,1,0:T(8,128)(2,1)S(1)} collective-permute-done((bf16[64,16,128]{2,1,0:T(8,128)(2,1)}, bf16[64,16,128]{2,1,0:T(8,128)(2,1)S(1)}, u32[]{:S(2)}, u32[]{:S(2)}) %collective-permute-start.1) | collective-permute-done | bytes 262176 | tf_op jit(solution)/shard_map/ppermute | solution.py:19
  19.2 15.9 %collective-permute-done.2.refs_2_ = bf16[64,16,128]{2,1,0:T(8,128)(2,1)S(1)} collective-permute-done((bf16[64,16,128]{2,1,0:T(8,128)(2,1)S(1)}, bf16[64,16,128]{2,1,0:T(8,128)(2,1)S(1)}, u32[]{:S(2)}, u32[]{:S(2)}) %collective-permute-start.2) | collective-permute-done | bytes 262176 | tf_op jit(solution)/shard_map/ppermute | solution.py:19
  35.2 3.6 %collective-permute-done.3.refs_3_ = bf16[64,16,128]{2,1,0:T(8,128)(2,1)S(1)} collective-permute-done((bf16[64,16,128]{2,1,0:T(8,128)(2,1)S(1)}, bf16[64,16,128]{2,1,0:T(8,128)(2,1)S(1)}, u32[]{:S(2)}, u32[]{:S(2)}) %collective-permute-start.3) | collective-permute-done | bytes 262176 | tf_op jit(solution)/shard_map/ppermute | solution.py:19
  38.8 0.1 broadcast_in_dim.4.refs_4_
  38.9 0.5 activation.1
  39.4 0.1 collective-permute-start.6
  39.4 1.5 %collective-permute-start.4 = (bf16[64,16,128]{2,1,0:T(8,128)(2,1)S(1)}, bf16[64,16,128]{2,1,0:T(8,128)(2,1)S(1)}, u32[]{:S(2)}, u32[]{:S(2)}) collective-permute-start(bf16[64,16,128]{2,1,0:T(8,128)(2,1)S(1)} %get-tuple-element.5.refs_0_), channel_id=1, source_target_pairs={{0,1},{1,2},{2,3},{3,0},{4,5},{5,6},{6,7},{7,4},{8,9},{9,10},{10,1... | collective-permute-start | bytes 786440 | tf_op jit(solution)/shard_map/ppermute | solution.py:19
  40.9 1.3 %collective-permute-start.5 = (bf16[64,16,128]{2,1,0:T(8,128)(2,1)S(1)}, bf16[64,16,128]{2,1,0:T(8,128)(2,1)S(1)}, u32[]{:S(2)}, u32[]{:S(2)}) collective-permute-start(bf16[64,16,128]{2,1,0:T(8,128)(2,1)S(1)} %get-tuple-element.5.refs_0_), channel_id=1, source_target_pairs={{0,2},{1,3},{2,0},{3,1},{4,6},{5,7},{6,4},{7,5},{8,10},{9,11},{10,... | collective-permute-start | bytes 786440 | tf_op jit(solution)/shard_map/ppermute | solution.py:19
  42.2 0.2 maximum_bitcast_fusion.2
  42.4 0.2 fusion.9
  42.6 0.1 pad_bitcast_fusion
  42.7 3.2 %collective-permute-start.7 = (bf16[64,16,128]{2,1,0:T(8,128)(2,1)S(1)}, bf16[64,16,128]{2,1,0:T(8,128)(2,1)S(1)}, u32[]{:S(2)}, u32[]{:S(2)}) collective-permute-start(bf16[64,16,128]{2,1,0:T(8,128)(2,1)S(1)} %get-tuple-element.5.refs_0_), channel_id=1, source_target_pairs={{0,28},{4,0},{8,4},{12,8},{16,12},{20,16},{24,20},{28,24},{1,29},{... | collective-permute-start | bytes 786440 | tf_op jit(solution)/shard_map/ppermute | solution.py:19
  45.9 2.5 %collective-permute-done.6.refs_3_ = bf16[64,16,128]{2,1,0:T(8,128)(2,1)S(1)} collective-permute-done((bf16[64,16,128]{2,1,0:T(8,128)(2,1)S(1)}, bf16[64,16,128]{2,1,0:T(8,128)(2,1)S(1)}, u32[]{:S(2)}, u32[]{:S(2)}) %collective-permute-start.6) | collective-permute-done | bytes 262176 | tf_op jit(solution)/shard_map/ppermute | solution.py:19
  48.4 11.9 %collective-permute-start.10 = (bf16[64,16,128]{2,1,0:T(8,128)(2,1)S(1)}, bf16[64,16,128]{2,1,0:T(8,128)(2,1)S(1)}, u32[]{:S(2)}, u32[]{:S(2)}) collective-permute-start(bf16[64,16,128]{2,1,0:T(8,128)(2,1)S(1)} %collective-permute-done.6.refs_3_), channel_id=1, source_target_pairs={{0,28},{4,0},{8,4},{12,8},{16,12},{20,16},{24,20},{28,24},{1,29},{... | collective-permute-start | bytes 786440 | tf_op jit(solution)/shard_map/ppermute | solution.py:19
  60.3 2.4 %collective-permute-done.5.refs_2_ = bf16[64,16,128]{2,1,0:T(8,128)(2,1)S(1)} collective-permute-done((bf16[64,16,128]{2,1,0:T(8,128)(2,1)S(1)}, bf16[64,16,128]{2,1,0:T(8,128)(2,1)S(1)}, u32[]{:S(2)}, u32[]{:S(2)}) %collective-permute-start.5) | collective-permute-done | bytes 262176 | tf_op jit(solution)/shard_map/ppermute | solution.py:19
  62.7 0.5 collective-permute-start.9
  63.2 0.2 maximum_bitcast_fusion.1
  63.4 0.3 fusion.4
  63.7 0.4 maximum_bitcast_fusion
  64.1 0.2 copy.53
  64.3 0.3 reshape.26.refs_8_
  64.6 0.8 %copy.54 = bf16[16,1,64,128]{3,2,1,0:T(8,128)(2,1)} copy(bf16[16,1,64,128]{3,0,2,1:T(8,128)(2,1)S(1)} %bitcast.68) | data formatting | bytes 524288
  65.4 0.0 collective-permute-done.10.refs_7_
  65.4 2.8 %collective-permute-done.8.refs_5_ = bf16[64,16,128]{2,1,0:T(8,128)(2,1)S(1)} collective-permute-done((bf16[64,16,128]{2,1,0:T(8,128)(2,1)S(1)}, bf16[64,16,128]{2,1,0:T(8,128)(2,1)S(1)}, u32[]{:S(2)}, u32[]{:S(2)}) %collective-permute-start.8) | collective-permute-done | bytes 262176 | tf_op jit(solution)/shard_map/ppermute | solution.py:19
  68.2 2.8 %collective-permute-done.9.refs_6_ = bf16[64,16,128]{2,1,0:T(8,128)(2,1)S(1)} collective-permute-done((bf16[64,16,128]{2,1,0:T(8,128)(2,1)S(1)}, bf16[64,16,128]{2,1,0:T(8,128)(2,1)S(1)}, u32[]{:S(2)}, u32[]{:S(2)}) %collective-permute-start.9) | collective-permute-done | bytes 262176 | tf_op jit(solution)/shard_map/ppermute | solution.py:19
  71.0 4.6 %transposed_taps.1 = bf16[8,2,128,256]{3,2,1,0:T(8,128)(2,1)} custom-call(bf16[64,16,128]{2,1,0:T(8,128)(2,1)S(1)} %get-tuple-element.5.refs_0_, bf16[64,16,128]{2,1,0:T(8,128)(2,1)S(1)} %collective-permute-done.4.refs_1_, bf16[64,16,128]{2,1,0:T(8,128)(2,1)S(1)} %collective-permute-done.5.refs_2_, bf16[64,16,128]{2,1,0:T(8,128)(2,1)S(1)} %collective-permute-done.6.refs_3_, ...), custom_call_target="tpu_custom_call" | custom-call | flops 402653184 | bytes 4194304 | tf_op jit(solution)/shard_map/transposed_taps/pallas_call | solution.py:243
  (15 shorter events, 0.2 us)
Async XLA Ops:
  0.6 3.0 %copy-start = (bf16[64,32,3,3,3]{0,1,4,3,2:T(8,128)(2,1)S(1)}, bf16[64,32,3,3,3]{0,1,4,3,2:T(8,128)(2,1)}, u32[]{:S(2)}) copy-start(bf16[64,32,3,3,3]{0,1,4,3,2:T(8,128)(2,1)} %param.5) | copy-start | bytes 331780
  0.6 4.5 %copy-start.1 = (bf16[8,2,128,256]{3,2,1,0:T(8,128)(2,1)S(1)}, bf16[8,2,128,256]{3,2,1,0:T(8,128)(2,1)}, u32[]{:S(2)}) copy-start(bf16[8,2,128,256]{3,2,1,0:T(8,128)(2,1)} %field_ref.1) | copy-start | bytes 3145732
  1.8 8.0 %collective-permute-start = (bf16[8,128,256]{2,1,0:T(8,128)(2,1)S(1)}, bf16[8,128,256]{2,1,0:T(8,128)(2,1)S(1)}, u32[]{:S(2)}, u32[]{:S(2)}) collective-permute-start(bf16[8,128,256]{2,1,0:T(8,128)(2,1)S(1)} %slice_bitcast_fusion), channel_id=1, source_target_pairs={{0,4},{4,8},{8,12},{12,16},{16,20},{20,24},{24,28},{28,0},{1,5},{5... | collective-permute-start | bytes 1572872 | tf_op jit(solution)/shard_map/ppermute | solution.py:19
  11.7 5.2 %copy-start.2 = (bf16[16,1,64,128]{3,2,1,0:T(8,128)(2,1)S(1)}, bf16[16,1,64,128]{3,2,1,0:T(8,128)(2,1)}, u32[]{:S(2)}) copy-start(bf16[16,1,64,128]{3,2,1,0:T(8,128)(2,1)} %param.7) | copy-start | bytes 786436
  11.7 27.1 %copy-start.3 = (f32[16]{0:T(128)S(1)}, f32[16]{0:T(128)}, u32[]{:S(2)}) copy-start(f32[16]{0:T(128)} %param.6) | copy-start | bytes 196
  12.6 6.6 %collective-permute-start.1 = (bf16[64,16,128]{2,1,0:T(8,128)(2,1)}, bf16[64,16,128]{2,1,0:T(8,128)(2,1)S(1)}, u32[]{:S(2)}, u32[]{:S(2)}) collective-permute-start(bf16[64,16,128]{2,1,0:T(8,128)(2,1)} %get-tuple-element.16), channel_id=1, source_target_pairs={{0,1},{1,2},{2,3},{3,0},{4,5},{5,6},{6,7},{7,4},{8,9},{9,10},{10,1... | collective-permute-start | bytes 786440 | tf_op jit(solution)/shard_map/ppermute | solution.py:19
  13.9 21.3 %collective-permute-start.2 = (bf16[64,16,128]{2,1,0:T(8,128)(2,1)S(1)}, bf16[64,16,128]{2,1,0:T(8,128)(2,1)S(1)}, u32[]{:S(2)}, u32[]{:S(2)}) collective-permute-start(bf16[64,16,128]{2,1,0:T(8,128)(2,1)S(1)} %get-tuple-element.15), channel_id=1, source_target_pairs={{0,2},{1,3},{2,0},{3,1},{4,6},{5,7},{6,4},{7,5},{8,10},{9,11},{10,... | collective-permute-start | bytes 786440 | tf_op jit(solution)/shard_map/ppermute | solution.py:19
  14.9 23.9 %collective-permute-start.3 = (bf16[64,16,128]{2,1,0:T(8,128)(2,1)S(1)}, bf16[64,16,128]{2,1,0:T(8,128)(2,1)S(1)}, u32[]{:S(2)}, u32[]{:S(2)}) collective-permute-start(bf16[64,16,128]{2,1,0:T(8,128)(2,1)S(1)} %get-tuple-element.14), channel_id=1, source_target_pairs={{0,3},{1,0},{2,1},{3,2},{4,7},{5,4},{6,5},{7,6},{8,11},{9,8},{10,9... | collective-permute-start | bytes 786440 | tf_op jit(solution)/shard_map/ppermute | solution.py:19
  39.4 9.1 %collective-permute-start.6 = (bf16[64,16,128]{2,1,0:T(8,128)(2,1)S(1)}, bf16[64,16,128]{2,1,0:T(8,128)(2,1)S(1)}, u32[]{:S(2)}, u32[]{:S(2)}) collective-permute-start(bf16[64,16,128]{2,1,0:T(8,128)(2,1)S(1)} %get-tuple-element.5.refs_0_), channel_id=1, source_target_pairs={{0,3},{1,0},{2,1},{3,2},{4,7},{5,4},{6,5},{7,6},{8,11},{9,8},{10,9... | collective-permute-start | bytes 786440 | tf_op jit(solution)/shard_map/ppermute | solution.py:19
  39.4 20.9 %collective-permute-start.4 = (bf16[64,16,128]{2,1,0:T(8,128)(2,1)S(1)}, bf16[64,16,128]{2,1,0:T(8,128)(2,1)S(1)}, u32[]{:S(2)}, u32[]{:S(2)}) collective-permute-start(bf16[64,16,128]{2,1,0:T(8,128)(2,1)S(1)} %get-tuple-element.5.refs_0_), channel_id=1, source_target_pairs={{0,1},{1,2},{2,3},{3,0},{4,5},{5,6},{6,7},{7,4},{8,9},{9,10},{10,1... | collective-permute-start | bytes 786440 | tf_op jit(solution)/shard_map/ppermute | solution.py:19
  40.9 21.9 %collective-permute-start.5 = (bf16[64,16,128]{2,1,0:T(8,128)(2,1)S(1)}, bf16[64,16,128]{2,1,0:T(8,128)(2,1)S(1)}, u32[]{:S(2)}, u32[]{:S(2)}) collective-permute-start(bf16[64,16,128]{2,1,0:T(8,128)(2,1)S(1)} %get-tuple-element.5.refs_0_), channel_id=1, source_target_pairs={{0,2},{1,3},{2,0},{3,1},{4,6},{5,7},{6,4},{7,5},{8,10},{9,11},{10,... | collective-permute-start | bytes 786440 | tf_op jit(solution)/shard_map/ppermute | solution.py:19
  42.7 22.7 %collective-permute-start.7 = (bf16[64,16,128]{2,1,0:T(8,128)(2,1)S(1)}, bf16[64,16,128]{2,1,0:T(8,128)(2,1)S(1)}, u32[]{:S(2)}, u32[]{:S(2)}) collective-permute-start(bf16[64,16,128]{2,1,0:T(8,128)(2,1)S(1)} %get-tuple-element.5.refs_0_), channel_id=1, source_target_pairs={{0,28},{4,0},{8,4},{12,8},{16,12},{20,16},{24,20},{28,24},{1,29},{... | collective-permute-start | bytes 786440 | tf_op jit(solution)/shard_map/ppermute | solution.py:19
  48.4 17.0 %collective-permute-start.10 = (bf16[64,16,128]{2,1,0:T(8,128)(2,1)S(1)}, bf16[64,16,128]{2,1,0:T(8,128)(2,1)S(1)}, u32[]{:S(2)}, u32[]{:S(2)}) collective-permute-start(bf16[64,16,128]{2,1,0:T(8,128)(2,1)S(1)} %collective-permute-done.6.refs_3_), channel_id=1, source_target_pairs={{0,28},{4,0},{8,4},{12,8},{16,12},{20,16},{24,20},{28,24},{1,29},{... | collective-permute-start | bytes 786440 | tf_op jit(solution)/shard_map/ppermute | solution.py:19
  60.3 7.9 %collective-permute-start.8 = (bf16[64,16,128]{2,1,0:T(8,128)(2,1)S(1)}, bf16[64,16,128]{2,1,0:T(8,128)(2,1)S(1)}, u32[]{:S(2)}, u32[]{:S(2)}) collective-permute-start(bf16[64,16,128]{2,1,0:T(8,128)(2,1)S(1)} %collective-permute-done.4.refs_1_), channel_id=1, source_target_pairs={{0,28},{4,0},{8,4},{12,8},{16,12},{20,16},{24,20},{28,24},{1,29},{... | collective-permute-start | bytes 786440 | tf_op jit(solution)/shard_map/ppermute | solution.py:19
  62.7 8.3 %collective-permute-start.9 = (bf16[64,16,128]{2,1,0:T(8,128)(2,1)S(1)}, bf16[64,16,128]{2,1,0:T(8,128)(2,1)S(1)}, u32[]{:S(2)}, u32[]{:S(2)}) collective-permute-start(bf16[64,16,128]{2,1,0:T(8,128)(2,1)S(1)} %collective-permute-done.5.refs_2_), channel_id=1, source_target_pairs={{0,28},{4,0},{8,4},{12,8},{16,12},{20,16},{24,20},{28,24},{1,29},{... | collective-permute-start | bytes 786440 | tf_op jit(solution)/shard_map/ppermute | solution.py:19

commit v2 on v1

v2 whole, which is shorter than its diff:
```python
import functools

import jax
import jax.numpy as jnp
from jax import lax
from jax.experimental import pallas as pl
from jax.experimental.pallas import tpu as pltpu
from jax.sharding import PartitionSpec as P

F32 = jnp.float32
BF16 = jnp.bfloat16
LANES = 128
ROWS = 16
PARAMS = pltpu.CompilerParams(vmem_limit_bytes=24 * 1024 * 1024)


def shifted(block, axis, distance):
    count = lax.axis_size(axis)
    return lax.ppermute(block, axis, [(i, (i + distance) % count) for i in range(count)])


def one_hot(shape, rule):
    rows = lax.broadcasted_iota(jnp.int32, shape, 0)
    cols = lax.broadcasted_iota(jnp.int32, shape, 1)
    return jnp.where(rule(rows, cols), 1.0, 0.0).astype(BF16)


def dot(left, right):
    return jnp.dot(left, right, preferred_element_type=F32)


def fill_taps(blocks, chans, span_z, taps_ref, first_row):
    half_z = span_z // 2
    size = chans * ROWS
    swap = one_hot((size, size), lambda r, c: c == (r % chans) * ROWS + r // chans)
    split = one_hot(
        (span_z, 3 * half_z),
        lambda z, m: z == (2 * (m % half_z) + m // half_z + span_z - 1) % span_z,
    )
    pair = 2 * chans
    for values, first, count, place in blocks:
        swapped = dot(swap, values()).astype(BF16)
        tapped = dot(swapped, split).astype(BF16)
        for j in range(count):
            for tap in range(3):
                row = first_row + tap * pair
                lane = (place + j) * half_z
                taps_ref[row : row + pair, lane : lane + half_z] = tapped[
                    (first + j) * pair : (first + j + 1) * pair, tap * half_z : (tap + 1) * half_z
                ]


def rows_of(ref, index, block):
    def values():
        rows = ref[(slice(None), *index, slice(block * ROWS, (block + 1) * ROWS))]
        return rows.reshape(rows.shape[0] * ROWS, rows.shape[-1])

    return values


def tap_sums(weights, taps_ref, lane, width, half_z):
    before = taps_ref[:, lane : lane + width]
    here = taps_ref[:, lane + half_z : lane + half_z + width]
    return dot(weights, jnp.concatenate([before, here], axis=0))


def local_kernel(field_ref, weight_ref, acc_ref, taps_ref):
    chans, planes, span_y, span_z = field_ref.shape
    half_z = span_z // 2
    count = span_y // ROWS
    for plane in range(planes):
        blocks = [(rows_of(field_ref, (plane,), b), 0, 8, 1 + 8 * b) for b in range(count)]
        blocks.append((rows_of(field_ref, (plane,), count - 1), 7, 1, 0))
        fill_taps(blocks, chans, span_z, taps_ref, plane * 6 * chans)
    weights = weight_ref[...]
    width = 8 * half_z
    for step in range(count):
        lane = step * width
        acc_ref[:, lane : lane + width] = tap_sums(weights, taps_ref, lane, width, half_z)


def halo_kernel(part, *refs):
    halo_refs, (weight_ref, acc_ref), part_refs, taps_ref = (
        refs[: part + 1],
        refs[part + 1 : part + 3],
        refs[part + 3 : -1],
        refs[-1],
    )
    chans, _, span_z = halo_refs[0].shape
    half_z = span_z // 2
    lower = halo_refs[0].shape[1] // ROWS - 1
    if part == 0:
        blocks = [(rows_of(halo_refs[0], (), 0), 7, 1, 0)]
        blocks += [(rows_of(halo_refs[0], (), 1 + b), 0, 8, 1 + 8 * b) for b in range(lower)]
    else:
        upper = halo_refs[1].shape[1] // ROWS
        blocks = [(rows_of(halo_refs[0], (), lower), 7, 1, 0)]
        blocks += [(rows_of(halo_refs[1], (), b), 0, 8, 1 + 8 * b) for b in range(upper)]
        blocks += [(rows_of(halo_refs[0], (), 0), 0, 8, 1 + 8 * upper)]
    fill_taps(blocks, chans, span_z, taps_ref, 0)
    weights = weight_ref[...]
    count, rows, _ = part_refs[0].shape
    width = 8 * half_z
    base = part * (acc_ref.shape[1] - count * half_z)
    for step in range(count // 8):
        lane = step * width
        sums = acc_ref[:, base + lane : base + lane + width]
        sums = (sums + tap_sums(weights, taps_ref, lane, width, half_z)).astype(BF16)
        for j in range(8):
            for peer, ref in enumerate(part_refs):
                ref[step * 8 + j] = sums[
                    peer * rows : (peer + 1) * rows, j * half_z : (j + 1) * half_z
                ]


def add_kernel(one_ref, two_ref, sum_ref):
    sum_ref[...] = (one_ref[...].astype(F32) + two_ref[...].astype(F32)).astype(BF16)


def act_kernel(*refs):
    *part_refs, bias_ref, cot_ref, out_ref, masked_ref = refs
    pre = bias_ref[...] + functools.reduce(
        lambda a, b: a + b, [ref[...].astype(F32) for ref in part_refs]
    )
    small = jnp.exp(-jnp.abs(pre))
    soft = jnp.maximum(pre, 0.0) + jnp.log(1.0 + small)
    out_ref[...] = (0.3 * pre + 0.7 * soft).astype(BF16)
    gate = jnp.where(pre >= 0.0, 1.0, small) / (1.0 + small)
    masked_ref[...] = (cot_ref[...].astype(F32) * (0.3 + 0.7 * gate)).astype(BF16)


def grad_blocks(held_ref, weights, blocks, chans, span_z, store):
    half_z = span_z // 2
    size = chans * ROWS
    swap = one_hot((size, size), lambda r, c: c == (r % ROWS) * chans + r // ROWS)
    weave = one_hot((span_z, span_z), lambda m, z: z == 2 * (m % half_z) + m // half_z)
    pair = 2 * chans
    width = 8 * half_z
    for step in range(blocks):
        lane = step * width
        here = held_ref[:, lane : lane + width]
        after = held_ref[:, lane + half_z : lane + half_z + width]
        sums = dot(weights, jnp.concatenate([here, after], axis=0))
        for parity_x in range(2):
            base = parity_x * 3 * pair
            rows = []
            for j in range(8):
                tile = sums[base : base + 3 * pair, j * half_z : (j + 1) * half_z]
                even = tile[:pair]
                odd = tile[pair : 2 * pair] + pltpu.roll(tile[2 * pair :], half_z - 1, 1)
                rows.append(jnp.concatenate([even.astype(BF16), odd.astype(BF16)], axis=1))
            swapped = dot(swap, jnp.concatenate(rows, axis=0)).astype(BF16)
            woven = dot(swapped, weave).astype(BF16)
            for chan in range(chans):
                store(chan, parity_x, step, woven[chan * ROWS : (chan + 1) * ROWS])


def lower_grad_kernel(*refs):
    *piece_refs, weight_ref, grad_ref, held_ref = refs
    chans, _, span_y, span_z = grad_ref.shape
    half_z = span_z // 2
    for index, ref in enumerate(piece_refs):
        row = index * ROWS
        for j in range(span_y // 2 + 1):
            held_ref[row : row + ROWS, j * half_z : (j + 1) * half_z] = ref[j]

    def store(chan, parity_x, step, values):
        grad_ref[chan, parity_x, step * ROWS : (step + 1) * ROWS, :] = values

    grad_blocks(held_ref, weight_ref[...], span_y // ROWS, chans, span_z, store)


def upper_grad_kernel(*refs):
    *piece_refs, weight_ref, lower_ref, grad_ref, held_ref = refs
    chans, _, span_y, span_z = grad_ref.shape
    half_z = span_z // 2
    done = lower_ref.shape[2]
    grad_ref[:, :, :done, :] = lower_ref[...]
    pieces = len(piece_refs) // 2
    for index in range(pieces):
        row = index * ROWS
        low, high = piece_refs[index], piece_refs[pieces + index]
        count = low.shape[0]
        tiles = [(low, j) for j in range(done // 2, count)]
        tiles += [(high, j) for j in range(high.shape[0])] + [(low, 0)]
        for place, (ref, j) in enumerate(tiles):
            held_ref[row : row + ROWS, place * half_z : (place + 1) * half_z] = ref[j]

    def store(chan, parity_x, step, values):
        first = done + step * ROWS
        grad_ref[chan, parity_x, first : first + ROWS, :] = values

    grad_blocks(held_ref, weight_ref[...], (span_y - done) // ROWS, chans, span_z, store)


def forward_weights(own):
    peers, rows, cin = own.shape[:3]
    lead = jnp.pad(own, ((0, 0),) * 4 + ((1, 0), (0, 0)))
    lead = lead.reshape(*lead.shape[:4], 2, 2, 3)
    cols = jnp.transpose(lead, (0, 1, 4, 3, 6, 5, 2))
    local = cols[:, :, :, 1:].reshape(peers * rows, 2 * 2 * 3 * 2 * cin)
    halo = cols[:, :, :, :1].reshape(peers * rows, 2 * 1 * 3 * 2 * cin)
    return local, halo


def backward_weights(own):
    peers, rows, cin = own.shape[:3]
    none = jnp.zeros_like(own[:, :, :, 0])
    by_x = jnp.stack(
        [
            jnp.stack([own[:, :, :, 1], none]),
            jnp.stack([own[:, :, :, 2], own[:, :, :, 0]]),
        ]
    )
    none = jnp.zeros_like(by_x[..., 0, :])
    by_y = jnp.stack(
        [
            jnp.stack([by_x[..., 1, :], none]),
            jnp.stack([by_x[..., 2, :], by_x[..., 0, :]]),
        ]
    )
    by_z = jnp.stack([by_y[..., 1], by_y[..., 2], by_y[..., 0]])
    turned = jnp.transpose(by_z, (3, 0, 1, 7, 2, 4, 5, 6))
    return turned.reshape(2 * 3 * 2 * cin, 2 * 2 * peers * rows)


def call(kernel, name, out_shape, args, scratch=(), flops=0, bytes_accessed=1 << 20, transcendentals=0):
    return pl.pallas_call(
        kernel,
        out_shape=out_shape,
        scratch_shapes=list(scratch),
        compiler_params=PARAMS,
        cost_estimate=pl.CostEstimate(
            flops=flops, bytes_accessed=bytes_accessed, transcendentals=transcendentals
        ),
        name=name,
    )(*args)


def on_device(field, kernel, bias, cotangent):
    peers = lax.axis_size("col")
    me = lax.axis_index("col")
    quarter = peers // 4
    cin, planes, span_y, span_z = field.shape
    cout = bias.shape[0]
    half_y, half_z = span_y // 2, span_z // 2
    mid = span_y // 2
    last = span_y - ROWS
    plane = field[:, planes - 1]
    halos = [
        shifted(jnp.concatenate([plane[:, last:], plane[:, :mid]], axis=1), "gx", 1),
        shifted(plane[:, mid:last], "gx", 1),
    ]

    chans = -(-cin // 8) * 8
    rows = -(-cout // ROWS) * ROWS
    own = lax.dynamic_slice_in_dim(kernel, me * cin, cin, 1)
    own = own.reshape(peers, cout, cin, 3, 3, 3)
    twice = jnp.concatenate([own, own], axis=0)
    ahead = lax.dynamic_slice_in_dim(twice, me, peers, 0)
    behind = lax.dynamic_slice_in_dim(twice[::-1], peers - 1 - me, peers, 0)
    fill_w = ((0, 0), (0, rows - cout), (0, chans - cin), (0, 0), (0, 0), (0, 0))
    ahead, behind = jnp.pad(ahead, fill_w), jnp.pad(behind, fill_w)
    fill_c = (0, chans - cin)
    field_p = jnp.pad(field, (fill_c, (0, 0), (0, 0), (0, 0)))
    halos = [jnp.pad(halo, (fill_c, (0, 0), (0, 0))) for halo in halos]
    weights_local, weights_halo = forward_weights(ahead)

    total = peers * rows
    points = half_y * half_z
    acc = call(
        local_kernel,
        "local_planes",
        jax.ShapeDtypeStruct((total, points), F32),
        (field_p, weights_local),
        [pltpu.VMEM((planes * 6 * chans, (1 + half_y) * half_z), BF16)],
        flops=2 * total * 24 * chans * points,
        bytes_accessed=1 << 22,
    )
    half = half_y // 2
    piece = jax.ShapeDtypeStruct((half, rows, half_z), BF16)
    parts = [
        call(
            functools.partial(halo_kernel, part),
            "halo_plane",
            [piece] * peers,
            (*halos[: part + 1], weights_halo, acc),
            [pltpu.VMEM((6 * chans, (1 + half) * half_z), BF16)],
            flops=total * 12 * chans * points,
            bytes_accessed=1 << 21,
        )
        for part in range(2)
    ]

    steps = (quarter, peers - quarter)
    relayed = [shifted(parts[h][2 * quarter], "col", steps[h]) for h in range(2)]
    direct = [
        [shifted(parts[h][r], "col", r) for r in range(1, peers) if r not in (steps[h], 2 * quarter)]
        for h in range(2)
    ]
    joined = [call(add_kernel, "add", piece, (relayed[h], parts[h][steps[h]])) for h in range(2)]
    joined = [shifted(joined[h], "col", steps[h]) for h in range(2)]

    fill_o = (0, rows - cout)
    bias_p = jnp.broadcast_to(jnp.pad(bias, fill_o)[None, :, None], (1, rows, half_z))
    cot = jnp.pad(jnp.transpose(cotangent[:, 0], (1, 0, 2)), ((0, 0), fill_o, (0, 0)))
    acts = [
        call(
            act_kernel,
            "activation",
            (piece, piece),
            (parts[h][0], joined[h], *direct[h], bias_p, cot[h * half : (h + 1) * half]),
            transcendentals=3 * half * rows * half_z,
        )
        for h in range(2)
    ]
    out = jnp.concatenate([out for out, _ in acts], axis=0)
    out_act = jnp.transpose(out[:, :cout], (1, 0, 2))[:, None]

    masked = [masked for _, masked in acts]
    gathered = [{0: masked[h]} for h in range(2)]
    for h in range(2):
        for r in range(1, peers):
            if r != 2 * quarter:
                gathered[h][r] = shifted(masked[h], "col", r)
    for h in range(2):
        gathered[h][2 * quarter] = shifted(gathered[h][steps[h]], "col", steps[h])
    gathered = [[gathered[h][r] for r in range(peers)] for h in range(2)]
    above = [[shifted(value, "gx", -1) for value in gathered[h]] for h in range(2)]
    weights_back = backward_weights(behind)
    done = span_y // 2 - ROWS
    lower = call(
        lower_grad_kernel,
        "lower_grad",
        jax.ShapeDtypeStruct((chans, planes, done, span_z), BF16),
        (*gathered[0], *above[0], weights_back),
        [pltpu.VMEM((2 * total, (1 + done // 2) * half_z), BF16)],
        flops=3 * total * 12 * chans * points,
    )
    in_grad = call(
        upper_grad_kernel,
        "upper_grad",
        jax.ShapeDtypeStruct((chans, planes, span_y, span_z), BF16),
        (*gathered[0], *above[0], *gathered[1], *above[1], weights_back, lower),
        [pltpu.VMEM((2 * total, (1 + (span_y - done) // 2) * half_z), BF16)],
        flops=5 * total * 12 * chans * points,
        bytes_accessed=1 << 21,
    )
    return out_act, in_grad[:cin]


def solution(mesh):
    in_specs = (P("col", "gx", None, None), P(), P("col"), P("col", "gx", None, None))
    out_specs = (P("col", "gx", None, None), P("col", "gx", None, None))
    return jax.shard_map(
        on_device, mesh=mesh, in_specs=in_specs, out_specs=out_specs, check_vma=False
    )
```

time: 76.7 us -> 63.4 us (0.83)
  the two profiles are of different devices: /device:TPU:11 before, /device:TPU:1 now
where the time goes in v2:
time: 63.4 us; the launch traced here: 63.3 us
  starting transfers between devices  27.8 us (44%)
  waiting for transfers between devices  16.9 us (27%)
  Pallas kernels  11.5 us (18%)
  local copies, waits for them, and re-layouts  4.06 us (6%)
  other arithmetic  2.11 us (3%)
  between operations  1 us (2%)
    ppermute x22, starting transfers between devices, shifted(): lax.ppermute(block, axis, [(i, (i + distance) % count) for i in range(cou...  27.8 us
    ppermute x22, waiting for transfers between devices, shifted(): lax.ppermute(block, axis, [(i, (i + distance) % count) for i in range(cou...  16.9 us
    pallas_call x9, Pallas kernels, call(): pl.pallas_call(kernel, out_shape=out_shape, scratch_shapes=list(scratch),...  11.5 us
  transfers between devices with their start and end apart: 22, of which 8 were waited for; matrix products, arithmetic and copies ran while one was open for 8% of the time, Pallas kernels for 13%

profile of v2, /device:TPU:1, one launch (start us, length us, event | category | flops | bytes accessed | tf_op | source)
XLA Modules:
  0.0 63.3 jit_solution(6291840874356567734)
XLA Ops:
  0.6 1.1 %slice_bitcast_fusion = bf16[8,128,256]{2,1,0:T(8,128)(2,1)S(1)} fusion(bf16[8,2,128,256]{3,2,1,0:T(8,128)(2,1)} %field_ref.1), kind=kLoop, calls=%fused_computation | loop fusion | bytes 1048576 | tf_op jit(solution)/shard_map/squeeze | solution.py:249
  1.9 2.7 %collective-permute-start = (bf16[8,80,256]{2,1,0:T(8,128)(2,1)S(1)}, bf16[8,80,256]{2,1,0:T(8,128)(2,1)S(1)}, u32[]{:S(2)}, u32[]{:S(2)}) collective-permute-start(bf16[8,80,256]{2,1,0:T(8,128)(2,1)S(1)} %pad_maximum_fusion.1), channel_id=1, source_target_pairs={{0,4},{4,8},{8,12},{12,16},{16,20},{20,24},{24,28},{28,0},{1,5},{5... | collective-permute-start | bytes 983048 | tf_op jit(solution)/shard_map/ppermute | solution.py:19
  4.6 0.1 reshape.22
  4.8 0.5 fusion
  5.4 0.2 copy.47
  5.6 0.1 reshape.25
  6.1 0.2 copy.65
  6.3 3.8 %local_planes.1.refs_2_.refs_3_ = f32[64,8192]{1,0:T(8,128)S(1)} custom-call(bf16[8,2,128,256]{3,2,1,0:T(8,128)(2,1)S(1)} %copy-done.1, bf16[64,192]{1,0:T(8,128)(2,1)S(1)} %copy.48.weight_ref), custom_call_target="tpu_custom_call" | custom-call | flops 201326592 | bytes 4194304 | tf_op jit(solution)/shard_map/local_planes/pallas_call | solution.py:228
  10.2 1.1 %halo_plane.2 = (bf16[32,16,128]{2,1,0:T(8,128)(2,1)S(1)}, bf16[32,16,128]{2,1,0:T(8,128)(2,1)S(1)}, bf16[32,16,128]{2,1,0:T(8,128)(2,1)S(1)}, bf16[32,16,128]{2,1,0:T(8,128)(2,1)S(1)}) custom-call(bf16[8,80,256]{2,1,0:T(8,128)(2,1)S(1)} %collective-permute-done.refs_0_, bf16[64,96]{1,0:T(8,128)(2,1)S(1)} %copy.49.refs_1_.refs_2_, ...), custom_call_target="tpu_custom_call" | custom-call | flops 50331648 | bytes 2097152 | tf_op jit(solution)/shard_map/halo_plane/pallas_call | solution.py:228
  11.3 1.4 %collective-permute-start.1 = (bf16[32,16,128]{2,1,0:T(8,128)(2,1)S(1)}, bf16[32,16,128]{2,1,0:T(8,128)(2,1)S(1)}, u32[]{:S(2)}, u32[]{:S(2)}) collective-permute-start(bf16[32,16,128]{2,1,0:T(8,128)(2,1)S(1)} %get-tuple-element.15), channel_id=1, source_target_pairs={{0,1},{1,2},{2,3},{3,0},{4,5},{5,6},{6,7},{7,4},{8,9},{9,10},{10,1... | collective-permute-start | bytes 393224 | tf_op jit(solution)/shard_map/ppermute | solution.py:19
  12.7 1.1 %halo_plane.3 = (bf16[32,16,128]{2,1,0:T(8,128)(2,1)S(1)}, bf16[32,16,128]{2,1,0:T(8,128)(2,1)S(1)}, bf16[32,16,128]{2,1,0:T(8,128)(2,1)S(1)}, bf16[32,16,128]{2,1,0:T(8,128)(2,1)S(1)}) custom-call(bf16[8,80,256]{2,1,0:T(8,128)(2,1)S(1)} %collective-permute-done.refs_0_, bf16[8,48,256]{2,1,0:T(8,128)(2,1)S(1)} %collective-permute-done.4.refs_1_, ...), custom_call_target="tpu_custom_call" | custom-call | flops 50331648 | bytes 2097152 | tf_op jit(solution)/shard_map/halo_plane/pallas_call | solution.py:228
  13.8 2.1 %collective-permute-start.5 = (bf16[32,16,128]{2,1,0:T(8,128)(2,1)S(1)}, bf16[32,16,128]{2,1,0:T(8,128)(2,1)S(1)}, u32[]{:S(2)}, u32[]{:S(2)}) collective-permute-start(bf16[32,16,128]{2,1,0:T(8,128)(2,1)S(1)} %get-tuple-element.20), channel_id=1, source_target_pairs={{0,3},{1,0},{2,1},{3,2},{4,7},{5,4},{6,5},{7,6},{8,11},{9,8},{10,9... | collective-permute-start | bytes 393224 | tf_op jit(solution)/shard_map/ppermute | solution.py:19
  15.9 0.3 pad_maximum_fusion
  16.2 0.2 rev.3
  16.4 1.5 %collective-permute-start.3 = (bf16[32,16,128]{2,1,0:T(8,128)(2,1)S(1)}, bf16[32,16,128]{2,1,0:T(8,128)(2,1)S(1)}, u32[]{:S(2)}, u32[]{:S(2)}) collective-permute-start(bf16[32,16,128]{2,1,0:T(8,128)(2,1)S(1)} %get-tuple-element.17), channel_id=1, source_target_pairs={{0,3},{1,0},{2,1},{3,2},{4,7},{5,4},{6,5},{7,6},{8,11},{9,8},{10,9... | collective-permute-start | bytes 393224 | tf_op jit(solution)/shard_map/ppermute | solution.py:19
  18.1 0.1 dynamic-slice_bitcast_fusion.2
  18.2 0.4 collective-permute-start.7
  18.6 2.9 %collective-permute-done.5.one_ref = bf16[32,16,128]{2,1,0:T(8,128)(2,1)S(1)} collective-permute-done((bf16[32,16,128]{2,1,0:T(8,128)(2,1)S(1)}, bf16[32,16,128]{2,1,0:T(8,128)(2,1)S(1)}, u32[]{:S(2)}, u32[]{:S(2)}) %collective-permute-start.5) | collective-permute-done | bytes 131104 | tf_op jit(solution)/shard_map/ppermute | solution.py:19
  21.5 0.2 collective-permute-start.6
  21.7 0.2 maximum_bitcast_fusion.3
  21.9 3.7 %collective-permute-done.3.refs_2_ = bf16[32,16,128]{2,1,0:T(8,128)(2,1)S(1)} collective-permute-done((bf16[32,16,128]{2,1,0:T(8,128)(2,1)S(1)}, bf16[32,16,128]{2,1,0:T(8,128)(2,1)S(1)}, u32[]{:S(2)}, u32[]{:S(2)}) %collective-permute-start.3) | collective-permute-done | bytes 131104 | tf_op jit(solution)/shard_map/ppermute | solution.py:19
  25.5 0.3 collective-permute-done.2.refs_1_
  25.9 0.2 activation.2
  26.1 0.6 collective-permute-start.8
  26.7 0.2 fusion.9
  26.9 1.7 %collective-permute-done.7.refs_2_ = bf16[32,16,128]{2,1,0:T(8,128)(2,1)S(1)} collective-permute-done((bf16[32,16,128]{2,1,0:T(8,128)(2,1)S(1)}, bf16[32,16,128]{2,1,0:T(8,128)(2,1)S(1)}, u32[]{:S(2)}, u32[]{:S(2)}) %collective-permute-start.7) | collective-permute-done | bytes 131104 | tf_op jit(solution)/shard_map/ppermute | solution.py:19
  28.6 5.3 %collective-permute-done.6.refs_1_ = bf16[32,16,128]{2,1,0:T(8,128)(2,1)S(1)} collective-permute-done((bf16[32,16,128]{2,1,0:T(8,128)(2,1)S(1)}, bf16[32,16,128]{2,1,0:T(8,128)(2,1)S(1)}, u32[]{:S(2)}, u32[]{:S(2)}) %collective-permute-start.6) | collective-permute-done | bytes 131104 | tf_op jit(solution)/shard_map/ppermute | solution.py:19
  33.9 0.2 activation.3
  34.2 1.5 %collective-permute-start.15 = (bf16[32,16,128]{2,1,0:T(8,128)(2,1)S(1)}, bf16[32,16,128]{2,1,0:T(8,128)(2,1)S(1)}, u32[]{:S(2)}, u32[]{:S(2)}) collective-permute-start(bf16[32,16,128]{2,1,0:T(8,128)(2,1)S(1)} %get-tuple-element.25.refs_8_), channel_id=1, source_target_pairs={{0,1},{1,2},{2,3},{3,0},{4,5},{5,6},{6,7},{7,4},{8,9},{9,10},{10,1... | collective-permute-start | bytes 393224 | tf_op jit(solution)/shard_map/ppermute | solution.py:19
  35.7 1.9 %collective-permute-start.10 = (bf16[32,16,128]{2,1,0:T(8,128)(2,1)S(1)}, bf16[32,16,128]{2,1,0:T(8,128)(2,1)S(1)}, u32[]{:S(2)}, u32[]{:S(2)}) collective-permute-start(bf16[32,16,128]{2,1,0:T(8,128)(2,1)S(1)} %get-tuple-element.24.refs_0_), channel_id=1, source_target_pairs={{0,3},{1,0},{2,1},{3,2},{4,7},{5,4},{6,5},{7,6},{8,11},{9,8},{10,9... | collective-permute-start | bytes 393224 | tf_op jit(solution)/shard_map/ppermute | solution.py:19
  37.7 0.2 maximum_bitcast_fusion.2
  37.9 3.8 %collective-permute-start.11 = (bf16[32,16,128]{2,1,0:T(8,128)(2,1)S(1)}, bf16[32,16,128]{2,1,0:T(8,128)(2,1)S(1)}, u32[]{:S(2)}, u32[]{:S(2)}) collective-permute-start(bf16[32,16,128]{2,1,0:T(8,128)(2,1)S(1)} %get-tuple-element.24.refs_0_), channel_id=1, source_target_pairs={{0,28},{4,0},{8,4},{12,8},{16,12},{20,16},{24,20},{28,24},{1,29},{... | collective-permute-start | bytes 393224 | tf_op jit(solution)/shard_map/ppermute | solution.py:19
  41.7 0.9 %collective-permute-start.12 = (bf16[32,16,128]{2,1,0:T(8,128)(2,1)S(1)}, bf16[32,16,128]{2,1,0:T(8,128)(2,1)S(1)}, u32[]{:S(2)}, u32[]{:S(2)}) collective-permute-start(bf16[32,16,128]{2,1,0:T(8,128)(2,1)S(1)} %collective-permute-done.8.refs_1_), channel_id=1, source_target_pairs={{0,28},{4,0},{8,4},{12,8},{16,12},{20,16},{24,20},{28,24},{1,29},{... | collective-permute-start | bytes 393224 | tf_op jit(solution)/shard_map/ppermute | solution.py:19
  42.6 2.8 %collective-permute-start.17 = (bf16[32,16,128]{2,1,0:T(8,128)(2,1)S(1)}, bf16[32,16,128]{2,1,0:T(8,128)(2,1)S(1)}, u32[]{:S(2)}, u32[]{:S(2)}) collective-permute-start(bf16[32,16,128]{2,1,0:T(8,128)(2,1)S(1)} %collective-permute-done.16.refs_11_), channel_id=1, source_target_pairs={{0,3},{1,0},{2,1},{3,2},{4,7},{5,4},{6,5},{7,6},{8,11},{9,8},{10,9... | collective-permute-start | bytes 393224 | tf_op jit(solution)/shard_map/ppermute | solution.py:19
  45.4 2.8 %collective-permute-start.14 = (bf16[32,16,128]{2,1,0:T(8,128)(2,1)S(1)}, bf16[32,16,128]{2,1,0:T(8,128)(2,1)S(1)}, u32[]{:S(2)}, u32[]{:S(2)}) collective-permute-start(bf16[32,16,128]{2,1,0:T(8,128)(2,1)S(1)} %collective-permute-done.10.refs_3_), channel_id=1, source_target_pairs={{0,28},{4,0},{8,4},{12,8},{16,12},{20,16},{24,20},{28,24},{1,29},{... | collective-permute-start | bytes 393224 | tf_op jit(solution)/shard_map/ppermute | solution.py:19
  48.2 0.3 fusion.4
  48.5 1.9 %collective-permute-start.13 = (bf16[32,16,128]{2,1,0:T(8,128)(2,1)S(1)}, bf16[32,16,128]{2,1,0:T(8,128)(2,1)S(1)}, u32[]{:S(2)}, u32[]{:S(2)}) collective-permute-start(bf16[32,16,128]{2,1,0:T(8,128)(2,1)S(1)} %collective-permute-done.9.refs_2_), channel_id=1, source_target_pairs={{0,28},{4,0},{8,4},{12,8},{16,12},{20,16},{24,20},{28,24},{1,29},{... | collective-permute-start | bytes 393224 | tf_op jit(solution)/shard_map/ppermute | solution.py:19
  50.4 0.4 maximum_bitcast_fusion
  50.8 0.2 copy.56
  51.0 0.3 reshape.26.refs_8_.refs_16_
  51.4 1.7 %collective-permute-start.21 = (bf16[32,16,128]{2,1,0:T(8,128)(2,1)S(1)}, bf16[32,16,128]{2,1,0:T(8,128)(2,1)S(1)}, u32[]{:S(2)}, u32[]{:S(2)}) collective-permute-start(bf16[32,16,128]{2,1,0:T(8,128)(2,1)S(1)} %collective-permute-done.16.refs_11_), channel_id=1, source_target_pairs={{0,28},{4,0},{8,4},{12,8},{16,12},{20,16},{24,20},{28,24},{1,29},{... | collective-permute-start | bytes 393224 | tf_op jit(solution)/shard_map/ppermute | solution.py:19
  53.1 1.4 %collective-permute-start.20 = (bf16[32,16,128]{2,1,0:T(8,128)(2,1)S(1)}, bf16[32,16,128]{2,1,0:T(8,128)(2,1)S(1)}, u32[]{:S(2)}, u32[]{:S(2)}) collective-permute-start(bf16[32,16,128]{2,1,0:T(8,128)(2,1)S(1)} %collective-permute-done.17.refs_10_), channel_id=1, source_target_pairs={{0,28},{4,0},{8,4},{12,8},{16,12},{20,16},{24,20},{28,24},{1,29},{... | collective-permute-start | bytes 393224 | tf_op jit(solution)/shard_map/ppermute | solution.py:19
  54.6 0.8 %copy.57 = bf16[16,1,64,128]{3,2,1,0:T(8,128)(2,1)} copy(bf16[16,1,64,128]{3,0,2,1:T(8,128)(2,1)S(1)} %maximum_bitcast_fusion.1) | data formatting | bytes 524288
  55.4 1.5 %lower_grad.1.refs_17_ = bf16[8,2,48,256]{3,2,1,0:T(8,128)(2,1)S(1)} custom-call(bf16[32,16,128]{2,1,0:T(8,128)(2,1)S(1)} %get-tuple-element.24.refs_0_, bf16[32,16,128]{2,1,0:T(8,128)(2,1)S(1)} %collective-permute-done.8.refs_1_, bf16[32,16,128]{2,1,0:T(8,128)(2,1)S(1)} %collective-permute-done.9.refs_2_, ...), custom_call_target="tpu_custom_call" | custom-call | flops 150994944 | bytes 1048576 | tf_op jit(solution)/shard_map/lower_grad/pallas_call | solution.py:228
  56.9 0.3 collective-permute-done.21.refs_15_
  57.2 1.4 %collective-permute-done.19.refs_13_ = bf16[32,16,128]{2,1,0:T(8,128)(2,1)S(1)} collective-permute-done((bf16[32,16,128]{2,1,0:T(8,128)(2,1)S(1)}, bf16[32,16,128]{2,1,0:T(8,128)(2,1)S(1)}, u32[]{:S(2)}, u32[]{:S(2)}) %collective-permute-start.19) | collective-permute-done | bytes 131104 | tf_op jit(solution)/shard_map/ppermute | solution.py:19
  58.6 1.4 %collective-permute-done.20.refs_14_ = bf16[32,16,128]{2,1,0:T(8,128)(2,1)S(1)} collective-permute-done((bf16[32,16,128]{2,1,0:T(8,128)(2,1)S(1)}, bf16[32,16,128]{2,1,0:T(8,128)(2,1)S(1)}, u32[]{:S(2)}, u32[]{:S(2)}) %collective-permute-start.20) | collective-permute-done | bytes 131104 | tf_op jit(solution)/shard_map/ppermute | solution.py:19
  60.0 3.3 %upper_grad.1 = bf16[8,2,128,256]{3,2,1,0:T(8,128)(2,1)} custom-call(bf16[32,16,128]{2,1,0:T(8,128)(2,1)S(1)} %get-tuple-element.24.refs_0_, bf16[32,16,128]{2,1,0:T(8,128)(2,1)S(1)} %collective-permute-done.8.refs_1_, bf16[32,16,128]{2,1,0:T(8,128)(2,1)S(1)} %collective-permute-done.9.refs_2_, bf16[32,16,128]{2,1,0:T(8,128)(2,1)S(1)} %collective-permute-done.10.refs_3_, ...), custom_call_target="tpu_custom_call" | custom-call | flops 251658240 | bytes 2097152 | tf_op jit(solution)/shard_map/upper_grad/pallas_call | solution.py:228
  (47 shorter events, 1.2 us)
Async XLA Ops:
  0.6 4.0 %copy-start = (bf16[64,32,3,3,3]{0,1,4,3,2:T(8,128)(2,1)S(1)}, bf16[64,32,3,3,3]{0,1,4,3,2:T(8,128)(2,1)}, u32[]{:S(2)}) copy-start(bf16[64,32,3,3,3]{0,1,4,3,2:T(8,128)(2,1)} %param.5) | copy-start | bytes 331780
  1.8 4.3 %copy-start.2 = (bf16[16,1,64,128]{3,2,1,0:T(8,128)(2,1)S(1)}, bf16[16,1,64,128]{3,2,1,0:T(8,128)(2,1)}, u32[]{:S(2)}) copy-start(bf16[16,1,64,128]{3,2,1,0:T(8,128)(2,1)} %param.7) | copy-start | bytes 786436
  1.9 8.3 %collective-permute-start = (bf16[8,80,256]{2,1,0:T(8,128)(2,1)S(1)}, bf16[8,80,256]{2,1,0:T(8,128)(2,1)S(1)}, u32[]{:S(2)}, u32[]{:S(2)}) collective-permute-start(bf16[8,80,256]{2,1,0:T(8,128)(2,1)S(1)} %pad_maximum_fusion.1), channel_id=1, source_target_pairs={{0,4},{4,8},{8,12},{12,16},{16,20},{20,24},{24,28},{28,0},{1,5},{5... | collective-permute-start | bytes 983048 | tf_op jit(solution)/shard_map/ppermute | solution.py:19
  4.5 1.8 %copy-start.1 = (bf16[8,2,128,256]{3,2,1,0:T(8,128)(2,1)S(1)}, bf16[8,2,128,256]{3,2,1,0:T(8,128)(2,1)}, u32[]{:S(2)}) copy-start(bf16[8,2,128,256]{3,2,1,0:T(8,128)(2,1)} %field_ref.1) | copy-start | bytes 3145732
  4.5 8.1 %collective-permute-start.4 = (bf16[8,48,256]{2,1,0:T(8,128)(2,1)S(1)}, bf16[8,48,256]{2,1,0:T(8,128)(2,1)S(1)}, u32[]{:S(2)}, u32[]{:S(2)}) collective-permute-start(bf16[8,48,256]{2,1,0:T(8,128)(2,1)S(1)} %slice.73), channel_id=1, source_target_pairs={{0,4},{4,8},{8,12},{12,16},{16,20},{20,24},{24,28},{28,0},{1,5},{5... | collective-permute-start | bytes 589832 | tf_op jit(solution)/shard_map/ppermute | solution.py:19
  11.3 6.6 %collective-permute-start.1 = (bf16[32,16,128]{2,1,0:T(8,128)(2,1)S(1)}, bf16[32,16,128]{2,1,0:T(8,128)(2,1)S(1)}, u32[]{:S(2)}, u32[]{:S(2)}) collective-permute-start(bf16[32,16,128]{2,1,0:T(8,128)(2,1)S(1)} %get-tuple-element.15), channel_id=1, source_target_pairs={{0,1},{1,2},{2,3},{3,0},{4,5},{5,6},{6,7},{7,4},{8,9},{9,10},{10,1... | collective-permute-start | bytes 393224 | tf_op jit(solution)/shard_map/ppermute | solution.py:19
  13.8 12.0 %copy-start.3 = (f32[16]{0:T(128)S(1)}, f32[16]{0:T(128)}, u32[]{:S(2)}) copy-start(f32[16]{0:T(128)} %param.6) | copy-start | bytes 196
  13.8 7.6 %collective-permute-start.5 = (bf16[32,16,128]{2,1,0:T(8,128)(2,1)S(1)}, bf16[32,16,128]{2,1,0:T(8,128)(2,1)S(1)}, u32[]{:S(2)}, u32[]{:S(2)}) collective-permute-start(bf16[32,16,128]{2,1,0:T(8,128)(2,1)S(1)} %get-tuple-element.20), channel_id=1, source_target_pairs={{0,3},{1,0},{2,1},{3,2},{4,7},{5,4},{6,5},{7,6},{8,11},{9,8},{10,9... | collective-permute-start | bytes 393224 | tf_op jit(solution)/shard_map/ppermute | solution.py:19
  16.4 9.1 %collective-permute-start.3 = (bf16[32,16,128]{2,1,0:T(8,128)(2,1)S(1)}, bf16[32,16,128]{2,1,0:T(8,128)(2,1)S(1)}, u32[]{:S(2)}, u32[]{:S(2)}) collective-permute-start(bf16[32,16,128]{2,1,0:T(8,128)(2,1)S(1)} %get-tuple-element.17), channel_id=1, source_target_pairs={{0,3},{1,0},{2,1},{3,2},{4,7},{5,4},{6,5},{7,6},{8,11},{9,8},{10,9... | collective-permute-start | bytes 393224 | tf_op jit(solution)/shard_map/ppermute | solution.py:19
  18.0 7.8 %collective-permute-start.2 = (bf16[32,16,128]{2,1,0:T(8,128)(2,1)S(1)}, bf16[32,16,128]{2,1,0:T(8,128)(2,1)S(1)}, u32[]{:S(2)}, u32[]{:S(2)}) collective-permute-start(bf16[32,16,128]{2,1,0:T(8,128)(2,1)S(1)} %add.23), channel_id=1, source_target_pairs={{0,1},{1,2},{2,3},{3,0},{4,5},{5,6},{6,7},{7,4},{8,9},{9,10},{10,1... | collective-permute-start | bytes 393224 | tf_op jit(solution)/shard_map/ppermute | solution.py:19
  18.2 10.5 %collective-permute-start.7 = (bf16[32,16,128]{2,1,0:T(8,128)(2,1)S(1)}, bf16[32,16,128]{2,1,0:T(8,128)(2,1)S(1)}, u32[]{:S(2)}, u32[]{:S(2)}) collective-permute-start(bf16[32,16,128]{2,1,0:T(8,128)(2,1)S(1)} %get-tuple-element.22), channel_id=1, source_target_pairs={{0,1},{1,2},{2,3},{3,0},{4,5},{5,6},{6,7},{7,4},{8,9},{9,10},{10,1... | collective-permute-start | bytes 393224 | tf_op jit(solution)/shard_map/ppermute | solution.py:19
  21.5 12.4 %collective-permute-start.6 = (bf16[32,16,128]{2,1,0:T(8,128)(2,1)S(1)}, bf16[32,16,128]{2,1,0:T(8,128)(2,1)S(1)}, u32[]{:S(2)}, u32[]{:S(2)}) collective-permute-start(bf16[32,16,128]{2,1,0:T(8,128)(2,1)S(1)} %add.24), channel_id=1, source_target_pairs={{0,3},{1,0},{2,1},{3,2},{4,7},{5,4},{6,5},{7,6},{8,11},{9,8},{10,9... | collective-permute-start | bytes 393224 | tf_op jit(solution)/shard_map/ppermute | solution.py:19
  26.1 11.5 %collective-permute-start.8 = (bf16[32,16,128]{2,1,0:T(8,128)(2,1)S(1)}, bf16[32,16,128]{2,1,0:T(8,128)(2,1)S(1)}, u32[]{:S(2)}, u32[]{:S(2)}) collective-permute-start(bf16[32,16,128]{2,1,0:T(8,128)(2,1)S(1)} %get-tuple-element.24.refs_0_), channel_id=1, source_target_pairs={{0,1},{1,2},{2,3},{3,0},{4,5},{5,6},{6,7},{7,4},{8,9},{9,10},{10,1... | collective-permute-start | bytes 393224 | tf_op jit(solution)/shard_map/ppermute | solution.py:19
  34.1 7.5 %collective-permute-start.16 = (bf16[32,16,128]{2,1,0:T(8,128)(2,1)S(1)}, bf16[32,16,128]{2,1,0:T(8,128)(2,1)S(1)}, u32[]{:S(2)}, u32[]{:S(2)}) collective-permute-start(bf16[32,16,128]{2,1,0:T(8,128)(2,1)S(1)} %get-tuple-element.25.refs_8_), channel_id=1, source_target_pairs={{0,3},{1,0},{2,1},{3,2},{4,7},{5,4},{6,5},{7,6},{8,11},{9,8},{10,9... | collective-permute-start | bytes 393224 | tf_op jit(solution)/shard_map/ppermute | solution.py:19
  34.2 8.4 %collective-permute-start.15 = (bf16[32,16,128]{2,1,0:T(8,128)(2,1)S(1)}, bf16[32,16,128]{2,1,0:T(8,128)(2,1)S(1)}, u32[]{:S(2)}, u32[]{:S(2)}) collective-permute-start(bf16[32,16,128]{2,1,0:T(8,128)(2,1)S(1)} %get-tuple-element.25.refs_8_), channel_id=1, source_target_pairs={{0,1},{1,2},{2,3},{3,0},{4,5},{5,6},{6,7},{7,4},{8,9},{9,10},{10,1... | collective-permute-start | bytes 393224 | tf_op jit(solution)/shard_map/ppermute | solution.py:19
  35.7 9.8 %collective-permute-start.10 = (bf16[32,16,128]{2,1,0:T(8,128)(2,1)S(1)}, bf16[32,16,128]{2,1,0:T(8,128)(2,1)S(1)}, u32[]{:S(2)}, u32[]{:S(2)}) collective-permute-start(bf16[32,16,128]{2,1,0:T(8,128)(2,1)S(1)} %get-tuple-element.24.refs_0_), channel_id=1, source_target_pairs={{0,3},{1,0},{2,1},{3,2},{4,7},{5,4},{6,5},{7,6},{8,11},{9,8},{10,9... | collective-permute-start | bytes 393224 | tf_op jit(solution)/shard_map/ppermute | solution.py:19
  37.6 10.9 %collective-permute-start.9 = (bf16[32,16,128]{2,1,0:T(8,128)(2,1)S(1)}, bf16[32,16,128]{2,1,0:T(8,128)(2,1)S(1)}, u32[]{:S(2)}, u32[]{:S(2)}) collective-permute-start(bf16[32,16,128]{2,1,0:T(8,128)(2,1)S(1)} %collective-permute-done.8.refs_1_), channel_id=1, source_target_pairs={{0,1},{1,2},{2,3},{3,0},{4,5},{5,6},{6,7},{7,4},{8,9},{9,10},{10,1... | collective-permute-start | bytes 393224 | tf_op jit(solution)/shard_map/ppermute | solution.py:19
  37.9 13.5 %collective-permute-start.11 = (bf16[32,16,128]{2,1,0:T(8,128)(2,1)S(1)}, bf16[32,16,128]{2,1,0:T(8,128)(2,1)S(1)}, u32[]{:S(2)}, u32[]{:S(2)}) collective-permute-start(bf16[32,16,128]{2,1,0:T(8,128)(2,1)S(1)} %get-tuple-element.24.refs_0_), channel_id=1, source_target_pairs={{0,28},{4,0},{8,4},{12,8},{16,12},{20,16},{24,20},{28,24},{1,29},{... | collective-permute-start | bytes 393224 | tf_op jit(solution)/shard_map/ppermute | solution.py:19
  41.7 11.5 %collective-permute-start.12 = (bf16[32,16,128]{2,1,0:T(8,128)(2,1)S(1)}, bf16[32,16,128]{2,1,0:T(8,128)(2,1)S(1)}, u32[]{:S(2)}, u32[]{:S(2)}) collective-permute-start(bf16[32,16,128]{2,1,0:T(8,128)(2,1)S(1)} %collective-permute-done.8.refs_1_), channel_id=1, source_target_pairs={{0,28},{4,0},{8,4},{12,8},{16,12},{20,16},{24,20},{28,24},{1,29},{... | collective-permute-start | bytes 393224 | tf_op jit(solution)/shard_map/ppermute | solution.py:19
  42.6 8.8 %collective-permute-start.17 = (bf16[32,16,128]{2,1,0:T(8,128)(2,1)S(1)}, bf16[32,16,128]{2,1,0:T(8,128)(2,1)S(1)}, u32[]{:S(2)}, u32[]{:S(2)}) collective-permute-start(bf16[32,16,128]{2,1,0:T(8,128)(2,1)S(1)} %collective-permute-done.16.refs_11_), channel_id=1, source_target_pairs={{0,3},{1,0},{2,1},{3,2},{4,7},{5,4},{6,5},{7,6},{8,11},{9,8},{10,9... | collective-permute-start | bytes 393224 | tf_op jit(solution)/shard_map/ppermute | solution.py:19
  45.4 7.7 %collective-permute-start.14 = (bf16[32,16,128]{2,1,0:T(8,128)(2,1)S(1)}, bf16[32,16,128]{2,1,0:T(8,128)(2,1)S(1)}, u32[]{:S(2)}, u32[]{:S(2)}) collective-permute-start(bf16[32,16,128]{2,1,0:T(8,128)(2,1)S(1)} %collective-permute-done.10.refs_3_), channel_id=1, source_target_pairs={{0,28},{4,0},{8,4},{12,8},{16,12},{20,16},{24,20},{28,24},{1,29},{... | collective-permute-start | bytes 393224 | tf_op jit(solution)/shard_map/ppermute | solution.py:19
  48.5 6.9 %collective-permute-start.13 = (bf16[32,16,128]{2,1,0:T(8,128)(2,1)S(1)}, bf16[32,16,128]{2,1,0:T(8,128)(2,1)S(1)}, u32[]{:S(2)}, u32[]{:S(2)}) collective-permute-start(bf16[32,16,128]{2,1,0:T(8,128)(2,1)S(1)} %collective-permute-done.9.refs_2_), channel_id=1, source_target_pairs={{0,28},{4,0},{8,4},{12,8},{16,12},{20,16},{24,20},{28,24},{1,29},{... | collective-permute-start | bytes 393224 | tf_op jit(solution)/shard_map/ppermute | solution.py:19
  51.3 5.6 %collective-permute-start.18 = (bf16[32,16,128]{2,1,0:T(8,128)(2,1)S(1)}, bf16[32,16,128]{2,1,0:T(8,128)(2,1)S(1)}, u32[]{:S(2)}, u32[]{:S(2)}) collective-permute-start(bf16[32,16,128]{2,1,0:T(8,128)(2,1)S(1)} %get-tuple-element.25.refs_8_), channel_id=1, source_target_pairs={{0,28},{4,0},{8,4},{12,8},{16,12},{20,16},{24,20},{28,24},{1,29},{... | collective-permute-start | bytes 393224 | tf_op jit(solution)/shard_map/ppermute | solution.py:19
  51.4 5.8 %collective-permute-start.21 = (bf16[32,16,128]{2,1,0:T(8,128)(2,1)S(1)}, bf16[32,16,128]{2,1,0:T(8,128)(2,1)S(1)}, u32[]{:S(2)}, u32[]{:S(2)}) collective-permute-start(bf16[32,16,128]{2,1,0:T(8,128)(2,1)S(1)} %collective-permute-done.16.refs_11_), channel_id=1, source_target_pairs={{0,28},{4,0},{8,4},{12,8},{16,12},{20,16},{24,20},{28,24},{1,29},{... | collective-permute-start | bytes 393224 | tf_op jit(solution)/shard_map/ppermute | solution.py:19
  53.1 5.5 %collective-permute-start.19 = (bf16[32,16,128]{2,1,0:T(8,128)(2,1)S(1)}, bf16[32,16,128]{2,1,0:T(8,128)(2,1)S(1)}, u32[]{:S(2)}, u32[]{:S(2)}) collective-permute-start(bf16[32,16,128]{2,1,0:T(8,128)(2,1)S(1)} %collective-permute-done.15.refs_9_), channel_id=1, source_target_pairs={{0,28},{4,0},{8,4},{12,8},{16,12},{20,16},{24,20},{28,24},{1,29},{... | collective-permute-start | bytes 393224 | tf_op jit(solution)/shard_map/ppermute | solution.py:19
  53.1 6.8 %collective-permute-start.20 = (bf16[32,16,128]{2,1,0:T(8,128)(2,1)S(1)}, bf16[32,16,128]{2,1,0:T(8,128)(2,1)S(1)}, u32[]{:S(2)}, u32[]{:S(2)}) collective-permute-start(bf16[32,16,128]{2,1,0:T(8,128)(2,1)S(1)} %collective-permute-done.17.refs_10_), channel_id=1, source_target_pairs={{0,28},{4,0},{8,4},{12,8},{16,12},{20,16},{24,20},{28,24},{1,29},{... | collective-permute-start | bytes 393224 | tf_op jit(solution)/shard_map/ppermute | solution.py:19

commit v3 on v2

v3 whole, which is shorter than its diff:
```python
import functools

import jax
import jax.numpy as jnp
from jax import lax
from jax.experimental import pallas as pl
from jax.experimental.pallas import tpu as pltpu
from jax.sharding import PartitionSpec as P

F32 = jnp.float32
BF16 = jnp.bfloat16
LANES = 128
ROWS = 16
PARAMS = pltpu.CompilerParams(vmem_limit_bytes=24 * 1024 * 1024)


OPT = dict(rs_relay=(1, 1), ag_relay=(1, 1), ag_tie=1, gx_merge=1, delay=1, lower=32, fold=1, tie_own=0, rs_tie=2, tie_act=1)


def ring_device(place, count):
    if not OPT["fold"]:
        return place
    return jnp.where(2 * place < count, 2 * place, 2 * (count - place) - 1)


def ring_place(device, count):
    if not OPT["fold"]:
        return device
    return jnp.where(device % 2 == 0, device // 2, count - (device + 1) // 2)


def shifted(block, axis, distance):
    count = lax.axis_size(axis)
    ring = list(range(count))
    if axis == "col" and OPT["fold"]:
        ring = ring[::2] + ring[1::2][::-1]
    return lax.ppermute(block, axis, [(ring[i], ring[(i + distance) % count]) for i in range(count)])


def one_hot(shape, rule):
    rows = lax.broadcasted_iota(jnp.int32, shape, 0)
    cols = lax.broadcasted_iota(jnp.int32, shape, 1)
    return jnp.where(rule(rows, cols), 1.0, 0.0).astype(BF16)


def dot(left, right):
    return jnp.dot(left, right, preferred_element_type=F32)


def fill_taps(blocks, chans, span_z, taps_ref, first_row):
    half_z = span_z // 2
    size = chans * ROWS
    swap = one_hot((size, size), lambda r, c: c == (r % chans) * ROWS + r // chans)
    split = one_hot(
        (span_z, 3 * half_z),
        lambda z, m: z == (2 * (m % half_z) + m // half_z + span_z - 1) % span_z,
    )
    pair = 2 * chans
    beside = jnp.concatenate([values() for values, _, _, _ in blocks], axis=1)
    swapped = dot(swap, beside).astype(BF16)
    below = [swapped[:, i * span_z : (i + 1) * span_z] for i in range(len(blocks))]
    tapped = dot(jnp.concatenate(below, axis=0), split).astype(BF16)
    for index, (_, first, count, place) in enumerate(blocks):
        for j in range(count):
            for tap in range(3):
                source = index * size + (first + j) * pair
                row = first_row + tap * pair
                lane = (place + j) * half_z
                taps_ref[row : row + pair, lane : lane + half_z] = tapped[
                    source : source + pair, tap * half_z : (tap + 1) * half_z
                ]


def rows_of(ref, index, block):
    def values():
        rows = ref[(slice(None), *index, slice(block * ROWS, (block + 1) * ROWS))]
        return rows.reshape(rows.shape[0] * ROWS, rows.shape[-1])

    return values


def tap_sums(weights, taps_ref, lane, width, half_z):
    before = taps_ref[:, lane : lane + width]
    here = taps_ref[:, lane + half_z : lane + half_z + width]
    return dot(weights, jnp.concatenate([before, here], axis=0))


def local_kernel(field_ref, weight_ref, acc_ref, taps_ref):
    chans, planes, span_y, span_z = field_ref.shape
    half_z = span_z // 2
    count = span_y // ROWS
    for plane in range(planes):
        blocks = [(rows_of(field_ref, (plane,), b), 0, 8, 1 + 8 * b) for b in range(count)]
        fill_taps(blocks, chans, span_z, taps_ref, plane * 6 * chans)
    taps_ref[:, :half_z] = taps_ref[:, count * 8 * half_z :]
    weights = weight_ref[...]
    width = 8 * half_z
    for step in range(count):
        lane = step * width
        acc_ref[:, lane : lane + width] = tap_sums(weights, taps_ref, lane, width, half_z)


def halo_kernel(counts, halo_ref, weight_ref, acc_ref, *refs):
    *part_refs, taps_ref = refs
    chans, span_y, span_z = halo_ref.shape
    half_z = span_z // 2
    blocks = [(rows_of(halo_ref, (), b), 0, 8, 1 + 8 * b) for b in range(span_y // ROWS)]
    fill_taps(blocks, chans, span_z, taps_ref, 0)
    taps_ref[:, :half_z] = taps_ref[:, span_y // 2 * half_z :]
    weights = weight_ref[...]
    peers = len(part_refs) // len(counts)
    rows = part_refs[0].shape[1]
    width = 8 * half_z
    for step in range(span_y // 16):
        lane = step * width
        sums = acc_ref[:, lane : lane + width]
        sums = (sums + tap_sums(weights, taps_ref, lane, width, half_z)).astype(BF16)
        part = int(step * 8 >= counts[0])
        first = step * 8 - part * counts[0]
        for j in range(8):
            for peer in range(peers):
                part_refs[part * peers + peer][first + j] = sums[
                    peer * rows : (peer + 1) * rows, j * half_z : (j + 1) * half_z
                ]


def add_kernel(one_ref, two_ref, sum_ref):
    sum_ref[...] = (one_ref[...].astype(F32) + two_ref[...].astype(F32)).astype(BF16)


def act_kernel(*refs):
    *part_refs, bias_ref, cot_ref, out_ref, masked_ref = refs
    pre = bias_ref[...] + functools.reduce(
        lambda a, b: a + b, [ref[...].astype(F32) for ref in part_refs]
    )
    small = jnp.exp(-jnp.abs(pre))
    soft = jnp.maximum(pre, 0.0) + jnp.log(1.0 + small)
    out_ref[...] = (0.3 * pre + 0.7 * soft).astype(BF16)
    gate = jnp.where(pre >= 0.0, 1.0, small) / (1.0 + small)
    masked_ref[...] = (cot_ref[...].astype(F32) * (0.3 + 0.7 * gate)).astype(BF16)


def grad_blocks(held_ref, weights, blocks, chans, span_z, store):
    half_z = span_z // 2
    size = chans * ROWS
    swap = one_hot((size, size), lambda r, c: c == (r % ROWS) * chans + r // ROWS)
    weave = one_hot((span_z, span_z), lambda m, z: z == 2 * (m % half_z) + m // half_z)
    pair = 2 * chans
    width = blocks * 8 * half_z
    here, after = held_ref[:, :width], held_ref[:, half_z : half_z + width]
    sums = dot(weights, jnp.concatenate([here, after], axis=0))
    beside = []
    for step in range(blocks):
        for parity_x in range(2):
            base = parity_x * 3 * pair
            rows = []
            for j in range(step * 8, step * 8 + 8):
                tile = sums[base : base + 3 * pair, j * half_z : (j + 1) * half_z]
                even = tile[:pair]
                odd = tile[pair : 2 * pair] + pltpu.roll(tile[2 * pair :], half_z - 1, 1)
                rows.append(jnp.concatenate([even.astype(BF16), odd.astype(BF16)], axis=1))
            beside.append(jnp.concatenate(rows, axis=0))
    swapped = dot(swap, jnp.concatenate(beside, axis=1)).astype(BF16)
    below = [swapped[:, i * span_z : (i + 1) * span_z] for i in range(2 * blocks)]
    woven = dot(jnp.concatenate(below, axis=0), weave).astype(BF16)
    for step in range(blocks):
        for parity_x in range(2):
            for chan in range(chans):
                first = (step * 2 + parity_x) * size + chan * ROWS
                store(chan, parity_x, step, woven[first : first + ROWS])


def lower_grad_kernel(pieces, *refs):
    *piece_refs, weight_ref, grad_ref, held_ref = refs
    chans, _, span_y, span_z = grad_ref.shape
    half_z = span_z // 2
    for index, ((number, first), _) in enumerate(pieces):
        row = index * ROWS
        for j in range(span_y // 2 + 1):
            held_ref[row : row + ROWS, j * half_z : (j + 1) * half_z] = piece_refs[number][first + j]

    def store(chan, parity_x, step, values):
        grad_ref[chan, parity_x, step * ROWS : (step + 1) * ROWS, :] = values

    grad_blocks(held_ref, weight_ref[...], span_y // ROWS, chans, span_z, store)


def upper_grad_kernel(pieces, counts, *refs):
    *piece_refs, weight_ref, lower_ref, grad_ref, held_ref = refs
    chans, _, span_y, span_z = grad_ref.shape
    half_z = span_z // 2
    done = lower_ref.shape[2]
    grad_ref[:, :, :done, :] = lower_ref[...]
    for index, ((low, low_first), (high, high_first)) in enumerate(pieces):
        row = index * ROWS
        tiles = [(low, low_first + j) for j in range(done // 2, counts[0])]
        tiles += [(high, high_first + j) for j in range(counts[1])] + [(low, low_first)]
        for place, (number, j) in enumerate(tiles):
            held_ref[row : row + ROWS, place * half_z : (place + 1) * half_z] = piece_refs[number][j]

    def store(chan, parity_x, step, values):
        first = done + step * ROWS
        grad_ref[chan, parity_x, first : first + ROWS, :] = values

    grad_blocks(held_ref, weight_ref[...], (span_y - done) // ROWS, chans, span_z, store)


def weights_kernel(peers, me_ref, own_ref, local_ref, halo_ref, back_ref):
    _, chans, total = own_ref.shape
    rows = total // peers
    place = ring_place(me_ref[0], peers)

    def tile(tap_x, tap_y, tap_z):
        return own_ref[(tap_x * 3 + tap_y) * 3 + tap_z].astype(F32)

    none = jnp.zeros((chans, total), F32)

    def ahead(r, c):
        return c == ring_device((place + r // rows) % peers, peers) * rows + r % rows

    pick = one_hot((total, total), ahead)
    for ref, taps_x in ((local_ref, (1, 2)), (halo_ref, (0,))):
        tiles = [
            none if tap_y < 0 else tile(tap_x, tap_y, tap_z)
            for taps_y in ((-1, 0), (1, 2))
            for tap_x in taps_x
            for tap_z in range(3)
            for tap_y in taps_y
        ]
        stack = jnp.concatenate(tiles, axis=0).astype(BF16)
        ref[...] = lax.dot_general(
            pick, stack, (((1,), (1,)), ((), ())), preferred_element_type=F32
        ).astype(BF16)

    back = jnp.zeros(back_ref.shape, F32)
    by_offset = ((1, 2), (-1, 0))
    for offset in range(2):
        for plane in range(2):
            tiles = [
                none if min(tap_x, tap_y) < 0 else tile(tap_x, tap_y, tap_z)
                for tap_x in by_offset[plane]
                for tap_z in (1, 2, 0)
                for tap_y in by_offset[offset]
            ]
            stack = jnp.concatenate(tiles, axis=0).astype(BF16)
            first = (offset * 2 + plane) * total

            def behind(r, c, first=first):
                c = c - first
                device = ring_device((place + peers - c // rows) % peers, peers)
                return (r == device * rows + c % rows) & (c >= 0) & (c < total)

            back = back + dot(stack, one_hot((total, 4 * total), behind))
    back_ref[...] = back.astype(BF16)


def call(kernel, name, out_shape, args, scratch=(), flops=0, bytes_accessed=1 << 20, transcendentals=0):
    return pl.pallas_call(
        kernel,
        out_shape=out_shape,
        scratch_shapes=list(scratch),
        compiler_params=PARAMS,
        cost_estimate=pl.CostEstimate(
            flops=flops, bytes_accessed=bytes_accessed, transcendentals=transcendentals
        ),
        name=name,
    )(*args)


def on_device(field, kernel, bias, cotangent):
    peers = lax.axis_size("col")
    me = lax.axis_index("col")
    quarter = peers // 4
    cin, planes, span_y, span_z = field.shape
    cout = bias.shape[0]
    half_y, half_z = span_y // 2, span_z // 2
    counts = (OPT["lower"], half_y - OPT["lower"])
    starts = (0, counts[0])
    mid = 2 * counts[0]
    halo = shifted(field[:, planes - 1], "gx", 1)

    chans = -(-cin // 8) * 8
    rows = -(-cout // ROWS) * ROWS
    total = peers * rows
    fill_c = (0, chans - cin)
    fill_o = (0, rows - cout)
    own = lax.dynamic_slice_in_dim(jnp.transpose(kernel, (2, 3, 4, 1, 0)), me * cin, cin, 3)
    own = own.reshape(27, cin, peers, cout)
    own = jnp.pad(own, ((0, 0), fill_c, (0, 0), fill_o)).reshape(27, chans, total)
    field_p = jnp.pad(field, (fill_c, (0, 0), (0, 0), (0, 0)))

    points = half_y * half_z
    vmem = pl.BlockSpec(memory_space=pltpu.VMEM)
    weights_local, weights_halo, weights_back = pl.pallas_call(
        functools.partial(weights_kernel, peers),
        out_shape=[
            jax.ShapeDtypeStruct((total, 24 * chans), BF16),
            jax.ShapeDtypeStruct((total, 12 * chans), BF16),
            jax.ShapeDtypeStruct((12 * chans, 4 * total), BF16),
        ],
        in_specs=[pl.BlockSpec(memory_space=pltpu.SMEM), vmem],
        out_specs=[vmem] * 3,
        compiler_params=PARAMS,
        cost_estimate=pl.CostEstimate(flops=1 << 27, bytes_accessed=1 << 19, transcendentals=0),
        name="weights",
    )(me.astype(jnp.int32).reshape(1), own)
    acc = call(
        local_kernel,
        "local_planes",
        jax.ShapeDtypeStruct((total, points), F32),
        (field_p, weights_local),
        [
            pltpu.VMEM((planes * 6 * chans, (1 + half_y) * half_z), BF16),
        ],
        flops=2 * total * 24 * chans * points,
        bytes_accessed=1 << 22,
    )
    halo = jnp.pad(halo, (fill_c, (0, 0), (0, 0)))
    shapes = [jax.ShapeDtypeStruct((count, rows, half_z), BF16) for count in counts]
    sums = call(
        functools.partial(halo_kernel, counts),
        "halo_plane",
        [shapes[part] for part in range(2) for _ in range(peers)],
        (halo, weights_halo, acc),
        [
            pltpu.VMEM((6 * chans, (1 + half_y) * half_z), BF16),
        ],
        flops=2 * total * 12 * chans * points,
        bytes_accessed=1 << 22,
    )
    parts = (sums[:peers], sums[peers:])

    far = 2 * quarter
    steps = (quarter, peers - quarter)
    arrived = [[parts[h][0]] for h in range(2)]
    relayed = [shifted(parts[h][far], "col", steps[h]) if OPT["rs_relay"][h] else None for h in range(2)]
    for h in range(2):
        for r in range(1, peers):
            if not OPT["rs_relay"][h] or r not in (steps[h], far):
                sent = parts[h][r]
                if h and OPT["rs_tie"] >= 2:
                    sent, relayed[0] = lax.optimization_barrier((sent, relayed[0]))
                arrived[h].append(shifted(sent, "col", r))
    for h in range(2):
        if OPT["rs_tie"] == 1 or (OPT["rs_tie"] >= 3 and h == 0):
            relayed[h], arrived[h] = lax.optimization_barrier((relayed[h], arrived[h]))
        if OPT["rs_relay"][h]:
            joined = call(add_kernel, "add", shapes[h], (relayed[h], parts[h][steps[h]]))
            arrived[h].append(shifted(joined, "col", steps[h]))

    bias_p = jnp.broadcast_to(jnp.pad(bias, fill_o)[None, :, None], (1, rows, half_z))
    cot = jnp.pad(jnp.transpose(cotangent[:, 0], (1, 0, 2)), ((0, 0), fill_o, (0, 0)))
    acts = []
    for h in range(2):
        if h and OPT['tie_act']:
            bias_p, acts[0] = lax.optimization_barrier((bias_p, acts[0]))
        acts.append(
            call(
                act_kernel,
                "activation",
                (shapes[h], shapes[h]),
                (*arrived[h], bias_p, cot[starts[h] : starts[h] + counts[h]]),
                transcendentals=3 * counts[h] * rows * half_z,
            )
        )
    out = jnp.concatenate([out for out, _ in acts], axis=0)
    out_act = jnp.transpose(out[:, :cout], (1, 0, 2))[:, None]

    masked = [masked for _, masked in acts]
    gathered = [{0: masked[h]} for h in range(2)]
    for h in range(2):
        for r in range(1, peers):
            if r != far or not OPT["ag_relay"][h]:
                gathered[h][r] = shifted(masked[h], "col", r)
    above = [{}, {}]
    arrays = []

    def spec(value, *at):
        arrays.append(value)
        return len(arrays) - 1

    if OPT["gx_merge"]:
        whole = shifted(jnp.concatenate(masked, axis=0), "gx", -1)
        number = spec(whole)
        for h in range(2):
            above[h][0] = (number, starts[h])
    else:
        for h in range(2):
            above[h][0] = (spec(shifted(masked[h], "gx", -1)), 0)
    for h in range(2):
        if OPT["ag_tie"]:
            gathered[h] = lax.optimization_barrier(gathered[h])
        if h == 1 and OPT["tie_own"]:
            gathered[1][steps[1]], whole = lax.optimization_barrier((gathered[1][steps[1]], arrays[0]))
            arrays[0] = whole
    for h in range(2):
        near = [r for r in range(1, peers) if r != far]
        if OPT["gx_merge"]:
            number = spec(shifted(jnp.concatenate([gathered[h][r] for r in near], axis=0), "gx", -1))
            for i, r in enumerate(near):
                above[h][r] = (number, i * counts[h])
        else:
            for r in near:
                above[h][r] = (spec(shifted(gathered[h][r], "gx", -1)), 0)
    for h in range(2):
        if OPT["ag_relay"][h]:
            gathered[h][far] = shifted(gathered[h][steps[h]], "col", steps[h])
        above[h][far] = (spec(shifted(gathered[h][far], "gx", -1)), 0)
    mine = [{r: (spec(gathered[h][r]), 0) for r in range(peers)} for h in range(2)]
    order = [[places[h][r] for h in range(2)] for places in (mine, above) for r in range(peers)]

    def grad_call(kernel, name, shape, used, extra, blocks):
        used = sorted(used)
        renamed = [[(used.index(n) if n in used else -1, at) for n, at in both] for both in order]
        return call(
            functools.partial(kernel, renamed),
            name,
            shape,
            (*[arrays[n] for n in used], weights_back, *extra),
            [
                pltpu.VMEM((2 * total, (1 + 8 * blocks) * half_z), BF16),
            ],
            flops=8 * total * 12 * chans * 8 * blocks * half_z,
        )

    done = mid - ROWS
    lower = grad_call(
        lower_grad_kernel,
        "lower_grad",
        jax.ShapeDtypeStruct((chans, planes, done, span_z), BF16),
        {both[0][0] for both in order},
        (),
        done // ROWS,
    )
    in_grad = grad_call(
        lambda pieces, *refs: upper_grad_kernel(pieces, counts, *refs),
        "upper_grad",
        jax.ShapeDtypeStruct((chans, planes, span_y, span_z), BF16),
        {n for both in order for n, _ in both},
        (lower,),
        (span_y - done) // ROWS,
    )
    return out_act, in_grad[:cin]


def solution(mesh):
    in_specs = (P("col", "gx", None, None), P(), P("col"), P("col", "gx", None, None))
    out_specs = (P("col", "gx", None, None), P("col", "gx", None, None))
    return jax.shard_map(
        on_device, mesh=mesh, in_specs=in_specs, out_specs=out_specs, check_vma=False
    )
```

time: 63.4 us -> 60 us (0.946)
  starting transfers between devices: 27.8 us -> 35.5 us
  Pallas kernels: 11.5 us -> 6.25 us
  other arithmetic: 2.11 us -> 0.1 us
  local copies, waits for them, and re-layouts: 4.06 us -> 2.25 us
  waiting for transfers between devices: 16.9 us -> 15.1 us
    ppermute x22 -> x18, starting transfers between devices: 27.8 us -> 35.5 us  [shifted(): lax.ppermute(block, axis, [(ring[i], ring[(i + distance) % count]) for i...]
    pallas_call x9 -> x8, Pallas kernels: 11.5 us -> 6.01 us  [call(): pl.pallas_call(kernel, out_shape=out_shape, scratch_shapes=list(scratch),...]
    ppermute x22 -> x18, waiting for transfers between devices: 16.9 us -> 15.1 us  [shifted(): lax.ppermute(block, axis, [(ring[i], ring[(i + distance) % count]) for i...]
    another operation x4 -> x0, other arithmetic: 0.93 us -> none  [the longest x1 0.33 us: backward_weights(): by_z = jnp.stack([by_y[..., 1], by_y[..., 2], by_y[..., 0]])]
    reshape x6 -> x0, local copies, waits for them, and re-layouts: 0.91 us -> none  [the longest x1 0.34 us: backward_weights(): return turned.reshape(2 * 3 * 2 * cin, 2 * 2 * peers * rows)]
    concatenate x3, other arithmetic: 0.79 us -> 0.07 us  [the longest x2 0.05 us: on_device(): jnp.concatenate([gathered[h][r] for r in near], axis=0)]
  transfers between devices with their start and end apart: 22 -> 18, of which waited for: 8 -> 7; matrix products, arithmetic and copies ran while one was open for 8% -> 2% of each run, Pallas kernels for 13% -> 5%
where the time goes in v3:
time: 60 us; the launch traced here: 59.9 us
  starting transfers between devices  35.5 us (59%)
  waiting for transfers between devices  15.1 us (25%)
  Pallas kernels  6.25 us (10%)
  local copies, waits for them, and re-layouts  2.25 us (4%)
  between operations  0.75 us (1%)
    ppermute x18, starting transfers between devices, shifted(): lax.ppermute(block, axis, [(ring[i], ring[(i + distance) % count]) for i...  35.5 us
    ppermute x18, waiting for transfers between devices, shifted(): lax.ppermute(block, axis, [(ring[i], ring[(i + distance) % count]) for i...  15.1 us
    pallas_call x8, Pallas kernels, call(): pl.pallas_call(kernel, out_shape=out_shape, scratch_shapes=list(scratch),...  6.01 us
  transfers between devices with their start and end apart: 18, of which 7 were waited for; matrix products, arithmetic and copies ran while one was open for 2% of the time, Pallas kernels for 5%

profile of v3, /device:TPU:1, one launch (start us, length us, event | category | flops | bytes accessed | tf_op | source)
XLA Modules:
  0.0 59.9 jit_solution(12424187051379182165)
XLA Ops:
  0.6 0.0 copy-start
  0.7 1.2 %slice_bitcast_fusion = bf16[8,128,256]{2,1,0:T(8,128)(2,1)S(1)} fusion(bf16[8,2,128,256]{3,2,1,0:T(8,128)(2,1)} %field_ref.1), kind=kLoop, calls=%fused_computation | loop fusion | bytes 1048576 | tf_op jit(solution)/shard_map/squeeze | solution.py:280
  1.8 2.7 %collective-permute-start = (bf16[8,128,256]{2,1,0:T(8,128)(2,1)S(1)}, bf16[8,128,256]{2,1,0:T(8,128)(2,1)S(1)}, u32[]{:S(2)}, u32[]{:S(2)}) collective-permute-start(bf16[8,128,256]{2,1,0:T(8,128)(2,1)S(1)} %slice_bitcast_fusion), channel_id=1, source_target_pairs={{0,4},{4,8},{8,12},{12,16},{16,20},{20,24},{24,28},{28,0},{1,5},{5... | collective-permute-start | bytes 1572872 | tf_op jit(solution)/shard_map/ppermute | solution.py:37
  4.5 0.2 weights.1
  4.8 1.5 %local_planes.1.acc_ref = f32[64,8192]{1,0:T(8,128)S(1)} custom-call(bf16[8,2,128,256]{3,2,1,0:T(8,128)(2,1)S(1)} %copy-done.1, bf16[64,192]{1,0:T(8,128)(2,1)S(1)} %get-tuple-element.29.weight_ref), custom_call_target="tpu_custom_call" | custom-call | flops 201326592 | bytes 4194304 | tf_op jit(solution)/shard_map/local_planes/pallas_call | solution.py:258
  6.3 0.0 copy-start.2
  6.3 4.3 %collective-permute-done.halo_ref = bf16[8,128,256]{2,1,0:T(8,128)(2,1)S(1)} collective-permute-done((bf16[8,128,256]{2,1,0:T(8,128)(2,1)S(1)}, bf16[8,128,256]{2,1,0:T(8,128)(2,1)S(1)}, u32[]{:S(2)}, u32[]{:S(2)}) %collective-permute-start) | collective-permute-done | bytes 524320 | tf_op jit(solution)/shard_map/ppermute | solution.py:37
  10.6 1.0 %halo_plane.1 = (bf16[32,16,128]{2,1,0:T(8,128)(2,1)S(1)}, bf16[32,16,128]{2,1,0:T(8,128)(2,1)S(1)}, bf16[32,16,128]{2,1,0:T(8,128)(2,1)S(1)}, bf16[32,16,128]{2...) custom-call(bf16[8,128,256]{2,1,0:T(8,128)(2,1)S(1)} %collective-per, ...), custom_call_target="tpu_custom_call" | custom-call | flops 100663296 | bytes 4194304 | tf_op jit(solution)/shard_map/halo_plane/pallas_call | solution.py:258
  11.6 2.4 %collective-permute-start.2 = (bf16[32,16,128]{2,1,0:T(8,128)(2,1)S(1)}, bf16[32,16,128]{2,1,0:T(8,128)(2,1)S(1)}, u32[]{:S(2)}, u32[]{:S(2)}) collective-permute-start(bf16[32,16,128]{2,1,0:T(8,128)(2,1)S(1)} %get-tuple-element.33), channel_id=1, source_target_pairs={{0,2},{2,3},{3,1},{1,0},{4,6},{6,7},{7,5},{5,4},{8,10},{10,11},{11... | collective-permute-start | bytes 393224 | tf_op jit(solution)/shard_map/ppermute | solution.py:37
  14.0 0.0 collective-permute-start.5
  14.0 0.2 copy.11
  14.2 1.4 %collective-permute-start.1 = (bf16[32,16,128]{2,1,0:T(8,128)(2,1)S(1)}, bf16[32,16,128]{2,1,0:T(8,128)(2,1)S(1)}, u32[]{:S(2)}, u32[]{:S(2)}) collective-permute-start(bf16[32,16,128]{2,1,0:T(8,128)(2,1)S(1)} %get-tuple-element.31), channel_id=1, source_target_pairs={{0,1},{2,0},{3,2},{1,3},{4,5},{6,4},{7,6},{5,7},{8,9},{10,8},{11,1... | collective-permute-start | bytes 393224 | tf_op jit(solution)/shard_map/ppermute | solution.py:37
  15.6 0.4 collective-permute-done.2.one_ref
  15.9 2.9 %collective-permute-start.4 = (bf16[32,16,128]{2,1,0:T(8,128)(2,1)S(1)}, bf16[32,16,128]{2,1,0:T(8,128)(2,1)S(1)}, u32[]{:S(2)}, u32[]{:S(2)}) collective-permute-start(bf16[32,16,128]{2,1,0:T(8,128)(2,1)S(1)} %get-tuple-element.40), channel_id=1, source_target_pairs={{0,2},{2,3},{3,1},{1,0},{4,6},{6,7},{7,5},{5,4},{8,10},{10,11},{11... | collective-permute-start | bytes 393224 | tf_op jit(solution)/shard_map/ppermute | solution.py:37
  18.8 0.1 collective-permute-done.5.one_ref
  18.9 0.6 %collective-permute-start.6 = (bf16[32,16,128]{2,1,0:T(8,128)(2,1)S(1)}, bf16[32,16,128]{2,1,0:T(8,128)(2,1)S(1)}, u32[]{:S(2)}, u32[]{:S(2)}) collective-permute-start(bf16[32,16,128]{2,1,0:T(8,128)(2,1)S(1)} %add.7), channel_id=1, source_target_pairs={{0,1},{2,0},{3,2},{1,3},{4,5},{6,4},{7,6},{5,7},{8,9},{10,8},{11,1... | collective-permute-start | bytes 393224 | tf_op jit(solution)/shard_map/ppermute | solution.py:37
  19.6 1.8 %collective-permute-start.3 = (bf16[32,16,128]{2,1,0:T(8,128)(2,1)S(1)}, bf16[32,16,128]{2,1,0:T(8,128)(2,1)S(1)}, u32[]{:S(2)}, u32[]{:S(2)}) collective-permute-start(bf16[32,16,128]{2,1,0:T(8,128)(2,1)S(1)} %add.6), channel_id=1, source_target_pairs={{0,2},{2,3},{3,1},{1,0},{4,6},{6,7},{7,5},{5,4},{8,10},{10,11},{11... | collective-permute-start | bytes 393224 | tf_op jit(solution)/shard_map/ppermute | solution.py:37
  21.5 1.8 %collective-permute-done.1.refs_1_ = bf16[32,16,128]{2,1,0:T(8,128)(2,1)S(1)} collective-permute-done((bf16[32,16,128]{2,1,0:T(8,128)(2,1)S(1)}, bf16[32,16,128]{2,1,0:T(8,128)(2,1)S(1)}, u32[]{:S(2)}, u32[]{:S(2)}) %collective-permute-start.1) | collective-permute-done | bytes 131104 | tf_op jit(solution)/shard_map/ppermute | solution.py:37
  23.2 5.5 %collective-permute-done.3.refs_2_ = bf16[32,16,128]{2,1,0:T(8,128)(2,1)S(1)} collective-permute-done((bf16[32,16,128]{2,1,0:T(8,128)(2,1)S(1)}, bf16[32,16,128]{2,1,0:T(8,128)(2,1)S(1)}, u32[]{:S(2)}, u32[]{:S(2)}) %collective-permute-start.3) | collective-permute-done | bytes 131104 | tf_op jit(solution)/shard_map/ppermute | solution.py:37
  28.8 0.1 broadcast_in_dim.4.refs_3_
  28.8 0.2 activation.2
  29.1 2.9 %collective-permute-start.8 = (bf16[32,16,128]{2,1,0:T(8,128)(2,1)S(1)}, bf16[32,16,128]{2,1,0:T(8,128)(2,1)S(1)}, u32[]{:S(2)}, u32[]{:S(2)}) collective-permute-start(bf16[32,16,128]{2,1,0:T(8,128)(2,1)S(1)} %get-tuple-element.51.refs_3_.refs_5_), channel_id=1, source_target_pairs={{0,2},{2,3},{3,1},{1,0},{4,6},{6,7},{7,5},{5,4},{8,10},{10,11},{11... | collective-permute-start | bytes 393224 | tf_op jit(solution)/shard_map/ppermute | solution.py:37
  32.0 0.0 collective-permute-start.9
  32.0 0.0 collective-permute-done.4.refs_1_
  32.0 0.0 collective-permute-done.6.refs_2_
  32.0 0.2 activation.3
  32.2 2.4 %collective-permute-start.11 = (bf16[32,16,128]{2,1,0:T(8,128)(2,1)S(1)}, bf16[32,16,128]{2,1,0:T(8,128)(2,1)S(1)}, u32[]{:S(2)}, u32[]{:S(2)}) collective-permute-start(bf16[32,16,128]{2,1,0:T(8,128)(2,1)S(1)} %get-tuple-element.52.refs_9_), channel_id=1, source_target_pairs={{0,2},{2,3},{3,1},{1,0},{4,6},{6,7},{7,5},{5,4},{8,10},{10,11},{11... | collective-permute-start | bytes 393224 | tf_op jit(solution)/shard_map/ppermute | solution.py:37
  34.7 0.0 collective-permute-start.12
  34.7 4.1 %collective-permute-start.7 = (bf16[64,16,128]{2,1,0:T(8,128)(2,1)S(1)}, bf16[64,16,128]{2,1,0:T(8,128)(2,1)S(1)}, u32[]{:S(2)}, u32[]{:S(2)}) collective-permute-start(bf16[64,16,128]{2,1,0:T(8,128)(2,1)S(1)} %pad_maximum_fusion), channel_id=1, source_target_pairs={{0,28},{4,0},{8,4},{12,8},{16,12},{20,16},{24,20},{28,24},{1,29},{... | collective-permute-start | bytes 786440 | tf_op jit(solution)/shard_map/ppermute | solution.py:37
  38.8 0.0 collective-permute-done.8.refs_4_.refs_6_
  38.8 0.0 collective-permute-done.9.refs_6_.refs_8_
  38.8 2.6 %collective-permute-start.14 = (bf16[32,16,128]{2,1,0:T(8,128)(2,1)S(1)}, bf16[32,16,128]{2,1,0:T(8,128)(2,1)S(1)}, u32[]{:S(2)}, u32[]{:S(2)}) collective-permute-start(bf16[32,16,128]{2,1,0:T(8,128)(2,1)S(1)} %collective-permute-done.8.refs_4_.refs_6_), channel_id=1, source_target_pairs={{0,2},{2,3},{3,1},{1,0},{4,6},{6,7},{7,5},{5,4},{8,10},{10,11},{11... | collective-permute-start | bytes 393224 | tf_op jit(solution)/shard_map/ppermute | solution.py:37
  41.5 3.1 %collective-permute-start.10 = (bf16[64,16,128]{2,1,0:T(8,128)(2,1)S(1)}, bf16[64,16,128]{2,1,0:T(8,128)(2,1)S(1)}, u32[]{:S(2)}, u32[]{:S(2)}) collective-permute-start(bf16[64,16,128]{2,1,0:T(8,128)(2,1)S(1)} %pad_maximum_fusion.1), channel_id=1, source_target_pairs={{0,28},{4,0},{8,4},{12,8},{16,12},{20,16},{24,20},{28,24},{1,29},{... | collective-permute-start | bytes 786440 | tf_op jit(solution)/shard_map/ppermute | solution.py:37
  44.6 0.0 collective-permute-done.11.refs_10_
  44.7 0.0 collective-permute-done.12.refs_12_
  44.7 1.7 %collective-permute-start.16 = (bf16[32,16,128]{2,1,0:T(8,128)(2,1)S(1)}, bf16[32,16,128]{2,1,0:T(8,128)(2,1)S(1)}, u32[]{:S(2)}, u32[]{:S(2)}) collective-permute-start(bf16[32,16,128]{2,1,0:T(8,128)(2,1)S(1)} %collective-permute-done.12.refs_12_), channel_id=1, source_target_pairs={{0,1},{2,0},{3,2},{1,3},{4,5},{6,4},{7,6},{5,7},{8,9},{10,8},{11,1... | collective-permute-start | bytes 393224 | tf_op jit(solution)/shard_map/ppermute | solution.py:37
  46.4 1.8 %collective-permute-start.13 = (bf16[64,16,128]{2,1,0:T(8,128)(2,1)S(1)}, bf16[64,16,128]{2,1,0:T(8,128)(2,1)S(1)}, u32[]{:S(2)}, u32[]{:S(2)}) collective-permute-start(bf16[64,16,128]{2,1,0:T(8,128)(2,1)S(1)} %pad_maximum_fusion.2), channel_id=1, source_target_pairs={{0,28},{4,0},{8,4},{12,8},{16,12},{20,16},{24,20},{28,24},{1,29},{... | collective-permute-start | bytes 786440 | tf_op jit(solution)/shard_map/ppermute | solution.py:37
  48.2 0.0 collective-permute-done.14.refs_5_.refs_7_
  48.2 2.7 %collective-permute-start.15 = (bf16[32,16,128]{2,1,0:T(8,128)(2,1)S(1)}, bf16[32,16,128]{2,1,0:T(8,128)(2,1)S(1)}, u32[]{:S(2)}, u32[]{:S(2)}) collective-permute-start(bf16[32,16,128]{2,1,0:T(8,128)(2,1)S(1)} %collective-permute-done.14.refs_5_.refs_7_), channel_id=1, source_target_pairs={{0,28},{4,0},{8,4},{12,8},{16,12},{20,16},{24,20},{28,24},{1,29},{... | collective-permute-start | bytes 393224 | tf_op jit(solution)/shard_map/ppermute | solution.py:37
  50.9 0.0 collective-permute-done.16.refs_11_
  50.9 2.2 %collective-permute-start.17 = (bf16[32,16,128]{2,1,0:T(8,128)(2,1)S(1)}, bf16[32,16,128]{2,1,0:T(8,128)(2,1)S(1)}, u32[]{:S(2)}, u32[]{:S(2)}) collective-permute-start(bf16[32,16,128]{2,1,0:T(8,128)(2,1)S(1)} %collective-permute-done.16.refs_11_), channel_id=1, source_target_pairs={{0,28},{4,0},{8,4},{12,8},{16,12},{20,16},{24,20},{28,24},{1,29},{... | collective-permute-start | bytes 393224 | tf_op jit(solution)/shard_map/ppermute | solution.py:37
  53.2 0.8 %copy.8 = bf16[16,1,64,128]{3,2,1,0:T(8,128)(2,1)} copy(bf16[16,1,64,128]{3,0,2,1:T(8,128)(2,1)S(1)} %maximum_bitcast_fusion) | data formatting | bytes 524288
  53.9 0.0 collective-permute-done.7.refs_0_
  53.9 1.4 %collective-permute-done.15.refs_2_.refs_3_ = bf16[32,16,128]{2,1,0:T(8,128)(2,1)S(1)} collective-permute-done((bf16[32,16,128]{2,1,0:T(8,128)(2,1)S(1)}, bf16[32,16,128]{2,1,0:T(8,128)(2,1)S(1)}, u32[]{:S(2)}, u32[]{:S(2)}) %collective-permute-start.15) | collective-permute-done | bytes 131104 | tf_op jit(solution)/shard_map/ppermute | solution.py:37
  55.4 0.9 %lower_grad.1.refs_14_ = bf16[8,2,48,256]{3,2,1,0:T(8,128)(2,1)S(1)} custom-call(bf16[64,16,128]{2,1,0:T(8,128)(2,1)S(1)} %collective-permute-done.7.refs_0_, bf16[64,16,128]{2,1,0:T(8,128)(2,1)S(1)} %collective-permute-done.10.refs_1_, bf16[32,16,128]{2,1,0:T(8,128)(2,1)S(1)} %collective-permute-done.15.refs_2_.refs_3_, ...), custom_call_target="tpu_custom_call" | custom-call | flops 150994944 | bytes 1048576 | tf_op jit(solution)/shard_map/lower_grad/pallas_call | solution.py:258
  56.3 1.5 %collective-permute-done.17.refs_4_ = bf16[32,16,128]{2,1,0:T(8,128)(2,1)S(1)} collective-permute-done((bf16[32,16,128]{2,1,0:T(8,128)(2,1)S(1)}, bf16[32,16,128]{2,1,0:T(8,128)(2,1)S(1)}, u32[]{:S(2)}, u32[]{:S(2)}) %collective-permute-start.17) | collective-permute-done | bytes 131104 | tf_op jit(solution)/shard_map/ppermute | solution.py:37
  57.8 0.0 collective-permute-done.13.refs_2_
  57.8 2.1 %upper_grad.1 = bf16[8,2,128,256]{3,2,1,0:T(8,128)(2,1)} custom-call(bf16[64,16,128]{2,1,0:T(8,128)(2,1)S(1)} %collective-permute-done.7.refs_0_, bf16[64,16,128]{2,1,0:T(8,128)(2,1)S(1)} %collective-permute-done.10.refs_1_, bf16[64,16,128]{2,1,0:T(8,128)(2,1)S(1)} %collective-permute-done.13.refs_2_, ...), custom_call_target="tpu_custom_call" | custom-call | flops 251658240 | bytes 1048576 | tf_op jit(solution)/shard_map/upper_grad/pallas_call | solution.py:258
  (15 shorter events, 0.2 us)
Async XLA Ops:
  0.6 3.9 %copy-start = (bf16[64,32,3,3,3]{0,1,4,3,2:T(8,128)(2,1)S(1)}, bf16[64,32,3,3,3]{0,1,4,3,2:T(8,128)(2,1)}, u32[]{:S(2)}) copy-start(bf16[64,32,3,3,3]{0,1,4,3,2:T(8,128)(2,1)} %param.5) | copy-start | bytes 331780
  0.6 4.1 %copy-start.1 = (bf16[8,2,128,256]{3,2,1,0:T(8,128)(2,1)S(1)}, bf16[8,2,128,256]{3,2,1,0:T(8,128)(2,1)}, u32[]{:S(2)}) copy-start(bf16[8,2,128,256]{3,2,1,0:T(8,128)(2,1)} %field_ref.1) | copy-start | bytes 3145732
  1.8 8.8 %collective-permute-start = (bf16[8,128,256]{2,1,0:T(8,128)(2,1)S(1)}, bf16[8,128,256]{2,1,0:T(8,128)(2,1)S(1)}, u32[]{:S(2)}, u32[]{:S(2)}) collective-permute-start(bf16[8,128,256]{2,1,0:T(8,128)(2,1)S(1)} %slice_bitcast_fusion), channel_id=1, source_target_pairs={{0,4},{4,8},{8,12},{12,16},{16,20},{20,24},{24,28},{28,0},{1,5},{5... | collective-permute-start | bytes 1572872 | tf_op jit(solution)/shard_map/ppermute | solution.py:37
  6.3 7.7 %copy-start.2 = (bf16[16,1,64,128]{3,2,1,0:T(8,128)(2,1)S(1)}, bf16[16,1,64,128]{3,2,1,0:T(8,128)(2,1)}, u32[]{:S(2)}) copy-start(bf16[16,1,64,128]{3,2,1,0:T(8,128)(2,1)} %param.7) | copy-start | bytes 786436
  10.6 18.2 %copy-start.3 = (f32[16]{0:T(128)S(1)}, f32[16]{0:T(128)}, u32[]{:S(2)}) copy-start(f32[16]{0:T(128)} %param.6) | copy-start | bytes 196
  11.6 4.3 %collective-permute-start.2 = (bf16[32,16,128]{2,1,0:T(8,128)(2,1)S(1)}, bf16[32,16,128]{2,1,0:T(8,128)(2,1)S(1)}, u32[]{:S(2)}, u32[]{:S(2)}) collective-permute-start(bf16[32,16,128]{2,1,0:T(8,128)(2,1)S(1)} %get-tuple-element.33), channel_id=1, source_target_pairs={{0,2},{2,3},{3,1},{1,0},{4,6},{6,7},{7,5},{5,4},{8,10},{10,11},{11... | collective-permute-start | bytes 393224 | tf_op jit(solution)/shard_map/ppermute | solution.py:37
  14.0 4.9 %collective-permute-start.5 = (bf16[32,16,128]{2,1,0:T(8,128)(2,1)S(1)}, bf16[32,16,128]{2,1,0:T(8,128)(2,1)S(1)}, u32[]{:S(2)}, u32[]{:S(2)}) collective-permute-start(bf16[32,16,128]{2,1,0:T(8,128)(2,1)S(1)} %get-tuple-element.41), channel_id=1, source_target_pairs={{0,1},{2,0},{3,2},{1,3},{4,5},{6,4},{7,6},{5,7},{8,9},{10,8},{11,1... | collective-permute-start | bytes 393224 | tf_op jit(solution)/shard_map/ppermute | solution.py:37
  14.2 9.1 %collective-permute-start.1 = (bf16[32,16,128]{2,1,0:T(8,128)(2,1)S(1)}, bf16[32,16,128]{2,1,0:T(8,128)(2,1)S(1)}, u32[]{:S(2)}, u32[]{:S(2)}) collective-permute-start(bf16[32,16,128]{2,1,0:T(8,128)(2,1)S(1)} %get-tuple-element.31), channel_id=1, source_target_pairs={{0,1},{2,0},{3,2},{1,3},{4,5},{6,4},{7,6},{5,7},{8,9},{10,8},{11,1... | collective-permute-start | bytes 393224 | tf_op jit(solution)/shard_map/ppermute | solution.py:37
  15.9 16.1 %collective-permute-start.4 = (bf16[32,16,128]{2,1,0:T(8,128)(2,1)S(1)}, bf16[32,16,128]{2,1,0:T(8,128)(2,1)S(1)}, u32[]{:S(2)}, u32[]{:S(2)}) collective-permute-start(bf16[32,16,128]{2,1,0:T(8,128)(2,1)S(1)} %get-tuple-element.40), channel_id=1, source_target_pairs={{0,2},{2,3},{3,1},{1,0},{4,6},{6,7},{7,5},{5,4},{8,10},{10,11},{11... | collective-permute-start | bytes 393224 | tf_op jit(solution)/shard_map/ppermute | solution.py:37
  18.9 13.1 %collective-permute-start.6 = (bf16[32,16,128]{2,1,0:T(8,128)(2,1)S(1)}, bf16[32,16,128]{2,1,0:T(8,128)(2,1)S(1)}, u32[]{:S(2)}, u32[]{:S(2)}) collective-permute-start(bf16[32,16,128]{2,1,0:T(8,128)(2,1)S(1)} %add.7), channel_id=1, source_target_pairs={{0,1},{2,0},{3,2},{1,3},{4,5},{6,4},{7,6},{5,7},{8,9},{10,8},{11,1... | collective-permute-start | bytes 393224 | tf_op jit(solution)/shard_map/ppermute | solution.py:37
  19.6 9.2 %collective-permute-start.3 = (bf16[32,16,128]{2,1,0:T(8,128)(2,1)S(1)}, bf16[32,16,128]{2,1,0:T(8,128)(2,1)S(1)}, u32[]{:S(2)}, u32[]{:S(2)}) collective-permute-start(bf16[32,16,128]{2,1,0:T(8,128)(2,1)S(1)} %add.6), channel_id=1, source_target_pairs={{0,2},{2,3},{3,1},{1,0},{4,6},{6,7},{7,5},{5,4},{8,10},{10,11},{11... | collective-permute-start | bytes 393224 | tf_op jit(solution)/shard_map/ppermute | solution.py:37
  29.1 9.7 %collective-permute-start.8 = (bf16[32,16,128]{2,1,0:T(8,128)(2,1)S(1)}, bf16[32,16,128]{2,1,0:T(8,128)(2,1)S(1)}, u32[]{:S(2)}, u32[]{:S(2)}) collective-permute-start(bf16[32,16,128]{2,1,0:T(8,128)(2,1)S(1)} %get-tuple-element.51.refs_3_.refs_5_), channel_id=1, source_target_pairs={{0,2},{2,3},{3,1},{1,0},{4,6},{6,7},{7,5},{5,4},{8,10},{10,11},{11... | collective-permute-start | bytes 393224 | tf_op jit(solution)/shard_map/ppermute | solution.py:37
  32.0 6.9 %collective-permute-start.9 = (bf16[32,16,128]{2,1,0:T(8,128)(2,1)S(1)}, bf16[32,16,128]{2,1,0:T(8,128)(2,1)S(1)}, u32[]{:S(2)}, u32[]{:S(2)}) collective-permute-start(bf16[32,16,128]{2,1,0:T(8,128)(2,1)S(1)} %get-tuple-element.51.refs_3_.refs_5_), channel_id=1, source_target_pairs={{0,1},{2,0},{3,2},{1,3},{4,5},{6,4},{7,6},{5,7},{8,9},{10,8},{11,1... | collective-permute-start | bytes 393224 | tf_op jit(solution)/shard_map/ppermute | solution.py:37
  32.2 12.4 %collective-permute-start.11 = (bf16[32,16,128]{2,1,0:T(8,128)(2,1)S(1)}, bf16[32,16,128]{2,1,0:T(8,128)(2,1)S(1)}, u32[]{:S(2)}, u32[]{:S(2)}) collective-permute-start(bf16[32,16,128]{2,1,0:T(8,128)(2,1)S(1)} %get-tuple-element.52.refs_9_), channel_id=1, source_target_pairs={{0,2},{2,3},{3,1},{1,0},{4,6},{6,7},{7,5},{5,4},{8,10},{10,11},{11... | collective-permute-start | bytes 393224 | tf_op jit(solution)/shard_map/ppermute | solution.py:37
  34.7 10.0 %collective-permute-start.12 = (bf16[32,16,128]{2,1,0:T(8,128)(2,1)S(1)}, bf16[32,16,128]{2,1,0:T(8,128)(2,1)S(1)}, u32[]{:S(2)}, u32[]{:S(2)}) collective-permute-start(bf16[32,16,128]{2,1,0:T(8,128)(2,1)S(1)} %get-tuple-element.52.refs_9_), channel_id=1, source_target_pairs={{0,1},{2,0},{3,2},{1,3},{4,5},{6,4},{7,6},{5,7},{8,9},{10,8},{11,1... | collective-permute-start | bytes 393224 | tf_op jit(solution)/shard_map/ppermute | solution.py:37
  34.7 19.3 %collective-permute-start.7 = (bf16[64,16,128]{2,1,0:T(8,128)(2,1)S(1)}, bf16[64,16,128]{2,1,0:T(8,128)(2,1)S(1)}, u32[]{:S(2)}, u32[]{:S(2)}) collective-permute-start(bf16[64,16,128]{2,1,0:T(8,128)(2,1)S(1)} %pad_maximum_fusion), channel_id=1, source_target_pairs={{0,28},{4,0},{8,4},{12,8},{16,12},{20,16},{24,20},{28,24},{1,29},{... | collective-permute-start | bytes 786440 | tf_op jit(solution)/shard_map/ppermute | solution.py:37
  38.8 9.4 %collective-permute-start.14 = (bf16[32,16,128]{2,1,0:T(8,128)(2,1)S(1)}, bf16[32,16,128]{2,1,0:T(8,128)(2,1)S(1)}, u32[]{:S(2)}, u32[]{:S(2)}) collective-permute-start(bf16[32,16,128]{2,1,0:T(8,128)(2,1)S(1)} %collective-permute-done.8.refs_4_.refs_6_), channel_id=1, source_target_pairs={{0,2},{2,3},{3,1},{1,0},{4,6},{6,7},{7,5},{5,4},{8,10},{10,11},{11... | collective-permute-start | bytes 393224 | tf_op jit(solution)/shard_map/ppermute | solution.py:37
  41.5 13.9 %collective-permute-start.10 = (bf16[64,16,128]{2,1,0:T(8,128)(2,1)S(1)}, bf16[64,16,128]{2,1,0:T(8,128)(2,1)S(1)}, u32[]{:S(2)}, u32[]{:S(2)}) collective-permute-start(bf16[64,16,128]{2,1,0:T(8,128)(2,1)S(1)} %pad_maximum_fusion.1), channel_id=1, source_target_pairs={{0,28},{4,0},{8,4},{12,8},{16,12},{20,16},{24,20},{28,24},{1,29},{... | collective-permute-start | bytes 786440 | tf_op jit(solution)/shard_map/ppermute | solution.py:37
  44.7 6.3 %collective-permute-start.16 = (bf16[32,16,128]{2,1,0:T(8,128)(2,1)S(1)}, bf16[32,16,128]{2,1,0:T(8,128)(2,1)S(1)}, u32[]{:S(2)}, u32[]{:S(2)}) collective-permute-start(bf16[32,16,128]{2,1,0:T(8,128)(2,1)S(1)} %collective-permute-done.12.refs_12_), channel_id=1, source_target_pairs={{0,1},{2,0},{3,2},{1,3},{4,5},{6,4},{7,6},{5,7},{8,9},{10,8},{11,1... | collective-permute-start | bytes 393224 | tf_op jit(solution)/shard_map/ppermute | solution.py:37
  46.4 11.4 %collective-permute-start.13 = (bf16[64,16,128]{2,1,0:T(8,128)(2,1)S(1)}, bf16[64,16,128]{2,1,0:T(8,128)(2,1)S(1)}, u32[]{:S(2)}, u32[]{:S(2)}) collective-permute-start(bf16[64,16,128]{2,1,0:T(8,128)(2,1)S(1)} %pad_maximum_fusion.2), channel_id=1, source_target_pairs={{0,28},{4,0},{8,4},{12,8},{16,12},{20,16},{24,20},{28,24},{1,29},{... | collective-permute-start | bytes 786440 | tf_op jit(solution)/shard_map/ppermute | solution.py:37
  48.2 7.2 %collective-permute-start.15 = (bf16[32,16,128]{2,1,0:T(8,128)(2,1)S(1)}, bf16[32,16,128]{2,1,0:T(8,128)(2,1)S(1)}, u32[]{:S(2)}, u32[]{:S(2)}) collective-permute-start(bf16[32,16,128]{2,1,0:T(8,128)(2,1)S(1)} %collective-permute-done.14.refs_5_.refs_7_), channel_id=1, source_target_pairs={{0,28},{4,0},{8,4},{12,8},{16,12},{20,16},{24,20},{28,24},{1,29},{... | collective-permute-start | bytes 393224 | tf_op jit(solution)/shard_map/ppermute | solution.py:37
  50.9 6.8 %collective-permute-start.17 = (bf16[32,16,128]{2,1,0:T(8,128)(2,1)S(1)}, bf16[32,16,128]{2,1,0:T(8,128)(2,1)S(1)}, u32[]{:S(2)}, u32[]{:S(2)}) collective-permute-start(bf16[32,16,128]{2,1,0:T(8,128)(2,1)S(1)} %collective-permute-done.16.refs_11_), channel_id=1, source_target_pairs={{0,28},{4,0},{8,4},{12,8},{16,12},{20,16},{24,20},{28,24},{1,29},{... | collective-permute-start | bytes 393224 | tf_op jit(solution)/shard_map/ppermute | solution.py:37

commit v4 on v3

--- a/solution.py
+++ b/solution.py
@@ -14,7 +14,7 @@
 PARAMS = pltpu.CompilerParams(vmem_limit_bytes=24 * 1024 * 1024)
 
 
-OPT = dict(rs_relay=(1, 1), ag_relay=(1, 1), ag_tie=1, gx_merge=1, delay=1, lower=32, fold=1, tie_own=0, rs_tie=2, tie_act=1)
+OPT = dict(rs_relay=(1, 1), ag_relay=(1, 1), ag_tie=2, gx_merge=1, delay=1, lower=32, fold=1, tie_own=0, rs_tie=2, tie_k2=1, tie_act=0)
 
 
 def ring_device(place, count):
@@ -100,26 +100,36 @@
         acc_ref[:, lane : lane + width] = tap_sums(weights, taps_ref, lane, width, half_z)
 
 
-def halo_kernel(counts, halo_ref, weight_ref, acc_ref, *refs):
-    *part_refs, taps_ref = refs
-    chans, span_y, span_z = halo_ref.shape
-    half_z = span_z // 2
-    blocks = [(rows_of(halo_ref, (), b), 0, 8, 1 + 8 * b) for b in range(span_y // ROWS)]
+def halo_kernel(part, *refs):
+    halo_refs, (weight_ref, acc_ref), part_refs, taps_ref = (
+        refs[: part + 1],
+        refs[part + 1 : part + 3],
+        refs[part + 3 : -1],
+        refs[-1],
+    )
+    chans, _, span_z = halo_refs[0].shape
+    half_z = span_z // 2
+    lower = halo_refs[0].shape[1] // ROWS - 1
+    if part == 0:
+        blocks = [(rows_of(halo_refs[0], (), 0), 7, 1, 0)]
+        blocks += [(rows_of(halo_refs[0], (), 1 + b), 0, 8, 1 + 8 * b) for b in range(lower)]
+    else:
+        upper = halo_refs[1].shape[1] // ROWS
+        blocks = [(rows_of(halo_refs[0], (), lower), 7, 1, 0)]
+        blocks += [(rows_of(halo_refs[1], (), b), 0, 8, 1 + 8 * b) for b in range(upper)]
+        blocks += [(rows_of(halo_refs[0], (), 0), 0, 8, 1 + 8 * upper)]
     fill_taps(blocks, chans, span_z, taps_ref, 0)
-    taps_ref[:, :half_z] = taps_ref[:, span_y // 2 * half_z :]
     weights = weight_ref[...]
-    peers = len(part_refs) // len(counts)
-    rows = part_refs[0].shape[1]
+    count, rows, _ = part_refs[0].shape
     width = 8 * half_z
-    for step in range(span_y // 16):
+    base = part * (acc_ref.shape[1] - count * half_z)
+    for step in range(count // 8):
         lane = step * width
-        sums = acc_ref[:, lane : lane + width]
+        sums = acc_ref[:, base + lane : base + lane + width]
         sums = (sums + tap_sums(weights, taps_ref, lane, width, half_z)).astype(BF16)
-        part = int(step * 8 >= counts[0])
-        first = step * 8 - part * counts[0]
         for j in range(8):
-            for peer in range(peers):
-                part_refs[part * peers + peer][first + j] = sums[
+            for peer, ref in enumerate(part_refs):
+                ref[step * 8 + j] = sums[
                     peer * rows : (peer + 1) * rows, j * half_z : (j + 1) * half_z
                 ]
 
@@ -277,7 +287,10 @@
     counts = (OPT["lower"], half_y - OPT["lower"])
     starts = (0, counts[0])
     mid = 2 * counts[0]
-    halo = shifted(field[:, planes - 1], "gx", 1)
+    last = span_y - ROWS
+    plane = lax.optimization_barrier(field[:, planes - 1])
+    halos = [jnp.concatenate([plane[:, last:], plane[:, :mid]], axis=1), plane[:, mid:last]]
+    halos = [shifted(halo, "gx", 1) for halo in halos]
 
     chans = -(-cin // 8) * 8
     rows = -(-cout // ROWS) * ROWS
@@ -315,20 +328,23 @@
         flops=2 * total * 24 * chans * points,
         bytes_accessed=1 << 22,
     )
-    halo = jnp.pad(halo, (fill_c, (0, 0), (0, 0)))
+    halos = [jnp.pad(halo, (fill_c, (0, 0), (0, 0))) for halo in halos]
     shapes = [jax.ShapeDtypeStruct((count, rows, half_z), BF16) for count in counts]
-    sums = call(
-        functools.partial(halo_kernel, counts),
-        "halo_plane",
-        [shapes[part] for part in range(2) for _ in range(peers)],
-        (halo, weights_halo, acc),
-        [
-            pltpu.VMEM((6 * chans, (1 + half_y) * half_z), BF16),
-        ],
-        flops=2 * total * 12 * chans * points,
-        bytes_accessed=1 << 22,
-    )
-    parts = (sums[:peers], sums[peers:])
+    parts = []
+    for part in range(2):
+        if part and OPT["tie_k2"]:
+            weights_halo, parts[0] = lax.optimization_barrier((weights_halo, parts[0]))
+        parts.append(
+            call(
+                functools.partial(halo_kernel, part),
+                "halo_plane",
+                [shapes[part]] * peers,
+                (*halos[: part + 1], weights_halo, acc),
+                [pltpu.VMEM((6 * chans, (1 + counts[part]) * half_z), BF16)],
+                flops=total * 12 * chans * points,
+                bytes_accessed=1 << 21,
+            )
+        )
 
     far = 2 * quarter
     steps = (quarter, peers - quarter)
@@ -388,7 +404,7 @@
         for h in range(2):
             above[h][0] = (spec(shifted(masked[h], "gx", -1)), 0)
     for h in range(2):
-        if OPT["ag_tie"]:
+        if OPT["ag_tie"] == 1 or (OPT["ag_tie"] and h == 0):
             gathered[h] = lax.optimization_barrier(gathered[h])
         if h == 1 and OPT["tie_own"]:
             gathered[1][steps[1]], whole = lax.optimization_barrier((gathered[1][steps[1]], arrays[0]))
@@ -405,6 +421,12 @@
     for h in range(2):
         if OPT["ag_relay"][h]:
             gathered[h][far] = shifted(gathered[h][steps[h]], "col", steps[h])
+        if OPT["ag_tie"] == 3 and h == 0:
+            both = (gathered[0][far], gathered[1][steps[0]])
+            gathered[0][far], gathered[1][steps[0]] = lax.optimization_barrier(both)
+        if OPT["ag_tie"] == 4 and h == 0:
+            both = (gathered[0][far], gathered[1][steps[0]], gathered[1][steps[1]])
+            gathered[0][far], gathered[1][steps[0]], gathered[1][steps[1]] = lax.optimization_barrier(both)
         above[h][far] = (spec(shifted(gathered[h][far], "gx", -1)), 0)
     mine = [{r: (spec(gathered[h][r]), 0) for r in range(peers)} for h in range(2)]
     order = [[places[h][r] for h in range(2)] for places in (mine, above) for r in range(peers)]

time: 60 us -> 57.3 us (0.955)
  starting transfers between devices: 35.5 us -> 32.1 us
    ppermute x18 -> x19, starting transfers between devices: 35.5 us -> 32.1 us  [shifted(): lax.ppermute(block, axis, [(ring[i], ring[(i + distance) % count]) for i...]
    pallas_call x8 -> x9, Pallas kernels: 6.01 us -> 6.33 us  [call(): pl.pallas_call(kernel, out_shape=out_shape, scratch_shapes=list(scratch),...]
    ppermute x18 -> x19, waiting for transfers between devices: 15.1 us -> 15.3 us  [shifted(): lax.ppermute(block, axis, [(ring[i], ring[(i + distance) % count]) for i...]
  transfers between devices with their start and end apart: 18 -> 19, of which waited for: 7 -> 7; matrix products, arithmetic and copies ran while one was open for 2% -> 2% of each run, Pallas kernels for 5% -> 8%
where the time goes in v4:
time: 57.3 us; the launch traced here: 57.2 us
  starting transfers between devices  32.1 us (56%)
  waiting for transfers between devices  15.3 us (27%)
  Pallas kernels  6.56 us (11%)
  local copies, waits for them, and re-layouts  2.3 us (4%)
  between operations  0.79 us (1%)
    ppermute x19, starting transfers between devices, shifted(): lax.ppermute(block, axis, [(ring[i], ring[(i + distance) % count]) for i...  32.1 us
    ppermute x19, waiting for transfers between devices, shifted(): lax.ppermute(block, axis, [(ring[i], ring[(i + distance) % count]) for i...  15.3 us
    pallas_call x9, Pallas kernels, call(): pl.pallas_call(kernel, out_shape=out_shape, scratch_shapes=list(scratch),...  6.33 us
    squeeze x1, local copies, waits for them, and re-layouts, on_device(): plane = lax.optimization_barrier(field[:, planes - 1])  1.18 us
  transfers between devices with their start and end apart: 19, of which 7 were waited for; matrix products, arithmetic and copies ran while one was open for 2% of the time, Pallas kernels for 8%

profile of v4, /device:TPU:1, one launch (start us, length us, event | category | flops | bytes accessed | tf_op | source)
XLA Modules:
  0.0 57.2 jit_solution(18065675214418500660)
XLA Ops:
  0.6 0.0 copy-start
  0.7 1.2 %slice_bitcast_fusion = bf16[8,128,256]{2,1,0:T(8,128)(2,1)S(1)} fusion(bf16[8,2,128,256]{3,2,1,0:T(8,128)(2,1)} %field_ref.1), kind=kLoop, calls=%fused_computation | loop fusion | bytes 1048576 | tf_op jit(solution)/shard_map/squeeze | solution.py:291
  1.9 2.7 %collective-permute-start = (bf16[8,80,256]{2,1,0:T(8,128)(2,1)S(1)}, bf16[8,80,256]{2,1,0:T(8,128)(2,1)S(1)}, u32[]{:S(2)}, u32[]{:S(2)}) collective-permute-start(bf16[8,80,256]{2,1,0:T(8,128)(2,1)S(1)} %pad_maximum_fusion), channel_id=1, source_target_pairs={{0,4},{4,8},{8,12},{12,16},{16,20},{20,24},{24,28},{28,0},{1,5},{5... | collective-permute-start | bytes 983048 | tf_op jit(solution)/shard_map/ppermute | solution.py:37
  4.6 0.1 collective-permute-start.2
  4.7 0.2 weights.1
  4.9 1.5 %local_planes.1.refs_2_.refs_3_ = f32[64,8192]{1,0:T(8,128)S(1)} custom-call(bf16[8,2,128,256]{3,2,1,0:T(8,128)(2,1)S(1)} %copy-done.1, bf16[64,192]{1,0:T(8,128)(2,1)S(1)} %get-tuple-element.28.weight_ref), custom_call_target="tpu_custom_call" | custom-call | flops 201326592 | bytes 4194304 | tf_op jit(solution)/shard_map/local_planes/pallas_call | solution.py:268
  6.5 2.1 %collective-permute-done.refs_0_ = bf16[8,80,256]{2,1,0:T(8,128)(2,1)S(1)} collective-permute-done((bf16[8,80,256]{2,1,0:T(8,128)(2,1)S(1)}, bf16[8,80,256]{2,1,0:T(8,128)(2,1)S(1)}, u32[]{:S(2)}, u32[]{:S(2)}) %collective-permute-start) | collective-permute-done | bytes 327712 | tf_op jit(solution)/shard_map/ppermute | solution.py:37
  8.6 0.6 %halo_plane.2 = (bf16[32,16,128]{2,1,0:T(8,128)(2,1)S(1)}, bf16[32,16,128]{2,1,0:T(8,128)(2,1)S(1)}, bf16[32,16,128]{2,1,0:T(8,128)(2,1)S(1)}, bf16[32,16,128]{2,1,0:T(8,128)(2,1)S(1)}) custom-call(bf16[8,80,256]{2,1,0:T(8,128)(2,1)S(1)} %collective-permute-done.refs_0_, bf16[64,96]{1,0:T(8,128)(2,1)S(1)} %get-tuple-element.35.refs_1_.refs_2_, ...), custom_call_target="tpu_custom_call" | custom-call | flops 50331648 | bytes 2097152 | tf_op jit(solution)/shard_map/halo_plane/pallas_call | solution.py:268
  9.2 0.0 copy-start.3
  9.3 2.4 %collective-permute-start.3 = (bf16[32,16,128]{2,1,0:T(8,128)(2,1)S(1)}, bf16[32,16,128]{2,1,0:T(8,128)(2,1)S(1)}, u32[]{:S(2)}, u32[]{:S(2)}) collective-permute-start(bf16[32,16,128]{2,1,0:T(8,128)(2,1)S(1)} %get-tuple-element.37), channel_id=1, source_target_pairs={{0,2},{2,3},{3,1},{1,0},{4,6},{6,7},{7,5},{5,4},{8,10},{10,11},{11... | collective-permute-start | bytes 393224 | tf_op jit(solution)/shard_map/ppermute | solution.py:37
  11.6 0.0 collective-permute-done.2.refs_1_
  11.6 0.6 %halo_plane.3 = (bf16[32,16,128]{2,1,0:T(8,128)(2,1)S(1)}, bf16[32,16,128]{2,1,0:T(8,128)(2,1)S(1)}, bf16[32,16,128]{2,1,0:T(8,128)(2,1)S(1)}, bf16[32,16,128]{2,1,0:T(8,128)(2,1)S(1)}) custom-call(bf16[8,80,256]{2,1,0:T(8,128)(2,1)S(1)} %collective-permute-done.refs_0_, bf16[8,48,256]{2,1,0:T(8,128)(2,1)S(1)} %collective-permute-done.2.refs_1_, ...), custom_call_target="tpu_custom_call" | custom-call | flops 50331648 | bytes 2097152 | tf_op jit(solution)/shard_map/halo_plane/pallas_call | solution.py:268
  12.3 0.4 collective-permute-start.6
  12.7 0.2 copy.11
  12.9 2.4 %collective-permute-start.1 = (bf16[32,16,128]{2,1,0:T(8,128)(2,1)S(1)}, bf16[32,16,128]{2,1,0:T(8,128)(2,1)S(1)}, u32[]{:S(2)}, u32[]{:S(2)}) collective-permute-start(bf16[32,16,128]{2,1,0:T(8,128)(2,1)S(1)} %get-tuple-element.34), channel_id=1, source_target_pairs={{0,1},{2,0},{3,2},{1,3},{4,5},{6,4},{7,6},{5,7},{8,9},{10,8},{11,1... | collective-permute-start | bytes 393224 | tf_op jit(solution)/shard_map/ppermute | solution.py:37
  15.2 0.0 collective-permute-done.3.one_ref
  15.2 1.1 %collective-permute-start.5 = (bf16[32,16,128]{2,1,0:T(8,128)(2,1)S(1)}, bf16[32,16,128]{2,1,0:T(8,128)(2,1)S(1)}, u32[]{:S(2)}, u32[]{:S(2)}) collective-permute-start(bf16[32,16,128]{2,1,0:T(8,128)(2,1)S(1)} %get-tuple-element.42), channel_id=1, source_target_pairs={{0,2},{2,3},{3,1},{1,0},{4,6},{6,7},{7,5},{5,4},{8,10},{10,11},{11... | collective-permute-start | bytes 393224 | tf_op jit(solution)/shard_map/ppermute | solution.py:37
  16.3 1.4 %collective-permute-done.6.one_ref = bf16[32,16,128]{2,1,0:T(8,128)(2,1)S(1)} collective-permute-done((bf16[32,16,128]{2,1,0:T(8,128)(2,1)S(1)}, bf16[32,16,128]{2,1,0:T(8,128)(2,1)S(1)}, u32[]{:S(2)}, u32[]{:S(2)}) %collective-permute-start.6) | collective-permute-done | bytes 131104 | tf_op jit(solution)/shard_map/ppermute | solution.py:37
  17.8 0.6 %collective-permute-start.7 = (bf16[32,16,128]{2,1,0:T(8,128)(2,1)S(1)}, bf16[32,16,128]{2,1,0:T(8,128)(2,1)S(1)}, u32[]{:S(2)}, u32[]{:S(2)}) collective-permute-start(bf16[32,16,128]{2,1,0:T(8,128)(2,1)S(1)} %add.7), channel_id=1, source_target_pairs={{0,1},{2,0},{3,2},{1,3},{4,5},{6,4},{7,6},{5,7},{8,9},{10,8},{11,1... | collective-permute-start | bytes 393224 | tf_op jit(solution)/shard_map/ppermute | solution.py:37
  18.5 1.8 %collective-permute-start.4 = (bf16[32,16,128]{2,1,0:T(8,128)(2,1)S(1)}, bf16[32,16,128]{2,1,0:T(8,128)(2,1)S(1)}, u32[]{:S(2)}, u32[]{:S(2)}) collective-permute-start(bf16[32,16,128]{2,1,0:T(8,128)(2,1)S(1)} %add.6), channel_id=1, source_target_pairs={{0,2},{2,3},{3,1},{1,0},{4,6},{6,7},{7,5},{5,4},{8,10},{10,11},{11... | collective-permute-start | bytes 393224 | tf_op jit(solution)/shard_map/ppermute | solution.py:37
  20.3 0.7 %collective-permute-done.1.refs_1_ = bf16[32,16,128]{2,1,0:T(8,128)(2,1)S(1)} collective-permute-done((bf16[32,16,128]{2,1,0:T(8,128)(2,1)S(1)}, bf16[32,16,128]{2,1,0:T(8,128)(2,1)S(1)}, u32[]{:S(2)}, u32[]{:S(2)}) %collective-permute-start.1) | collective-permute-done | bytes 131104 | tf_op jit(solution)/shard_map/ppermute | solution.py:37
  21.1 6.9 %collective-permute-done.4.refs_2_ = bf16[32,16,128]{2,1,0:T(8,128)(2,1)S(1)} collective-permute-done((bf16[32,16,128]{2,1,0:T(8,128)(2,1)S(1)}, bf16[32,16,128]{2,1,0:T(8,128)(2,1)S(1)}, u32[]{:S(2)}, u32[]{:S(2)}) %collective-permute-start.4) | collective-permute-done | bytes 131104 | tf_op jit(solution)/shard_map/ppermute | solution.py:37
  27.9 0.1 broadcast_in_dim.4.refs_3_
  28.0 0.2 activation.2
  28.3 1.5 %collective-permute-start.9 = (bf16[32,16,128]{2,1,0:T(8,128)(2,1)S(1)}, bf16[32,16,128]{2,1,0:T(8,128)(2,1)S(1)}, u32[]{:S(2)}, u32[]{:S(2)}) collective-permute-start(bf16[32,16,128]{2,1,0:T(8,128)(2,1)S(1)} %get-tuple-element.50.refs_3_.refs_5_), channel_id=1, source_target_pairs={{0,2},{2,3},{3,1},{1,0},{4,6},{6,7},{7,5},{5,4},{8,10},{10,11},{11... | collective-permute-start | bytes 393224 | tf_op jit(solution)/shard_map/ppermute | solution.py:37
  29.7 0.0 collective-permute-start.10
  29.8 0.0 collective-permute-done.5.refs_1_
  29.8 0.0 collective-permute-done.7.refs_2_
  29.8 0.2 activation.3
  30.0 2.0 %collective-permute-start.13 = (bf16[32,16,128]{2,1,0:T(8,128)(2,1)S(1)}, bf16[32,16,128]{2,1,0:T(8,128)(2,1)S(1)}, u32[]{:S(2)}, u32[]{:S(2)}) collective-permute-start(bf16[32,16,128]{2,1,0:T(8,128)(2,1)S(1)} %get-tuple-element.47.refs_9_), channel_id=1, source_target_pairs={{0,1},{2,0},{3,2},{1,3},{4,5},{6,4},{7,6},{5,7},{8,9},{10,8},{11,1... | collective-permute-start | bytes 393224 | tf_op jit(solution)/shard_map/ppermute | solution.py:37
  32.0 0.4 collective-permute-start.12
  32.5 4.3 %collective-permute-start.8 = (bf16[64,16,128]{2,1,0:T(8,128)(2,1)S(1)}, bf16[64,16,128]{2,1,0:T(8,128)(2,1)S(1)}, u32[]{:S(2)}, u32[]{:S(2)}) collective-permute-start(bf16[64,16,128]{2,1,0:T(8,128)(2,1)S(1)} %pad_maximum_fusion.1), channel_id=1, source_target_pairs={{0,28},{4,0},{8,4},{12,8},{16,12},{20,16},{24,20},{28,24},{1,29},{... | collective-permute-start | bytes 786440 | tf_op jit(solution)/shard_map/ppermute | solution.py:37
  36.8 0.0 collective-permute-done.9.refs_4_.refs_6_
  36.8 0.0 collective-permute-done.10.refs_6_.refs_8_
  36.8 1.5 %collective-permute-start.15 = (bf16[32,16,128]{2,1,0:T(8,128)(2,1)S(1)}, bf16[32,16,128]{2,1,0:T(8,128)(2,1)S(1)}, u32[]{:S(2)}, u32[]{:S(2)}) collective-permute-start(bf16[32,16,128]{2,1,0:T(8,128)(2,1)S(1)} %collective-permute-done.9.refs_4_.refs_6_), channel_id=1, source_target_pairs={{0,2},{2,3},{3,1},{1,0},{4,6},{6,7},{7,5},{5,4},{8,10},{10,11},{11... | collective-permute-start | bytes 393224 | tf_op jit(solution)/shard_map/ppermute | solution.py:37
  38.4 3.8 %collective-permute-start.11 = (bf16[64,16,128]{2,1,0:T(8,128)(2,1)S(1)}, bf16[64,16,128]{2,1,0:T(8,128)(2,1)S(1)}, u32[]{:S(2)}, u32[]{:S(2)}) collective-permute-start(bf16[64,16,128]{2,1,0:T(8,128)(2,1)S(1)} %pad_maximum_fusion.2), channel_id=1, source_target_pairs={{0,28},{4,0},{8,4},{12,8},{16,12},{20,16},{24,20},{28,24},{1,29},{... | collective-permute-start | bytes 786440 | tf_op jit(solution)/shard_map/ppermute | solution.py:37
  42.2 1.3 %collective-permute-start.17 = (bf16[32,16,128]{2,1,0:T(8,128)(2,1)S(1)}, bf16[32,16,128]{2,1,0:T(8,128)(2,1)S(1)}, u32[]{:S(2)}, u32[]{:S(2)}) collective-permute-start(bf16[32,16,128]{2,1,0:T(8,128)(2,1)S(1)} %collective-permute-done.13.refs_12_), channel_id=1, source_target_pairs={{0,1},{2,0},{3,2},{1,3},{4,5},{6,4},{7,6},{5,7},{8,9},{10,8},{11,1... | collective-permute-start | bytes 393224 | tf_op jit(solution)/shard_map/ppermute | solution.py:37
  43.5 0.0 collective-permute-done.12.refs_10_
  43.5 2.3 %collective-permute-start.14 = (bf16[64,16,128]{2,1,0:T(8,128)(2,1)S(1)}, bf16[64,16,128]{2,1,0:T(8,128)(2,1)S(1)}, u32[]{:S(2)}, u32[]{:S(2)}) collective-permute-start(bf16[64,16,128]{2,1,0:T(8,128)(2,1)S(1)} %pad_maximum_fusion.3), channel_id=1, source_target_pairs={{0,28},{4,0},{8,4},{12,8},{16,12},{20,16},{24,20},{28,24},{1,29},{... | collective-permute-start | bytes 786440 | tf_op jit(solution)/shard_map/ppermute | solution.py:37
  45.8 1.7 %collective-permute-start.16 = (bf16[32,16,128]{2,1,0:T(8,128)(2,1)S(1)}, bf16[32,16,128]{2,1,0:T(8,128)(2,1)S(1)}, u32[]{:S(2)}, u32[]{:S(2)}) collective-permute-start(bf16[32,16,128]{2,1,0:T(8,128)(2,1)S(1)} %collective-permute-done.15.refs_5_.refs_7_), channel_id=1, source_target_pairs={{0,28},{4,0},{8,4},{12,8},{16,12},{20,16},{24,20},{28,24},{1,29},{... | collective-permute-start | bytes 393224 | tf_op jit(solution)/shard_map/ppermute | solution.py:37
  47.5 0.8 %collective-permute-done.17.refs_11_ = bf16[32,16,128]{2,1,0:T(8,128)(2,1)S(1)} collective-permute-done((bf16[32,16,128]{2,1,0:T(8,128)(2,1)S(1)}, bf16[32,16,128]{2,1,0:T(8,128)(2,1)S(1)}, u32[]{:S(2)}, u32[]{:S(2)}) %collective-permute-start.17) | collective-permute-done | bytes 131104 | tf_op jit(solution)/shard_map/ppermute | solution.py:37
  48.2 1.8 %collective-permute-start.18 = (bf16[32,16,128]{2,1,0:T(8,128)(2,1)S(1)}, bf16[32,16,128]{2,1,0:T(8,128)(2,1)S(1)}, u32[]{:S(2)}, u32[]{:S(2)}) collective-permute-start(bf16[32,16,128]{2,1,0:T(8,128)(2,1)S(1)} %collective-permute-done.17.refs_11_), channel_id=1, source_target_pairs={{0,28},{4,0},{8,4},{12,8},{16,12},{20,16},{24,20},{28,24},{1,29},{... | collective-permute-start | bytes 393224 | tf_op jit(solution)/shard_map/ppermute | solution.py:37
  50.1 0.8 %copy.8 = bf16[16,1,64,128]{3,2,1,0:T(8,128)(2,1)} copy(bf16[16,1,64,128]{3,0,2,1:T(8,128)(2,1)S(1)} %maximum_bitcast_fusion) | data formatting | bytes 524288
  50.8 0.0 collective-permute-done.8.refs_0_
  50.8 2.4 %collective-permute-done.16.refs_2_.refs_3_ = bf16[32,16,128]{2,1,0:T(8,128)(2,1)S(1)} collective-permute-done((bf16[32,16,128]{2,1,0:T(8,128)(2,1)S(1)}, bf16[32,16,128]{2,1,0:T(8,128)(2,1)S(1)}, u32[]{:S(2)}, u32[]{:S(2)}) %collective-permute-start.16) | collective-permute-done | bytes 131104 | tf_op jit(solution)/shard_map/ppermute | solution.py:37
  53.2 0.9 %lower_grad.1.refs_14_ = bf16[8,2,48,256]{3,2,1,0:T(8,128)(2,1)S(1)} custom-call(bf16[64,16,128]{2,1,0:T(8,128)(2,1)S(1)} %collective-permute-done.8.refs_0_, bf16[64,16,128]{2,1,0:T(8,128)(2,1)S(1)} %collective-permute-done.11.refs_1_, bf16[32,16,128]{2,1,0:T(8,128)(2,1)S(1)} %collective-permute-done.16.refs_2_.refs_3_, ...), custom_call_target="tpu_custom_call" | custom-call | flops 150994944 | bytes 1048576 | tf_op jit(solution)/shard_map/lower_grad/pallas_call | solution.py:268
  54.1 1.0 %collective-permute-done.18.refs_4_ = bf16[32,16,128]{2,1,0:T(8,128)(2,1)S(1)} collective-permute-done((bf16[32,16,128]{2,1,0:T(8,128)(2,1)S(1)}, bf16[32,16,128]{2,1,0:T(8,128)(2,1)S(1)}, u32[]{:S(2)}, u32[]{:S(2)}) %collective-permute-start.18) | collective-permute-done | bytes 131104 | tf_op jit(solution)/shard_map/ppermute | solution.py:37
  55.1 2.1 %upper_grad.1 = bf16[8,2,128,256]{3,2,1,0:T(8,128)(2,1)} custom-call(bf16[64,16,128]{2,1,0:T(8,128)(2,1)S(1)} %collective-permute-done.8.refs_0_, bf16[64,16,128]{2,1,0:T(8,128)(2,1)S(1)} %collective-permute-done.11.refs_1_, bf16[64,16,128]{2,1,0:T(8,128)(2,1)S(1)} %collective-permute-done.14.refs_2_, ...), custom_call_target="tpu_custom_call" | custom-call | flops 251658240 | bytes 1048576 | tf_op jit(solution)/shard_map/upper_grad/pallas_call | solution.py:268
  (22 shorter events, 0.3 us)
Async XLA Ops:
  0.6 4.0 %copy-start = (bf16[64,32,3,3,3]{0,1,4,3,2:T(8,128)(2,1)S(1)}, bf16[64,32,3,3,3]{0,1,4,3,2:T(8,128)(2,1)}, u32[]{:S(2)}) copy-start(bf16[64,32,3,3,3]{0,1,4,3,2:T(8,128)(2,1)} %param.5) | copy-start | bytes 331780
  0.6 4.3 %copy-start.1 = (bf16[8,2,128,256]{3,2,1,0:T(8,128)(2,1)S(1)}, bf16[8,2,128,256]{3,2,1,0:T(8,128)(2,1)}, u32[]{:S(2)}) copy-start(bf16[8,2,128,256]{3,2,1,0:T(8,128)(2,1)} %field_ref.1) | copy-start | bytes 3145732
  1.9 6.7 %collective-permute-start = (bf16[8,80,256]{2,1,0:T(8,128)(2,1)S(1)}, bf16[8,80,256]{2,1,0:T(8,128)(2,1)S(1)}, u32[]{:S(2)}, u32[]{:S(2)}) collective-permute-start(bf16[8,80,256]{2,1,0:T(8,128)(2,1)S(1)} %pad_maximum_fusion), channel_id=1, source_target_pairs={{0,4},{4,8},{8,12},{12,16},{16,20},{20,24},{24,28},{28,0},{1,5},{5... | collective-permute-start | bytes 983048 | tf_op jit(solution)/shard_map/ppermute | solution.py:37
  4.6 7.0 %collective-permute-start.2 = (bf16[8,48,256]{2,1,0:T(8,128)(2,1)S(1)}, bf16[8,48,256]{2,1,0:T(8,128)(2,1)S(1)}, u32[]{:S(2)}, u32[]{:S(2)}) collective-permute-start(bf16[8,48,256]{2,1,0:T(8,128)(2,1)S(1)} %slice.26), channel_id=1, source_target_pairs={{0,4},{4,8},{8,12},{12,16},{16,20},{20,24},{24,28},{28,0},{1,5},{5... | collective-permute-start | bytes 589832 | tf_op jit(solution)/shard_map/ppermute | solution.py:37
  8.6 4.1 %copy-start.2 = (bf16[16,1,64,128]{3,2,1,0:T(8,128)(2,1)S(1)}, bf16[16,1,64,128]{3,2,1,0:T(8,128)(2,1)}, u32[]{:S(2)}) copy-start(bf16[16,1,64,128]{3,2,1,0:T(8,128)(2,1)} %param.7) | copy-start | bytes 786436
  9.2 18.7 %copy-start.3 = (f32[16]{0:T(128)S(1)}, f32[16]{0:T(128)}, u32[]{:S(2)}) copy-start(f32[16]{0:T(128)} %param.6) | copy-start | bytes 196
  9.3 6.0 %collective-permute-start.3 = (bf16[32,16,128]{2,1,0:T(8,128)(2,1)S(1)}, bf16[32,16,128]{2,1,0:T(8,128)(2,1)S(1)}, u32[]{:S(2)}, u32[]{:S(2)}) collective-permute-start(bf16[32,16,128]{2,1,0:T(8,128)(2,1)S(1)} %get-tuple-element.37), channel_id=1, source_target_pairs={{0,2},{2,3},{3,1},{1,0},{4,6},{6,7},{7,5},{5,4},{8,10},{10,11},{11... | collective-permute-start | bytes 393224 | tf_op jit(solution)/shard_map/ppermute | solution.py:37
  12.3 5.5 %collective-permute-start.6 = (bf16[32,16,128]{2,1,0:T(8,128)(2,1)S(1)}, bf16[32,16,128]{2,1,0:T(8,128)(2,1)S(1)}, u32[]{:S(2)}, u32[]{:S(2)}) collective-permute-start(bf16[32,16,128]{2,1,0:T(8,128)(2,1)S(1)} %get-tuple-element.43), channel_id=1, source_target_pairs={{0,1},{2,0},{3,2},{1,3},{4,5},{6,4},{7,6},{5,7},{8,9},{10,8},{11,1... | collective-permute-start | bytes 393224 | tf_op jit(solution)/shard_map/ppermute | solution.py:37
  12.9 8.2 %collective-permute-start.1 = (bf16[32,16,128]{2,1,0:T(8,128)(2,1)S(1)}, bf16[32,16,128]{2,1,0:T(8,128)(2,1)S(1)}, u32[]{:S(2)}, u32[]{:S(2)}) collective-permute-start(bf16[32,16,128]{2,1,0:T(8,128)(2,1)S(1)} %get-tuple-element.34), channel_id=1, source_target_pairs={{0,1},{2,0},{3,2},{1,3},{4,5},{6,4},{7,6},{5,7},{8,9},{10,8},{11,1... | collective-permute-start | bytes 393224 | tf_op jit(solution)/shard_map/ppermute | solution.py:37
  15.2 14.5 %collective-permute-start.5 = (bf16[32,16,128]{2,1,0:T(8,128)(2,1)S(1)}, bf16[32,16,128]{2,1,0:T(8,128)(2,1)S(1)}, u32[]{:S(2)}, u32[]{:S(2)}) collective-permute-start(bf16[32,16,128]{2,1,0:T(8,128)(2,1)S(1)} %get-tuple-element.42), channel_id=1, source_target_pairs={{0,2},{2,3},{3,1},{1,0},{4,6},{6,7},{7,5},{5,4},{8,10},{10,11},{11... | collective-permute-start | bytes 393224 | tf_op jit(solution)/shard_map/ppermute | solution.py:37
  17.8 12.0 %collective-permute-start.7 = (bf16[32,16,128]{2,1,0:T(8,128)(2,1)S(1)}, bf16[32,16,128]{2,1,0:T(8,128)(2,1)S(1)}, u32[]{:S(2)}, u32[]{:S(2)}) collective-permute-start(bf16[32,16,128]{2,1,0:T(8,128)(2,1)S(1)} %add.7), channel_id=1, source_target_pairs={{0,1},{2,0},{3,2},{1,3},{4,5},{6,4},{7,6},{5,7},{8,9},{10,8},{11,1... | collective-permute-start | bytes 393224 | tf_op jit(solution)/shard_map/ppermute | solution.py:37
  18.5 9.5 %collective-permute-start.4 = (bf16[32,16,128]{2,1,0:T(8,128)(2,1)S(1)}, bf16[32,16,128]{2,1,0:T(8,128)(2,1)S(1)}, u32[]{:S(2)}, u32[]{:S(2)}) collective-permute-start(bf16[32,16,128]{2,1,0:T(8,128)(2,1)S(1)} %add.6), channel_id=1, source_target_pairs={{0,2},{2,3},{3,1},{1,0},{4,6},{6,7},{7,5},{5,4},{8,10},{10,11},{11... | collective-permute-start | bytes 393224 | tf_op jit(solution)/shard_map/ppermute | solution.py:37
  28.3 8.5 %collective-permute-start.9 = (bf16[32,16,128]{2,1,0:T(8,128)(2,1)S(1)}, bf16[32,16,128]{2,1,0:T(8,128)(2,1)S(1)}, u32[]{:S(2)}, u32[]{:S(2)}) collective-permute-start(bf16[32,16,128]{2,1,0:T(8,128)(2,1)S(1)} %get-tuple-element.50.refs_3_.refs_5_), channel_id=1, source_target_pairs={{0,2},{2,3},{3,1},{1,0},{4,6},{6,7},{7,5},{5,4},{8,10},{10,11},{11... | collective-permute-start | bytes 393224 | tf_op jit(solution)/shard_map/ppermute | solution.py:37
  29.7 7.0 %collective-permute-start.10 = (bf16[32,16,128]{2,1,0:T(8,128)(2,1)S(1)}, bf16[32,16,128]{2,1,0:T(8,128)(2,1)S(1)}, u32[]{:S(2)}, u32[]{:S(2)}) collective-permute-start(bf16[32,16,128]{2,1,0:T(8,128)(2,1)S(1)} %get-tuple-element.50.refs_3_.refs_5_), channel_id=1, source_target_pairs={{0,1},{2,0},{3,2},{1,3},{4,5},{6,4},{7,6},{5,7},{8,9},{10,8},{11,1... | collective-permute-start | bytes 393224 | tf_op jit(solution)/shard_map/ppermute | solution.py:37
  30.0 12.2 %collective-permute-start.13 = (bf16[32,16,128]{2,1,0:T(8,128)(2,1)S(1)}, bf16[32,16,128]{2,1,0:T(8,128)(2,1)S(1)}, u32[]{:S(2)}, u32[]{:S(2)}) collective-permute-start(bf16[32,16,128]{2,1,0:T(8,128)(2,1)S(1)} %get-tuple-element.47.refs_9_), channel_id=1, source_target_pairs={{0,1},{2,0},{3,2},{1,3},{4,5},{6,4},{7,6},{5,7},{8,9},{10,8},{11,1... | collective-permute-start | bytes 393224 | tf_op jit(solution)/shard_map/ppermute | solution.py:37
  32.0 11.5 %collective-permute-start.12 = (bf16[32,16,128]{2,1,0:T(8,128)(2,1)S(1)}, bf16[32,16,128]{2,1,0:T(8,128)(2,1)S(1)}, u32[]{:S(2)}, u32[]{:S(2)}) collective-permute-start(bf16[32,16,128]{2,1,0:T(8,128)(2,1)S(1)} %get-tuple-element.47.refs_9_), channel_id=1, source_target_pairs={{0,2},{2,3},{3,1},{1,0},{4,6},{6,7},{7,5},{5,4},{8,10},{10,11},{11... | collective-permute-start | bytes 393224 | tf_op jit(solution)/shard_map/ppermute | solution.py:37
  32.5 18.3 %collective-permute-start.8 = (bf16[64,16,128]{2,1,0:T(8,128)(2,1)S(1)}, bf16[64,16,128]{2,1,0:T(8,128)(2,1)S(1)}, u32[]{:S(2)}, u32[]{:S(2)}) collective-permute-start(bf16[64,16,128]{2,1,0:T(8,128)(2,1)S(1)} %pad_maximum_fusion.1), channel_id=1, source_target_pairs={{0,28},{4,0},{8,4},{12,8},{16,12},{20,16},{24,20},{28,24},{1,29},{... | collective-permute-start | bytes 786440 | tf_op jit(solution)/shard_map/ppermute | solution.py:37
  36.8 9.0 %collective-permute-start.15 = (bf16[32,16,128]{2,1,0:T(8,128)(2,1)S(1)}, bf16[32,16,128]{2,1,0:T(8,128)(2,1)S(1)}, u32[]{:S(2)}, u32[]{:S(2)}) collective-permute-start(bf16[32,16,128]{2,1,0:T(8,128)(2,1)S(1)} %collective-permute-done.9.refs_4_.refs_6_), channel_id=1, source_target_pairs={{0,2},{2,3},{3,1},{1,0},{4,6},{6,7},{7,5},{5,4},{8,10},{10,11},{11... | collective-permute-start | bytes 393224 | tf_op jit(solution)/shard_map/ppermute | solution.py:37
  38.4 14.8 %collective-permute-start.11 = (bf16[64,16,128]{2,1,0:T(8,128)(2,1)S(1)}, bf16[64,16,128]{2,1,0:T(8,128)(2,1)S(1)}, u32[]{:S(2)}, u32[]{:S(2)}) collective-permute-start(bf16[64,16,128]{2,1,0:T(8,128)(2,1)S(1)} %pad_maximum_fusion.2), channel_id=1, source_target_pairs={{0,28},{4,0},{8,4},{12,8},{16,12},{20,16},{24,20},{28,24},{1,29},{... | collective-permute-start | bytes 786440 | tf_op jit(solution)/shard_map/ppermute | solution.py:37
  42.2 6.0 %collective-permute-start.17 = (bf16[32,16,128]{2,1,0:T(8,128)(2,1)S(1)}, bf16[32,16,128]{2,1,0:T(8,128)(2,1)S(1)}, u32[]{:S(2)}, u32[]{:S(2)}) collective-permute-start(bf16[32,16,128]{2,1,0:T(8,128)(2,1)S(1)} %collective-permute-done.13.refs_12_), channel_id=1, source_target_pairs={{0,1},{2,0},{3,2},{1,3},{4,5},{6,4},{7,6},{5,7},{8,9},{10,8},{11,1... | collective-permute-start | bytes 393224 | tf_op jit(solution)/shard_map/ppermute | solution.py:37
  43.5 11.5 %collective-permute-start.14 = (bf16[64,16,128]{2,1,0:T(8,128)(2,1)S(1)}, bf16[64,16,128]{2,1,0:T(8,128)(2,1)S(1)}, u32[]{:S(2)}, u32[]{:S(2)}) collective-permute-start(bf16[64,16,128]{2,1,0:T(8,128)(2,1)S(1)} %pad_maximum_fusion.3), channel_id=1, source_target_pairs={{0,28},{4,0},{8,4},{12,8},{16,12},{20,16},{24,20},{28,24},{1,29},{... | collective-permute-start | bytes 786440 | tf_op jit(solution)/shard_map/ppermute | solution.py:37
  45.8 7.4 %collective-permute-start.16 = (bf16[32,16,128]{2,1,0:T(8,128)(2,1)S(1)}, bf16[32,16,128]{2,1,0:T(8,128)(2,1)S(1)}, u32[]{:S(2)}, u32[]{:S(2)}) collective-permute-start(bf16[32,16,128]{2,1,0:T(8,128)(2,1)S(1)} %collective-permute-done.15.refs_5_.refs_7_), channel_id=1, source_target_pairs={{0,28},{4,0},{8,4},{12,8},{16,12},{20,16},{24,20},{28,24},{1,29},{... | collective-permute-start | bytes 393224 | tf_op jit(solution)/shard_map/ppermute | solution.py:37
  48.2 6.8 %collective-permute-start.18 = (bf16[32,16,128]{2,1,0:T(8,128)(2,1)S(1)}, bf16[32,16,128]{2,1,0:T(8,128)(2,1)S(1)}, u32[]{:S(2)}, u32[]{:S(2)}) collective-permute-start(bf16[32,16,128]{2,1,0:T(8,128)(2,1)S(1)} %collective-permute-done.17.refs_11_), channel_id=1, source_target_pairs={{0,28},{4,0},{8,4},{12,8},{16,12},{20,16},{24,20},{28,24},{1,29},{... | collective-permute-start | bytes 393224 | tf_op jit(solution)/shard_map/ppermute | solution.py:37

commit v5 on v4

--- a/solution.py
+++ b/solution.py
@@ -14,25 +14,18 @@
 PARAMS = pltpu.CompilerParams(vmem_limit_bytes=24 * 1024 * 1024)
 
 
-OPT = dict(rs_relay=(1, 1), ag_relay=(1, 1), ag_tie=2, gx_merge=1, delay=1, lower=32, fold=1, tie_own=0, rs_tie=2, tie_k2=1, tie_act=0)
-
-
 def ring_device(place, count):
-    if not OPT["fold"]:
-        return place
     return jnp.where(2 * place < count, 2 * place, 2 * (count - place) - 1)
 
 
 def ring_place(device, count):
-    if not OPT["fold"]:
-        return device
     return jnp.where(device % 2 == 0, device // 2, count - (device + 1) // 2)
 
 
 def shifted(block, axis, distance):
     count = lax.axis_size(axis)
     ring = list(range(count))
-    if axis == "col" and OPT["fold"]:
+    if axis == "col":
         ring = ring[::2] + ring[1::2][::-1]
     return lax.ppermute(block, axis, [(ring[i], ring[(i + distance) % count]) for i in range(count)])
 
@@ -284,7 +277,7 @@
     cin, planes, span_y, span_z = field.shape
     cout = bias.shape[0]
     half_y, half_z = span_y // 2, span_z // 2
-    counts = (OPT["lower"], half_y - OPT["lower"])
+    counts = (half_y // 2, half_y - half_y // 2)
     starts = (0, counts[0])
     mid = 2 * counts[0]
     last = span_y - ROWS
@@ -332,7 +325,7 @@
     shapes = [jax.ShapeDtypeStruct((count, rows, half_z), BF16) for count in counts]
     parts = []
     for part in range(2):
-        if part and OPT["tie_k2"]:
+        if part:
             weights_halo, parts[0] = lax.optimization_barrier((weights_halo, parts[0]))
         parts.append(
             call(
@@ -349,86 +342,58 @@
     far = 2 * quarter
     steps = (quarter, peers - quarter)
     arrived = [[parts[h][0]] for h in range(2)]
-    relayed = [shifted(parts[h][far], "col", steps[h]) if OPT["rs_relay"][h] else None for h in range(2)]
+    relayed = [shifted(parts[h][far], "col", steps[h]) for h in range(2)]
     for h in range(2):
         for r in range(1, peers):
-            if not OPT["rs_relay"][h] or r not in (steps[h], far):
+            if r not in (steps[h], far):
                 sent = parts[h][r]
-                if h and OPT["rs_tie"] >= 2:
+                if h:
                     sent, relayed[0] = lax.optimization_barrier((sent, relayed[0]))
                 arrived[h].append(shifted(sent, "col", r))
     for h in range(2):
-        if OPT["rs_tie"] == 1 or (OPT["rs_tie"] >= 3 and h == 0):
-            relayed[h], arrived[h] = lax.optimization_barrier((relayed[h], arrived[h]))
-        if OPT["rs_relay"][h]:
-            joined = call(add_kernel, "add", shapes[h], (relayed[h], parts[h][steps[h]]))
-            arrived[h].append(shifted(joined, "col", steps[h]))
+        if h:
+            relayed[1], arrived[0][-1] = lax.optimization_barrier((relayed[1], arrived[0][-1]))
+        joined = call(add_kernel, "add", shapes[h], (relayed[h], parts[h][steps[h]]))
+        arrived[h].append(shifted(joined, "col", steps[h]))
 
     bias_p = jnp.broadcast_to(jnp.pad(bias, fill_o)[None, :, None], (1, rows, half_z))
     cot = jnp.pad(jnp.transpose(cotangent[:, 0], (1, 0, 2)), ((0, 0), fill_o, (0, 0)))
-    acts = []
-    for h in range(2):
-        if h and OPT['tie_act']:
-            bias_p, acts[0] = lax.optimization_barrier((bias_p, acts[0]))
-        acts.append(
-            call(
-                act_kernel,
-                "activation",
-                (shapes[h], shapes[h]),
-                (*arrived[h], bias_p, cot[starts[h] : starts[h] + counts[h]]),
-                transcendentals=3 * counts[h] * rows * half_z,
-            )
+    acts = [
+        call(
+            act_kernel,
+            "activation",
+            (shapes[h], shapes[h]),
+            (*arrived[h], bias_p, cot[starts[h] : starts[h] + counts[h]]),
+            transcendentals=3 * counts[h] * rows * half_z,
         )
+        for h in range(2)
+    ]
     out = jnp.concatenate([out for out, _ in acts], axis=0)
     out_act = jnp.transpose(out[:, :cout], (1, 0, 2))[:, None]
 
     masked = [masked for _, masked in acts]
-    gathered = [{0: masked[h]} for h in range(2)]
-    for h in range(2):
-        for r in range(1, peers):
-            if r != far or not OPT["ag_relay"][h]:
-                gathered[h][r] = shifted(masked[h], "col", r)
+    near = [r for r in range(1, peers) if r != far]
+    gathered = [{0: masked[h], **{r: shifted(masked[h], "col", r) for r in near}} for h in range(2)]
     above = [{}, {}]
     arrays = []
 
-    def spec(value, *at):
+    def place_of(value):
         arrays.append(value)
         return len(arrays) - 1
 
-    if OPT["gx_merge"]:
-        whole = shifted(jnp.concatenate(masked, axis=0), "gx", -1)
-        number = spec(whole)
-        for h in range(2):
-            above[h][0] = (number, starts[h])
-    else:
-        for h in range(2):
-            above[h][0] = (spec(shifted(masked[h], "gx", -1)), 0)
+    whole = place_of(shifted(jnp.concatenate(masked, axis=0), "gx", -1))
     for h in range(2):
-        if OPT["ag_tie"] == 1 or (OPT["ag_tie"] and h == 0):
-            gathered[h] = lax.optimization_barrier(gathered[h])
-        if h == 1 and OPT["tie_own"]:
-            gathered[1][steps[1]], whole = lax.optimization_barrier((gathered[1][steps[1]], arrays[0]))
-            arrays[0] = whole
+        above[h][0] = (whole, starts[h])
+    gathered[0] = lax.optimization_barrier(gathered[0])
     for h in range(2):
-        near = [r for r in range(1, peers) if r != far]
-        if OPT["gx_merge"]:
-            number = spec(shifted(jnp.concatenate([gathered[h][r] for r in near], axis=0), "gx", -1))
-            for i, r in enumerate(near):
-                above[h][r] = (number, i * counts[h])
-        else:
-            for r in near:
-                above[h][r] = (spec(shifted(gathered[h][r], "gx", -1)), 0)
+        joined = jnp.concatenate([gathered[h][r] for r in near], axis=0)
+        number = place_of(shifted(joined, "gx", -1))
+        for i, r in enumerate(near):
+            above[h][r] = (number, i * counts[h])
     for h in range(2):
-        if OPT["ag_relay"][h]:
-            gathered[h][far] = shifted(gathered[h][steps[h]], "col", steps[h])
-        if OPT["ag_tie"] == 3 and h == 0:
-            both = (gathered[0][far], gathered[1][steps[0]])
-            gathered[0][far], gathered[1][steps[0]] = lax.optimization_barrier(both)
-        if OPT["ag_tie"] == 4 and h == 0:
-            both = (gathered[0][far], gathered[1][steps[0]], gathered[1][steps[1]])
-            gathered[0][far], gathered[1][steps[0]], gathered[1][steps[1]] = lax.optimization_barrier(both)
-        above[h][far] = (spec(shifted(gathered[h][far], "gx", -1)), 0)
-    mine = [{r: (spec(gathered[h][r]), 0) for r in range(peers)} for h in range(2)]
+        gathered[h][far] = shifted(gathered[h][steps[h]], "col", steps[h])
+        above[h][far] = (place_of(shifted(gathered[h][far], "gx", -1)), 0)
+    mine = [{r: (place_of(gathered[h][r]), 0) for r in range(peers)} for h in range(2)]
     order = [[places[h][r] for h in range(2)] for places in (mine, above) for r in range(peers)]
 
     def grad_call(kernel, name, shape, used, extra, blocks):

time: 57.3 us -> 57.1 us (level)
  the two profiles are of different devices: /device:TPU:1 before, /device:TPU:11 now
where the time goes in v5:
time: 57.1 us; the launch traced here: 56.9 us
  starting transfers between devices  31 us (54%)
  waiting for transfers between devices  16.1 us (28%)
  Pallas kernels  6.55 us (11%)
  local copies, waits for them, and re-layouts  2.3 us (4%)
  between operations  0.82 us (1%)
    ppermute x19, starting transfers between devices, shifted(): lax.ppermute(block, axis, [(ring[i], ring[(i + distance) % count]) for i...  31 us
    ppermute x19, waiting for transfers between devices, shifted(): lax.ppermute(block, axis, [(ring[i], ring[(i + distance) % count]) for i...  16.1 us
    pallas_call x9, Pallas kernels, call(): pl.pallas_call(kernel, out_shape=out_shape, scratch_shapes=list(scratch),...  6.32 us
    squeeze x1, local copies, waits for them, and re-layouts, on_device(): plane = lax.optimization_barrier(field[:, planes - 1])  1.18 us
  transfers between devices with their start and end apart: 19, of which 9 were waited for; matrix products, arithmetic and copies ran while one was open for 2% of the time, Pallas kernels for 8%

profile of v5, /device:TPU:11, one launch (start us, length us, event | category | flops | bytes accessed | tf_op | source)
XLA Modules:
  0.0 56.9 jit_solution(7259160773767642315)
XLA Ops:
  0.6 0.0 copy-start
  0.7 1.2 %slice_bitcast_fusion = bf16[8,128,256]{2,1,0:T(8,128)(2,1)S(1)} fusion(bf16[8,2,128,256]{3,2,1,0:T(8,128)(2,1)} %field_ref.1), kind=kLoop, calls=%fused_computation | loop fusion | bytes 1048576 | tf_op jit(solution)/shard_map/squeeze | solution.py:284
  1.9 1.8 %collective-permute-start = (bf16[8,80,256]{2,1,0:T(8,128)(2,1)S(1)}, bf16[8,80,256]{2,1,0:T(8,128)(2,1)S(1)}, u32[]{:S(2)}, u32[]{:S(2)}) collective-permute-start(bf16[8,80,256]{2,1,0:T(8,128)(2,1)S(1)} %pad_maximum_fusion), channel_id=1, source_target_pairs={{0,4},{4,8},{8,12},{12,16},{16,20},{20,24},{24,28},{28,0},{1,5},{5... | collective-permute-start | bytes 983048 | tf_op jit(solution)/shard_map/ppermute | solution.py:30
  3.8 0.1 collective-permute-start.2
  3.9 0.2 weights.1
  4.1 1.5 %local_planes.1.refs_2_.refs_3_ = f32[64,8192]{1,0:T(8,128)S(1)} custom-call(bf16[8,2,128,256]{3,2,1,0:T(8,128)(2,1)S(1)} %copy-done.1, bf16[64,192]{1,0:T(8,128)(2,1)S(1)} %get-tuple-element.30.weight_ref), custom_call_target="tpu_custom_call" | custom-call | flops 201326592 | bytes 4194304 | tf_op jit(solution)/shard_map/local_planes/pallas_call | solution.py:261
  5.6 2.1 %collective-permute-done.refs_0_ = bf16[8,80,256]{2,1,0:T(8,128)(2,1)S(1)} collective-permute-done((bf16[8,80,256]{2,1,0:T(8,128)(2,1)S(1)}, bf16[8,80,256]{2,1,0:T(8,128)(2,1)S(1)}, u32[]{:S(2)}, u32[]{:S(2)}) %collective-permute-start) | collective-permute-done | bytes 327712 | tf_op jit(solution)/shard_map/ppermute | solution.py:30
  7.8 0.6 %halo_plane.2 = (bf16[32,16,128]{2,1,0:T(8,128)(2,1)S(1)}, bf16[32,16,128]{2,1,0:T(8,128)(2,1)S(1)}, bf16[32,16,128]{2,1,0:T(8,128)(2,1)S(1)}, bf16[32,16,128]{2,1,0:T(8,128)(2,1)S(1)}) custom-call(bf16[8,80,256]{2,1,0:T(8,128)(2,1)S(1)} %collective-permute-done.refs_0_, bf16[64,96]{1,0:T(8,128)(2,1)S(1)} %get-tuple-element.37.refs_1_.refs_2_, ...), custom_call_target="tpu_custom_call" | custom-call | flops 50331648 | bytes 2097152 | tf_op jit(solution)/shard_map/halo_plane/pallas_call | solution.py:261
  8.4 0.0 copy-start.2
  8.4 0.0 copy-start.3
  8.4 0.2 collective-permute-start.4
  8.7 1.2 %collective-permute-done.2.refs_1_ = bf16[8,48,256]{2,1,0:T(8,128)(2,1)S(1)} collective-permute-done((bf16[8,48,256]{2,1,0:T(8,128)(2,1)S(1)}, bf16[8,48,256]{2,1,0:T(8,128)(2,1)S(1)}, u32[]{:S(2)}, u32[]{:S(2)}) %collective-permute-start.2) | collective-permute-done | bytes 196640 | tf_op jit(solution)/shard_map/ppermute | solution.py:30
  9.9 0.6 %halo_plane.3 = (bf16[32,16,128]{2,1,0:T(8,128)(2,1)S(1)}, bf16[32,16,128]{2,1,0:T(8,128)(2,1)S(1)}, bf16[32,16,128]{2,1,0:T(8,128)(2,1)S(1)}, bf16[32,16,128]{2,1,0:T(8,128)(2,1)S(1)}) custom-call(bf16[8,80,256]{2,1,0:T(8,128)(2,1)S(1)} %collective-permute-done.refs_0_, bf16[8,48,256]{2,1,0:T(8,128)(2,1)S(1)} %collective-permute-done.2.refs_1_, ...), custom_call_target="tpu_custom_call" | custom-call | flops 50331648 | bytes 2097152 | tf_op jit(solution)/shard_map/halo_plane/pallas_call | solution.py:261
  10.5 2.4 %collective-permute-start.3 = (bf16[32,16,128]{2,1,0:T(8,128)(2,1)S(1)}, bf16[32,16,128]{2,1,0:T(8,128)(2,1)S(1)}, u32[]{:S(2)}, u32[]{:S(2)}) collective-permute-start(bf16[32,16,128]{2,1,0:T(8,128)(2,1)S(1)} %get-tuple-element.38), channel_id=1, source_target_pairs={{0,1},{2,0},{3,2},{1,3},{4,5},{6,4},{7,6},{5,7},{8,9},{10,8},{11,1... | collective-permute-start | bytes 393224 | tf_op jit(solution)/shard_map/ppermute | solution.py:30
  12.9 0.3 collective-permute-done.4.one_ref
  13.2 0.1 collective-permute-start.5
  13.3 0.2 copy.11
  13.5 2.4 %collective-permute-start.1 = (bf16[32,16,128]{2,1,0:T(8,128)(2,1)S(1)}, bf16[32,16,128]{2,1,0:T(8,128)(2,1)S(1)}, u32[]{:S(2)}, u32[]{:S(2)}) collective-permute-start(bf16[32,16,128]{2,1,0:T(8,128)(2,1)S(1)} %get-tuple-element.36), channel_id=1, source_target_pairs={{0,1},{2,0},{3,2},{1,3},{4,5},{6,4},{7,6},{5,7},{8,9},{10,8},{11,1... | collective-permute-start | bytes 393224 | tf_op jit(solution)/shard_map/ppermute | solution.py:30
  15.9 0.2 collective-permute-start.6
  16.1 0.4 collective-permute-done.3.one_ref
  16.5 2.9 %collective-permute-done.5.refs_2_ = bf16[32,16,128]{2,1,0:T(8,128)(2,1)S(1)} collective-permute-done((bf16[32,16,128]{2,1,0:T(8,128)(2,1)S(1)}, bf16[32,16,128]{2,1,0:T(8,128)(2,1)S(1)}, u32[]{:S(2)}, u32[]{:S(2)}) %collective-permute-start.5) | collective-permute-done | bytes 131104 | tf_op jit(solution)/shard_map/ppermute | solution.py:30
  19.4 1.1 %collective-permute-start.7 = (bf16[32,16,128]{2,1,0:T(8,128)(2,1)S(1)}, bf16[32,16,128]{2,1,0:T(8,128)(2,1)S(1)}, u32[]{:S(2)}, u32[]{:S(2)}) collective-permute-start(bf16[32,16,128]{2,1,0:T(8,128)(2,1)S(1)} %add.7), channel_id=1, source_target_pairs={{0,1},{2,0},{3,2},{1,3},{4,5},{6,4},{7,6},{5,7},{8,9},{10,8},{11,1... | collective-permute-start | bytes 393224 | tf_op jit(solution)/shard_map/ppermute | solution.py:30
  20.5 3.0 %collective-permute-done.1.refs_1_ = bf16[32,16,128]{2,1,0:T(8,128)(2,1)S(1)} collective-permute-done((bf16[32,16,128]{2,1,0:T(8,128)(2,1)S(1)}, bf16[32,16,128]{2,1,0:T(8,128)(2,1)S(1)}, u32[]{:S(2)}, u32[]{:S(2)}) %collective-permute-start.1) | collective-permute-done | bytes 131104 | tf_op jit(solution)/shard_map/ppermute | solution.py:30
  23.5 0.1 broadcast_in_dim.4.refs_3_
  23.5 0.2 activation.2
  23.8 0.1 collective-permute-start.9
  23.8 3.3 %collective-permute-start.10 = (bf16[32,16,128]{2,1,0:T(8,128)(2,1)S(1)}, bf16[32,16,128]{2,1,0:T(8,128)(2,1)S(1)}, u32[]{:S(2)}, u32[]{:S(2)}) collective-permute-start(bf16[32,16,128]{2,1,0:T(8,128)(2,1)S(1)} %get-tuple-element.54.refs_3_.refs_5_), channel_id=1, source_target_pairs={{0,1},{2,0},{3,2},{1,3},{4,5},{6,4},{7,6},{5,7},{8,9},{10,8},{11,1... | collective-permute-start | bytes 393224 | tf_op jit(solution)/shard_map/ppermute | solution.py:30
  27.1 0.0 collective-permute-done.6.refs_1_
  27.1 2.0 %collective-permute-done.7.refs_2_ = bf16[32,16,128]{2,1,0:T(8,128)(2,1)S(1)} collective-permute-done((bf16[32,16,128]{2,1,0:T(8,128)(2,1)S(1)}, bf16[32,16,128]{2,1,0:T(8,128)(2,1)S(1)}, u32[]{:S(2)}, u32[]{:S(2)}) %collective-permute-start.7) | collective-permute-done | bytes 131104 | tf_op jit(solution)/shard_map/ppermute | solution.py:30
  29.1 0.2 activation.3
  29.4 3.3 %collective-permute-start.13 = (bf16[32,16,128]{2,1,0:T(8,128)(2,1)S(1)}, bf16[32,16,128]{2,1,0:T(8,128)(2,1)S(1)}, u32[]{:S(2)}, u32[]{:S(2)}) collective-permute-start(bf16[32,16,128]{2,1,0:T(8,128)(2,1)S(1)} %get-tuple-element.51.refs_9_), channel_id=1, source_target_pairs={{0,1},{2,0},{3,2},{1,3},{4,5},{6,4},{7,6},{5,7},{8,9},{10,8},{11,1... | collective-permute-start | bytes 393224 | tf_op jit(solution)/shard_map/ppermute | solution.py:30
  32.7 0.0 collective-permute-start.12
  32.7 3.0 %collective-permute-start.8 = (bf16[64,16,128]{2,1,0:T(8,128)(2,1)S(1)}, bf16[64,16,128]{2,1,0:T(8,128)(2,1)S(1)}, u32[]{:S(2)}, u32[]{:S(2)}) collective-permute-start(bf16[64,16,128]{2,1,0:T(8,128)(2,1)S(1)} %pad_maximum_fusion.1), channel_id=1, source_target_pairs={{0,28},{4,0},{8,4},{12,8},{16,12},{20,16},{24,20},{28,24},{1,29},{... | collective-permute-start | bytes 786440 | tf_op jit(solution)/shard_map/ppermute | solution.py:30
  35.6 0.0 collective-permute-done.9.refs_4_.refs_6_
  35.6 0.0 collective-permute-done.10.refs_6_.refs_8_
  35.6 1.2 %collective-permute-start.15 = (bf16[32,16,128]{2,1,0:T(8,128)(2,1)S(1)}, bf16[32,16,128]{2,1,0:T(8,128)(2,1)S(1)}, u32[]{:S(2)}, u32[]{:S(2)}) collective-permute-start(bf16[32,16,128]{2,1,0:T(8,128)(2,1)S(1)} %collective-permute-done.9.refs_4_.refs_6_), channel_id=1, source_target_pairs={{0,2},{2,3},{3,1},{1,0},{4,6},{6,7},{7,5},{5,4},{8,10},{10,11},{11... | collective-permute-start | bytes 393224 | tf_op jit(solution)/shard_map/ppermute | solution.py:30
  36.9 1.8 %collective-permute-start.11 = (bf16[64,16,128]{2,1,0:T(8,128)(2,1)S(1)}, bf16[64,16,128]{2,1,0:T(8,128)(2,1)S(1)}, u32[]{:S(2)}, u32[]{:S(2)}) collective-permute-start(bf16[64,16,128]{2,1,0:T(8,128)(2,1)S(1)} %pad_maximum_fusion.2), channel_id=1, source_target_pairs={{0,28},{4,0},{8,4},{12,8},{16,12},{20,16},{24,20},{28,24},{1,29},{... | collective-permute-start | bytes 786440 | tf_op jit(solution)/shard_map/ppermute | solution.py:30
  38.7 2.7 %collective-permute-start.17 = (bf16[32,16,128]{2,1,0:T(8,128)(2,1)S(1)}, bf16[32,16,128]{2,1,0:T(8,128)(2,1)S(1)}, u32[]{:S(2)}, u32[]{:S(2)}) collective-permute-start(bf16[32,16,128]{2,1,0:T(8,128)(2,1)S(1)} %collective-permute-done.13.refs_12_), channel_id=1, source_target_pairs={{0,1},{2,0},{3,2},{1,3},{4,5},{6,4},{7,6},{5,7},{8,9},{10,8},{11,1... | collective-permute-start | bytes 393224 | tf_op jit(solution)/shard_map/ppermute | solution.py:30
  41.4 0.0 collective-permute-done.12.refs_10_
  41.4 5.1 %collective-permute-start.14 = (bf16[64,16,128]{2,1,0:T(8,128)(2,1)S(1)}, bf16[64,16,128]{2,1,0:T(8,128)(2,1)S(1)}, u32[]{:S(2)}, u32[]{:S(2)}) collective-permute-start(bf16[64,16,128]{2,1,0:T(8,128)(2,1)S(1)} %pad_maximum_fusion.3), channel_id=1, source_target_pairs={{0,28},{4,0},{8,4},{12,8},{16,12},{20,16},{24,20},{28,24},{1,29},{... | collective-permute-start | bytes 786440 | tf_op jit(solution)/shard_map/ppermute | solution.py:30
  46.5 0.0 collective-permute-done.15.refs_5_.refs_7_
  46.5 0.1 collective-permute-start.16
  46.6 2.4 %collective-permute-start.18 = (bf16[32,16,128]{2,1,0:T(8,128)(2,1)S(1)}, bf16[32,16,128]{2,1,0:T(8,128)(2,1)S(1)}, u32[]{:S(2)}, u32[]{:S(2)}) collective-permute-start(bf16[32,16,128]{2,1,0:T(8,128)(2,1)S(1)} %collective-permute-done.17.refs_11_), channel_id=1, source_target_pairs={{0,28},{4,0},{8,4},{12,8},{16,12},{20,16},{24,20},{28,24},{1,29},{... | collective-permute-start | bytes 393224 | tf_op jit(solution)/shard_map/ppermute | solution.py:30
  49.0 0.8 %copy.8 = bf16[16,1,64,128]{3,2,1,0:T(8,128)(2,1)} copy(bf16[16,1,64,128]{3,0,2,1:T(8,128)(2,1)S(1)} %maximum_bitcast_fusion) | data formatting | bytes 524288
  49.8 3.6 %collective-permute-done.16.refs_2_.refs_3_ = bf16[32,16,128]{2,1,0:T(8,128)(2,1)S(1)} collective-permute-done((bf16[32,16,128]{2,1,0:T(8,128)(2,1)S(1)}, bf16[32,16,128]{2,1,0:T(8,128)(2,1)S(1)}, u32[]{:S(2)}, u32[]{:S(2)}) %collective-permute-start.16) | collective-permute-done | bytes 131104 | tf_op jit(solution)/shard_map/ppermute | solution.py:30
  53.4 0.9 %lower_grad.1.refs_14_ = bf16[8,2,48,256]{3,2,1,0:T(8,128)(2,1)S(1)} custom-call(bf16[64,16,128]{2,1,0:T(8,128)(2,1)S(1)} %collective-permute-done.8.refs_0_, bf16[64,16,128]{2,1,0:T(8,128)(2,1)S(1)} %collective-permute-done.11.refs_1_, bf16[32,16,128]{2,1,0:T(8,128)(2,1)S(1)} %collective-permute-done.16.refs_2_.refs_3_, ...), custom_call_target="tpu_custom_call" | custom-call | flops 150994944 | bytes 1048576 | tf_op jit(solution)/shard_map/lower_grad/pallas_call | solution.py:261
  54.3 0.5 collective-permute-done.18.refs_4_
  54.8 2.1 %upper_grad.1 = bf16[8,2,128,256]{3,2,1,0:T(8,128)(2,1)} custom-call(bf16[64,16,128]{2,1,0:T(8,128)(2,1)S(1)} %collective-permute-done.8.refs_0_, bf16[64,16,128]{2,1,0:T(8,128)(2,1)S(1)} %collective-permute-done.11.refs_1_, bf16[64,16,128]{2,1,0:T(8,128)(2,1)S(1)} %collective-permute-done.14.refs_2_, ...), custom_call_target="tpu_custom_call" | custom-call | flops 251658240 | bytes 1048576 | tf_op jit(solution)/shard_map/upper_grad/pallas_call | solution.py:261
  (22 shorter events, 0.3 us)
Async XLA Ops:
  0.6 3.2 %copy-start = (bf16[64,32,3,3,3]{0,1,4,3,2:T(8,128)(2,1)S(1)}, bf16[64,32,3,3,3]{0,1,4,3,2:T(8,128)(2,1)}, u32[]{:S(2)}) copy-start(bf16[64,32,3,3,3]{0,1,4,3,2:T(8,128)(2,1)} %param.5) | copy-start | bytes 331780
  0.6 3.5 %copy-start.1 = (bf16[8,2,128,256]{3,2,1,0:T(8,128)(2,1)S(1)}, bf16[8,2,128,256]{3,2,1,0:T(8,128)(2,1)}, u32[]{:S(2)}) copy-start(bf16[8,2,128,256]{3,2,1,0:T(8,128)(2,1)} %field_ref.1) | copy-start | bytes 3145732
  1.9 5.8 %collective-permute-start = (bf16[8,80,256]{2,1,0:T(8,128)(2,1)S(1)}, bf16[8,80,256]{2,1,0:T(8,128)(2,1)S(1)}, u32[]{:S(2)}, u32[]{:S(2)}) collective-permute-start(bf16[8,80,256]{2,1,0:T(8,128)(2,1)S(1)} %pad_maximum_fusion), channel_id=1, source_target_pairs={{0,4},{4,8},{8,12},{12,16},{16,20},{20,24},{24,28},{28,0},{1,5},{5... | collective-permute-start | bytes 983048 | tf_op jit(solution)/shard_map/ppermute | solution.py:30
  3.8 6.1 %collective-permute-start.2 = (bf16[8,48,256]{2,1,0:T(8,128)(2,1)S(1)}, bf16[8,48,256]{2,1,0:T(8,128)(2,1)S(1)}, u32[]{:S(2)}, u32[]{:S(2)}) collective-permute-start(bf16[8,48,256]{2,1,0:T(8,128)(2,1)S(1)} %slice.26), channel_id=1, source_target_pairs={{0,4},{4,8},{8,12},{12,16},{16,20},{20,24},{24,28},{28,0},{1,5},{5... | collective-permute-start | bytes 589832 | tf_op jit(solution)/shard_map/ppermute | solution.py:30
  8.4 4.9 %copy-start.2 = (bf16[16,1,64,128]{3,2,1,0:T(8,128)(2,1)S(1)}, bf16[16,1,64,128]{3,2,1,0:T(8,128)(2,1)}, u32[]{:S(2)}) copy-start(bf16[16,1,64,128]{3,2,1,0:T(8,128)(2,1)} %param.7) | copy-start | bytes 786436
  8.4 15.0 %copy-start.3 = (f32[16]{0:T(128)S(1)}, f32[16]{0:T(128)}, u32[]{:S(2)}) copy-start(f32[16]{0:T(128)} %param.6) | copy-start | bytes 196
  8.4 4.8 %collective-permute-start.4 = (bf16[32,16,128]{2,1,0:T(8,128)(2,1)S(1)}, bf16[32,16,128]{2,1,0:T(8,128)(2,1)S(1)}, u32[]{:S(2)}, u32[]{:S(2)}) collective-permute-start(bf16[32,16,128]{2,1,0:T(8,128)(2,1)S(1)} %get-tuple-element.40), channel_id=1, source_target_pairs={{0,2},{2,3},{3,1},{1,0},{4,6},{6,7},{7,5},{5,4},{8,10},{10,11},{11... | collective-permute-start | bytes 393224 | tf_op jit(solution)/shard_map/ppermute | solution.py:30
  10.5 6.0 %collective-permute-start.3 = (bf16[32,16,128]{2,1,0:T(8,128)(2,1)S(1)}, bf16[32,16,128]{2,1,0:T(8,128)(2,1)S(1)}, u32[]{:S(2)}, u32[]{:S(2)}) collective-permute-start(bf16[32,16,128]{2,1,0:T(8,128)(2,1)S(1)} %get-tuple-element.38), channel_id=1, source_target_pairs={{0,1},{2,0},{3,2},{1,3},{4,5},{6,4},{7,6},{5,7},{8,9},{10,8},{11,1... | collective-permute-start | bytes 393224 | tf_op jit(solution)/shard_map/ppermute | solution.py:30
  13.2 6.1 %collective-permute-start.5 = (bf16[32,16,128]{2,1,0:T(8,128)(2,1)S(1)}, bf16[32,16,128]{2,1,0:T(8,128)(2,1)S(1)}, u32[]{:S(2)}, u32[]{:S(2)}) collective-permute-start(bf16[32,16,128]{2,1,0:T(8,128)(2,1)S(1)} %add.6), channel_id=1, source_target_pairs={{0,2},{2,3},{3,1},{1,0},{4,6},{6,7},{7,5},{5,4},{8,10},{10,11},{11... | collective-permute-start | bytes 393224 | tf_op jit(solution)/shard_map/ppermute | solution.py:30
  13.5 10.0 %collective-permute-start.1 = (bf16[32,16,128]{2,1,0:T(8,128)(2,1)S(1)}, bf16[32,16,128]{2,1,0:T(8,128)(2,1)S(1)}, u32[]{:S(2)}, u32[]{:S(2)}) collective-permute-start(bf16[32,16,128]{2,1,0:T(8,128)(2,1)S(1)} %get-tuple-element.36), channel_id=1, source_target_pairs={{0,1},{2,0},{3,2},{1,3},{4,5},{6,4},{7,6},{5,7},{8,9},{10,8},{11,1... | collective-permute-start | bytes 393224 | tf_op jit(solution)/shard_map/ppermute | solution.py:30
  15.9 11.3 %collective-permute-start.6 = (bf16[32,16,128]{2,1,0:T(8,128)(2,1)S(1)}, bf16[32,16,128]{2,1,0:T(8,128)(2,1)S(1)}, u32[]{:S(2)}, u32[]{:S(2)}) collective-permute-start(bf16[32,16,128]{2,1,0:T(8,128)(2,1)S(1)} %get-tuple-element.46), channel_id=1, source_target_pairs={{0,2},{2,3},{3,1},{1,0},{4,6},{6,7},{7,5},{5,4},{8,10},{10,11},{11... | collective-permute-start | bytes 393224 | tf_op jit(solution)/shard_map/ppermute | solution.py:30
  19.4 9.7 %collective-permute-start.7 = (bf16[32,16,128]{2,1,0:T(8,128)(2,1)S(1)}, bf16[32,16,128]{2,1,0:T(8,128)(2,1)S(1)}, u32[]{:S(2)}, u32[]{:S(2)}) collective-permute-start(bf16[32,16,128]{2,1,0:T(8,128)(2,1)S(1)} %add.7), channel_id=1, source_target_pairs={{0,1},{2,0},{3,2},{1,3},{4,5},{6,4},{7,6},{5,7},{8,9},{10,8},{11,1... | collective-permute-start | bytes 393224 | tf_op jit(solution)/shard_map/ppermute | solution.py:30
  23.8 11.9 %collective-permute-start.9 = (bf16[32,16,128]{2,1,0:T(8,128)(2,1)S(1)}, bf16[32,16,128]{2,1,0:T(8,128)(2,1)S(1)}, u32[]{:S(2)}, u32[]{:S(2)}) collective-permute-start(bf16[32,16,128]{2,1,0:T(8,128)(2,1)S(1)} %get-tuple-element.54.refs_3_.refs_5_), channel_id=1, source_target_pairs={{0,2},{2,3},{3,1},{1,0},{4,6},{6,7},{7,5},{5,4},{8,10},{10,11},{11... | collective-permute-start | bytes 393224 | tf_op jit(solution)/shard_map/ppermute | solution.py:30
  23.8 11.8 %collective-permute-start.10 = (bf16[32,16,128]{2,1,0:T(8,128)(2,1)S(1)}, bf16[32,16,128]{2,1,0:T(8,128)(2,1)S(1)}, u32[]{:S(2)}, u32[]{:S(2)}) collective-permute-start(bf16[32,16,128]{2,1,0:T(8,128)(2,1)S(1)} %get-tuple-element.54.refs_3_.refs_5_), channel_id=1, source_target_pairs={{0,1},{2,0},{3,2},{1,3},{4,5},{6,4},{7,6},{5,7},{8,9},{10,8},{11,1... | collective-permute-start | bytes 393224 | tf_op jit(solution)/shard_map/ppermute | solution.py:30
  29.4 9.3 %collective-permute-start.13 = (bf16[32,16,128]{2,1,0:T(8,128)(2,1)S(1)}, bf16[32,16,128]{2,1,0:T(8,128)(2,1)S(1)}, u32[]{:S(2)}, u32[]{:S(2)}) collective-permute-start(bf16[32,16,128]{2,1,0:T(8,128)(2,1)S(1)} %get-tuple-element.51.refs_9_), channel_id=1, source_target_pairs={{0,1},{2,0},{3,2},{1,3},{4,5},{6,4},{7,6},{5,7},{8,9},{10,8},{11,1... | collective-permute-start | bytes 393224 | tf_op jit(solution)/shard_map/ppermute | solution.py:30
  32.7 8.7 %collective-permute-start.12 = (bf16[32,16,128]{2,1,0:T(8,128)(2,1)S(1)}, bf16[32,16,128]{2,1,0:T(8,128)(2,1)S(1)}, u32[]{:S(2)}, u32[]{:S(2)}) collective-permute-start(bf16[32,16,128]{2,1,0:T(8,128)(2,1)S(1)} %get-tuple-element.51.refs_9_), channel_id=1, source_target_pairs={{0,2},{2,3},{3,1},{1,0},{4,6},{6,7},{7,5},{5,4},{8,10},{10,11},{11... | collective-permute-start | bytes 393224 | tf_op jit(solution)/shard_map/ppermute | solution.py:30
  32.7 20.7 %collective-permute-start.8 = (bf16[64,16,128]{2,1,0:T(8,128)(2,1)S(1)}, bf16[64,16,128]{2,1,0:T(8,128)(2,1)S(1)}, u32[]{:S(2)}, u32[]{:S(2)}) collective-permute-start(bf16[64,16,128]{2,1,0:T(8,128)(2,1)S(1)} %pad_maximum_fusion.1), channel_id=1, source_target_pairs={{0,28},{4,0},{8,4},{12,8},{16,12},{20,16},{24,20},{28,24},{1,29},{... | collective-permute-start | bytes 786440 | tf_op jit(solution)/shard_map/ppermute | solution.py:30
  35.6 10.9 %collective-permute-start.15 = (bf16[32,16,128]{2,1,0:T(8,128)(2,1)S(1)}, bf16[32,16,128]{2,1,0:T(8,128)(2,1)S(1)}, u32[]{:S(2)}, u32[]{:S(2)}) collective-permute-start(bf16[32,16,128]{2,1,0:T(8,128)(2,1)S(1)} %collective-permute-done.9.refs_4_.refs_6_), channel_id=1, source_target_pairs={{0,2},{2,3},{3,1},{1,0},{4,6},{6,7},{7,5},{5,4},{8,10},{10,11},{11... | collective-permute-start | bytes 393224 | tf_op jit(solution)/shard_map/ppermute | solution.py:30
  36.9 16.6 %collective-permute-start.11 = (bf16[64,16,128]{2,1,0:T(8,128)(2,1)S(1)}, bf16[64,16,128]{2,1,0:T(8,128)(2,1)S(1)}, u32[]{:S(2)}, u32[]{:S(2)}) collective-permute-start(bf16[64,16,128]{2,1,0:T(8,128)(2,1)S(1)} %pad_maximum_fusion.2), channel_id=1, source_target_pairs={{0,28},{4,0},{8,4},{12,8},{16,12},{20,16},{24,20},{28,24},{1,29},{... | collective-permute-start | bytes 786440 | tf_op jit(solution)/shard_map/ppermute | solution.py:30
  38.7 8.0 %collective-permute-start.17 = (bf16[32,16,128]{2,1,0:T(8,128)(2,1)S(1)}, bf16[32,16,128]{2,1,0:T(8,128)(2,1)S(1)}, u32[]{:S(2)}, u32[]{:S(2)}) collective-permute-start(bf16[32,16,128]{2,1,0:T(8,128)(2,1)S(1)} %collective-permute-done.13.refs_12_), channel_id=1, source_target_pairs={{0,1},{2,0},{3,2},{1,3},{4,5},{6,4},{7,6},{5,7},{8,9},{10,8},{11,1... | collective-permute-start | bytes 393224 | tf_op jit(solution)/shard_map/ppermute | solution.py:30
  41.4 13.4 %collective-permute-start.14 = (bf16[64,16,128]{2,1,0:T(8,128)(2,1)S(1)}, bf16[64,16,128]{2,1,0:T(8,128)(2,1)S(1)}, u32[]{:S(2)}, u32[]{:S(2)}) collective-permute-start(bf16[64,16,128]{2,1,0:T(8,128)(2,1)S(1)} %pad_maximum_fusion.3), channel_id=1, source_target_pairs={{0,28},{4,0},{8,4},{12,8},{16,12},{20,16},{24,20},{28,24},{1,29},{... | collective-permute-start | bytes 786440 | tf_op jit(solution)/shard_map/ppermute | solution.py:30
  46.5 6.9 %collective-permute-start.16 = (bf16[32,16,128]{2,1,0:T(8,128)(2,1)S(1)}, bf16[32,16,128]{2,1,0:T(8,128)(2,1)S(1)}, u32[]{:S(2)}, u32[]{:S(2)}) collective-permute-start(bf16[32,16,128]{2,1,0:T(8,128)(2,1)S(1)} %collective-permute-done.15.refs_5_.refs_7_), channel_id=1, source_target_pairs={{0,28},{4,0},{8,4},{12,8},{16,12},{20,16},{24,20},{28,24},{1,29},{... | collective-permute-start | bytes 393224 | tf_op jit(solution)/shard_map/ppermute | solution.py:30
  46.6 8.2 %collective-permute-start.18 = (bf16[32,16,128]{2,1,0:T(8,128)(2,1)S(1)}, bf16[32,16,128]{2,1,0:T(8,128)(2,1)S(1)}, u32[]{:S(2)}, u32[]{:S(2)}) collective-permute-start(bf16[32,16,128]{2,1,0:T(8,128)(2,1)S(1)} %collective-permute-done.17.refs_11_), channel_id=1, source_target_pairs={{0,28},{4,0},{8,4},{12,8},{16,12},{20,16},{24,20},{28,24},{1,29},{... | collective-permute-start | bytes 393224 | tf_op jit(solution)/shard_map/ppermute | solution.py:30

commit v6 on v5

--- a/solution.py
+++ b/solution.py
@@ -214,7 +214,7 @@
     place = ring_place(me_ref[0], peers)
 
     def tile(tap_x, tap_y, tap_z):
-        return own_ref[(tap_x * 3 + tap_y) * 3 + tap_z].astype(F32)
+        return own_ref[(tap_x * 3 + tap_y) * 3 + tap_z]
 
     none = jnp.zeros((chans, total), F32)
 
@@ -293,6 +293,7 @@
     own = lax.dynamic_slice_in_dim(jnp.transpose(kernel, (2, 3, 4, 1, 0)), me * cin, cin, 3)
     own = own.reshape(27, cin, peers, cout)
     own = jnp.pad(own, ((0, 0), fill_c, (0, 0), fill_o)).reshape(27, chans, total)
+    own = own.astype(F32)
     field_p = jnp.pad(field, (fill_c, (0, 0), (0, 0), (0, 0)))
 
     points = half_y * half_z
@@ -315,9 +316,7 @@
         "local_planes",
         jax.ShapeDtypeStruct((total, points), F32),
         (field_p, weights_local),
-        [
-            pltpu.VMEM((planes * 6 * chans, (1 + half_y) * half_z), BF16),
-        ],
+        [pltpu.VMEM((planes * 6 * chans, (1 + half_y) * half_z), BF16)],
         flops=2 * total * 24 * chans * points,
         bytes_accessed=1 << 22,
     )

time: 57.1 us -> 57.1 us (level)
  other arithmetic: 0.12 us -> 0.95 us
  waiting for transfers between devices: 16.1 us -> 15.3 us
    convert_element_type x0 -> x1, other arithmetic: none -> 0.83 us  [on_device(): own = own.astype(F32)]
    ppermute x19, waiting for transfers between devices: 16.1 us -> 15.3 us  [shifted(): lax.ppermute(block, axis, [(ring[i], ring[(i + distance) % count]) for i...]
  transfers between devices with their start and end apart: 19 -> 19, of which waited for: 9 -> 9; matrix products, arithmetic and copies ran while one was open for 2% -> 3% of each run, Pallas kernels for 8% -> 8%
where the time goes in v6:
time: 57.1 us; the launch traced here: 56.9 us
  starting transfers between devices  31 us (54%)
  waiting for transfers between devices  15.3 us (27%)
  Pallas kernels  6.55 us (11%)
  local copies, waits for them, and re-layouts  2.26 us (4%)
  other arithmetic  0.95 us (2%)
  between operations  0.8 us (1%)
    ppermute x19, starting transfers between devices, shifted(): lax.ppermute(block, axis, [(ring[i], ring[(i + distance) % count]) for i...  31 us
    ppermute x19, waiting for transfers between devices, shifted(): lax.ppermute(block, axis, [(ring[i], ring[(i + distance) % count]) for i...  15.3 us
    pallas_call x9, Pallas kernels, call(): pl.pallas_call(kernel, out_shape=out_shape, scratch_shapes=list(scratch),...  6.32 us
    squeeze x1, local copies, waits for them, and re-layouts, on_device(): plane = lax.optimization_barrier(field[:, planes - 1])  1.17 us
  transfers between devices with their start and end apart: 19, of which 9 were waited for; matrix products, arithmetic and copies ran while one was open for 3% of the time, Pallas kernels for 8%

profile of v6, /device:TPU:11, one launch (start us, length us, event | category | flops | bytes accessed | tf_op | source)
XLA Modules:
  0.0 56.9 jit_solution(8775257802732937079)
XLA Ops:
  0.6 1.2 %slice_bitcast_fusion = bf16[8,128,256]{2,1,0:T(8,128)(2,1)S(1)} fusion(bf16[8,2,128,256]{3,2,1,0:T(8,128)(2,1)} %field_ref.1), kind=kLoop, calls=%fused_computation | loop fusion | bytes 1048576 | tf_op jit(solution)/shard_map/squeeze | solution.py:284
  1.9 1.8 %collective-permute-start = (bf16[8,80,256]{2,1,0:T(8,128)(2,1)S(1)}, bf16[8,80,256]{2,1,0:T(8,128)(2,1)S(1)}, u32[]{:S(2)}, u32[]{:S(2)}) collective-permute-start(bf16[8,80,256]{2,1,0:T(8,128)(2,1)S(1)} %pad_maximum_fusion), channel_id=1, source_target_pairs={{0,4},{4,8},{8,12},{12,16},{16,20},{20,24},{24,28},{28,0},{1,5},{5... | collective-permute-start | bytes 983048 | tf_op jit(solution)/shard_map/ppermute | solution.py:30
  3.7 0.1 collective-permute-start.2
  3.8 0.8 %dynamic-slice_convert_fusion = f32[64,8,3,3,3]{0,1,4,3,2:T(8,128)S(1)} fusion(bf16[64,32,3,3,3]{0,1,4,3,2:T(8,128)(2,1)} %param.5, s32[]{:T(128)S(6)} %select_n.3), kind=kLoop, calls=%fused_computation.7 | loop fusion | flops 13824 | bytes 82948 | tf_op jit(solution)/shard_map/convert_element_type | solution.py:296
  4.6 0.2 weights.1
  4.9 1.5 %local_planes.1.refs_2_.refs_3_ = f32[64,8192]{1,0:T(8,128)S(1)} custom-call(bf16[8,2,128,256]{3,2,1,0:T(8,128)(2,1)S(1)} %copy-done, bf16[64,192]{1,0:T(8,128)(2,1)S(1)} %get-tuple-element.30.weight_ref), custom_call_target="tpu_custom_call" | custom-call | flops 201326592 | bytes 4194304 | tf_op jit(solution)/shard_map/local_planes/pallas_call | solution.py:261
  6.4 1.3 %collective-permute-done.refs_0_ = bf16[8,80,256]{2,1,0:T(8,128)(2,1)S(1)} collective-permute-done((bf16[8,80,256]{2,1,0:T(8,128)(2,1)S(1)}, bf16[8,80,256]{2,1,0:T(8,128)(2,1)S(1)}, u32[]{:S(2)}, u32[]{:S(2)}) %collective-permute-start) | collective-permute-done | bytes 327712 | tf_op jit(solution)/shard_map/ppermute | solution.py:30
  7.7 0.6 %halo_plane.2 = (bf16[32,16,128]{2,1,0:T(8,128)(2,1)S(1)}, bf16[32,16,128]{2,1,0:T(8,128)(2,1)S(1)}, bf16[32,16,128]{2,1,0:T(8,128)(2,1)S(1)}, bf16[32,16,128]{2,1,0:T(8,128)(2,1)S(1)}) custom-call(bf16[8,80,256]{2,1,0:T(8,128)(2,1)S(1)} %collective-permute-done.refs_0_, bf16[64,96]{1,0:T(8,128)(2,1)S(1)} %get-tuple-element.37.refs_1_.refs_2_, ...), custom_call_target="tpu_custom_call" | custom-call | flops 50331648 | bytes 2097152 | tf_op jit(solution)/shard_map/halo_plane/pallas_call | solution.py:261
  8.4 0.0 copy-start.1
  8.4 0.0 copy-start.2
  8.4 0.2 collective-permute-start.4
  8.6 1.2 %collective-permute-done.2.refs_1_ = bf16[8,48,256]{2,1,0:T(8,128)(2,1)S(1)} collective-permute-done((bf16[8,48,256]{2,1,0:T(8,128)(2,1)S(1)}, bf16[8,48,256]{2,1,0:T(8,128)(2,1)S(1)}, u32[]{:S(2)}, u32[]{:S(2)}) %collective-permute-start.2) | collective-permute-done | bytes 196640 | tf_op jit(solution)/shard_map/ppermute | solution.py:30
  9.8 0.6 %halo_plane.3 = (bf16[32,16,128]{2,1,0:T(8,128)(2,1)S(1)}, bf16[32,16,128]{2,1,0:T(8,128)(2,1)S(1)}, bf16[32,16,128]{2,1,0:T(8,128)(2,1)S(1)}, bf16[32,16,128]{2,1,0:T(8,128)(2,1)S(1)}) custom-call(bf16[8,80,256]{2,1,0:T(8,128)(2,1)S(1)} %collective-permute-done.refs_0_, bf16[8,48,256]{2,1,0:T(8,128)(2,1)S(1)} %collective-permute-done.2.refs_1_, ...), custom_call_target="tpu_custom_call" | custom-call | flops 50331648 | bytes 2097152 | tf_op jit(solution)/shard_map/halo_plane/pallas_call | solution.py:261
  10.5 2.4 %collective-permute-start.3 = (bf16[32,16,128]{2,1,0:T(8,128)(2,1)S(1)}, bf16[32,16,128]{2,1,0:T(8,128)(2,1)S(1)}, u32[]{:S(2)}, u32[]{:S(2)}) collective-permute-start(bf16[32,16,128]{2,1,0:T(8,128)(2,1)S(1)} %get-tuple-element.38), channel_id=1, source_target_pairs={{0,1},{2,0},{3,2},{1,3},{4,5},{6,4},{7,6},{5,7},{8,9},{10,8},{11,1... | collective-permute-start | bytes 393224 | tf_op jit(solution)/shard_map/ppermute | solution.py:30
  12.8 0.3 collective-permute-done.4.one_ref
  13.2 0.1 collective-permute-start.5
  13.3 0.2 copy.11
  13.5 2.4 %collective-permute-start.1 = (bf16[32,16,128]{2,1,0:T(8,128)(2,1)S(1)}, bf16[32,16,128]{2,1,0:T(8,128)(2,1)S(1)}, u32[]{:S(2)}, u32[]{:S(2)}) collective-permute-start(bf16[32,16,128]{2,1,0:T(8,128)(2,1)S(1)} %get-tuple-element.36), channel_id=1, source_target_pairs={{0,1},{2,0},{3,2},{1,3},{4,5},{6,4},{7,6},{5,7},{8,9},{10,8},{11,1... | collective-permute-start | bytes 393224 | tf_op jit(solution)/shard_map/ppermute | solution.py:30
  15.9 0.2 collective-permute-start.6
  16.1 0.4 collective-permute-done.3.one_ref
  16.5 2.9 %collective-permute-done.5.refs_2_ = bf16[32,16,128]{2,1,0:T(8,128)(2,1)S(1)} collective-permute-done((bf16[32,16,128]{2,1,0:T(8,128)(2,1)S(1)}, bf16[32,16,128]{2,1,0:T(8,128)(2,1)S(1)}, u32[]{:S(2)}, u32[]{:S(2)}) %collective-permute-start.5) | collective-permute-done | bytes 131104 | tf_op jit(solution)/shard_map/ppermute | solution.py:30
  19.4 1.1 %collective-permute-start.7 = (bf16[32,16,128]{2,1,0:T(8,128)(2,1)S(1)}, bf16[32,16,128]{2,1,0:T(8,128)(2,1)S(1)}, u32[]{:S(2)}, u32[]{:S(2)}) collective-permute-start(bf16[32,16,128]{2,1,0:T(8,128)(2,1)S(1)} %add.7), channel_id=1, source_target_pairs={{0,1},{2,0},{3,2},{1,3},{4,5},{6,4},{7,6},{5,7},{8,9},{10,8},{11,1... | collective-permute-start | bytes 393224 | tf_op jit(solution)/shard_map/ppermute | solution.py:30
  20.4 3.0 %collective-permute-done.1.refs_1_ = bf16[32,16,128]{2,1,0:T(8,128)(2,1)S(1)} collective-permute-done((bf16[32,16,128]{2,1,0:T(8,128)(2,1)S(1)}, bf16[32,16,128]{2,1,0:T(8,128)(2,1)S(1)}, u32[]{:S(2)}, u32[]{:S(2)}) %collective-permute-start.1) | collective-permute-done | bytes 131104 | tf_op jit(solution)/shard_map/ppermute | solution.py:30
  23.4 0.1 broadcast_in_dim.4.refs_3_
  23.5 0.2 activation.2
  23.7 0.1 collective-permute-start.9
  23.8 3.3 %collective-permute-start.10 = (bf16[32,16,128]{2,1,0:T(8,128)(2,1)S(1)}, bf16[32,16,128]{2,1,0:T(8,128)(2,1)S(1)}, u32[]{:S(2)}, u32[]{:S(2)}) collective-permute-start(bf16[32,16,128]{2,1,0:T(8,128)(2,1)S(1)} %get-tuple-element.54.refs_3_.refs_5_), channel_id=1, source_target_pairs={{0,1},{2,0},{3,2},{1,3},{4,5},{6,4},{7,6},{5,7},{8,9},{10,8},{11,1... | collective-permute-start | bytes 393224 | tf_op jit(solution)/shard_map/ppermute | solution.py:30
  27.1 0.0 collective-permute-done.6.refs_1_
  27.1 2.0 %collective-permute-done.7.refs_2_ = bf16[32,16,128]{2,1,0:T(8,128)(2,1)S(1)} collective-permute-done((bf16[32,16,128]{2,1,0:T(8,128)(2,1)S(1)}, bf16[32,16,128]{2,1,0:T(8,128)(2,1)S(1)}, u32[]{:S(2)}, u32[]{:S(2)}) %collective-permute-start.7) | collective-permute-done | bytes 131104 | tf_op jit(solution)/shard_map/ppermute | solution.py:30
  29.1 0.2 activation.3
  29.3 3.3 %collective-permute-start.13 = (bf16[32,16,128]{2,1,0:T(8,128)(2,1)S(1)}, bf16[32,16,128]{2,1,0:T(8,128)(2,1)S(1)}, u32[]{:S(2)}, u32[]{:S(2)}) collective-permute-start(bf16[32,16,128]{2,1,0:T(8,128)(2,1)S(1)} %get-tuple-element.51.refs_9_), channel_id=1, source_target_pairs={{0,1},{2,0},{3,2},{1,3},{4,5},{6,4},{7,6},{5,7},{8,9},{10,8},{11,1... | collective-permute-start | bytes 393224 | tf_op jit(solution)/shard_map/ppermute | solution.py:30
  32.6 0.0 collective-permute-start.12
  32.7 3.0 %collective-permute-start.8 = (bf16[64,16,128]{2,1,0:T(8,128)(2,1)S(1)}, bf16[64,16,128]{2,1,0:T(8,128)(2,1)S(1)}, u32[]{:S(2)}, u32[]{:S(2)}) collective-permute-start(bf16[64,16,128]{2,1,0:T(8,128)(2,1)S(1)} %pad_maximum_fusion.1), channel_id=1, source_target_pairs={{0,28},{4,0},{8,4},{12,8},{16,12},{20,16},{24,20},{28,24},{1,29},{... | collective-permute-start | bytes 786440 | tf_op jit(solution)/shard_map/ppermute | solution.py:30
  35.6 1.2 %collective-permute-start.15 = (bf16[32,16,128]{2,1,0:T(8,128)(2,1)S(1)}, bf16[32,16,128]{2,1,0:T(8,128)(2,1)S(1)}, u32[]{:S(2)}, u32[]{:S(2)}) collective-permute-start(bf16[32,16,128]{2,1,0:T(8,128)(2,1)S(1)} %collective-permute-done.9.refs_4_.refs_6_), channel_id=1, source_target_pairs={{0,2},{2,3},{3,1},{1,0},{4,6},{6,7},{7,5},{5,4},{8,10},{10,11},{11... | collective-permute-start | bytes 393224 | tf_op jit(solution)/shard_map/ppermute | solution.py:30
  36.9 1.8 %collective-permute-start.11 = (bf16[64,16,128]{2,1,0:T(8,128)(2,1)S(1)}, bf16[64,16,128]{2,1,0:T(8,128)(2,1)S(1)}, u32[]{:S(2)}, u32[]{:S(2)}) collective-permute-start(bf16[64,16,128]{2,1,0:T(8,128)(2,1)S(1)} %pad_maximum_fusion.2), channel_id=1, source_target_pairs={{0,28},{4,0},{8,4},{12,8},{16,12},{20,16},{24,20},{28,24},{1,29},{... | collective-permute-start | bytes 786440 | tf_op jit(solution)/shard_map/ppermute | solution.py:30
  38.6 2.7 %collective-permute-start.17 = (bf16[32,16,128]{2,1,0:T(8,128)(2,1)S(1)}, bf16[32,16,128]{2,1,0:T(8,128)(2,1)S(1)}, u32[]{:S(2)}, u32[]{:S(2)}) collective-permute-start(bf16[32,16,128]{2,1,0:T(8,128)(2,1)S(1)} %collective-permute-done.13.refs_12_), channel_id=1, source_target_pairs={{0,1},{2,0},{3,2},{1,3},{4,5},{6,4},{7,6},{5,7},{8,9},{10,8},{11,1... | collective-permute-start | bytes 393224 | tf_op jit(solution)/shard_map/ppermute | solution.py:30
  41.4 5.1 %collective-permute-start.14 = (bf16[64,16,128]{2,1,0:T(8,128)(2,1)S(1)}, bf16[64,16,128]{2,1,0:T(8,128)(2,1)S(1)}, u32[]{:S(2)}, u32[]{:S(2)}) collective-permute-start(bf16[64,16,128]{2,1,0:T(8,128)(2,1)S(1)} %pad_maximum_fusion.3), channel_id=1, source_target_pairs={{0,28},{4,0},{8,4},{12,8},{16,12},{20,16},{24,20},{28,24},{1,29},{... | collective-permute-start | bytes 786440 | tf_op jit(solution)/shard_map/ppermute | solution.py:30
  46.5 0.0 collective-permute-done.15.refs_5_.refs_7_
  46.5 0.1 collective-permute-start.16
  46.6 0.0 collective-permute-done.17.refs_11_
  46.6 2.4 %collective-permute-start.18 = (bf16[32,16,128]{2,1,0:T(8,128)(2,1)S(1)}, bf16[32,16,128]{2,1,0:T(8,128)(2,1)S(1)}, u32[]{:S(2)}, u32[]{:S(2)}) collective-permute-start(bf16[32,16,128]{2,1,0:T(8,128)(2,1)S(1)} %collective-permute-done.17.refs_11_), channel_id=1, source_target_pairs={{0,28},{4,0},{8,4},{12,8},{16,12},{20,16},{24,20},{28,24},{1,29},{... | collective-permute-start | bytes 393224 | tf_op jit(solution)/shard_map/ppermute | solution.py:30
  49.0 0.8 %copy.8 = bf16[16,1,64,128]{3,2,1,0:T(8,128)(2,1)} copy(bf16[16,1,64,128]{3,0,2,1:T(8,128)(2,1)S(1)} %maximum_bitcast_fusion) | data formatting | bytes 524288
  49.7 3.7 %collective-permute-done.16.refs_2_.refs_3_ = bf16[32,16,128]{2,1,0:T(8,128)(2,1)S(1)} collective-permute-done((bf16[32,16,128]{2,1,0:T(8,128)(2,1)S(1)}, bf16[32,16,128]{2,1,0:T(8,128)(2,1)S(1)}, u32[]{:S(2)}, u32[]{:S(2)}) %collective-permute-start.16) | collective-permute-done | bytes 131104 | tf_op jit(solution)/shard_map/ppermute | solution.py:30
  53.4 0.0 collective-permute-done.8.refs_0_
  53.4 0.0 collective-permute-done.11.refs_1_
  53.4 0.9 %lower_grad.1.refs_14_ = bf16[8,2,48,256]{3,2,1,0:T(8,128)(2,1)S(1)} custom-call(bf16[64,16,128]{2,1,0:T(8,128)(2,1)S(1)} %collective-permute-done.8.refs_0_, bf16[64,16,128]{2,1,0:T(8,128)(2,1)S(1)} %collective-permute-done.11.refs_1_, bf16[32,16,128]{2,1,0:T(8,128)(2,1)S(1)} %collective-permute-done.16.refs_2_.refs_3_, ...), custom_call_target="tpu_custom_call" | custom-call | flops 150994944 | bytes 1048576 | tf_op jit(solution)/shard_map/lower_grad/pallas_call | solution.py:261
  54.3 0.5 collective-permute-done.18.refs_4_
  54.8 2.1 %upper_grad.1 = bf16[8,2,128,256]{3,2,1,0:T(8,128)(2,1)} custom-call(bf16[64,16,128]{2,1,0:T(8,128)(2,1)S(1)} %collective-permute-done.8.refs_0_, bf16[64,16,128]{2,1,0:T(8,128)(2,1)S(1)} %collective-permute-done.11.refs_1_, bf16[64,16,128]{2,1,0:T(8,128)(2,1)S(1)} %collective-permute-done.14.refs_2_, ...), custom_call_target="tpu_custom_call" | custom-call | flops 251658240 | bytes 1048576 | tf_op jit(solution)/shard_map/upper_grad/pallas_call | solution.py:261
  (20 shorter events, 0.3 us)
Async XLA Ops:
  0.6 4.2 %copy-start = (bf16[8,2,128,256]{3,2,1,0:T(8,128)(2,1)S(1)}, bf16[8,2,128,256]{3,2,1,0:T(8,128)(2,1)}, u32[]{:S(2)}) copy-start(bf16[8,2,128,256]{3,2,1,0:T(8,128)(2,1)} %field_ref.1) | copy-start | bytes 3145732
  1.9 5.8 %collective-permute-start = (bf16[8,80,256]{2,1,0:T(8,128)(2,1)S(1)}, bf16[8,80,256]{2,1,0:T(8,128)(2,1)S(1)}, u32[]{:S(2)}, u32[]{:S(2)}) collective-permute-start(bf16[8,80,256]{2,1,0:T(8,128)(2,1)S(1)} %pad_maximum_fusion), channel_id=1, source_target_pairs={{0,4},{4,8},{8,12},{12,16},{16,20},{20,24},{24,28},{28,0},{1,5},{5... | collective-permute-start | bytes 983048 | tf_op jit(solution)/shard_map/ppermute | solution.py:30
  3.7 6.1 %collective-permute-start.2 = (bf16[8,48,256]{2,1,0:T(8,128)(2,1)S(1)}, bf16[8,48,256]{2,1,0:T(8,128)(2,1)S(1)}, u32[]{:S(2)}, u32[]{:S(2)}) collective-permute-start(bf16[8,48,256]{2,1,0:T(8,128)(2,1)S(1)} %slice.26), channel_id=1, source_target_pairs={{0,4},{4,8},{8,12},{12,16},{16,20},{20,24},{24,28},{28,0},{1,5},{5... | collective-permute-start | bytes 589832 | tf_op jit(solution)/shard_map/ppermute | solution.py:30
  8.4 4.9 %copy-start.1 = (bf16[16,1,64,128]{3,2,1,0:T(8,128)(2,1)S(1)}, bf16[16,1,64,128]{3,2,1,0:T(8,128)(2,1)}, u32[]{:S(2)}) copy-start(bf16[16,1,64,128]{3,2,1,0:T(8,128)(2,1)} %param.7) | copy-start | bytes 786436
  8.4 15.0 %copy-start.2 = (f32[16]{0:T(128)S(1)}, f32[16]{0:T(128)}, u32[]{:S(2)}) copy-start(f32[16]{0:T(128)} %param.6) | copy-start | bytes 196
  8.4 4.8 %collective-permute-start.4 = (bf16[32,16,128]{2,1,0:T(8,128)(2,1)S(1)}, bf16[32,16,128]{2,1,0:T(8,128)(2,1)S(1)}, u32[]{:S(2)}, u32[]{:S(2)}) collective-permute-start(bf16[32,16,128]{2,1,0:T(8,128)(2,1)S(1)} %get-tuple-element.40), channel_id=1, source_target_pairs={{0,2},{2,3},{3,1},{1,0},{4,6},{6,7},{7,5},{5,4},{8,10},{10,11},{11... | collective-permute-start | bytes 393224 | tf_op jit(solution)/shard_map/ppermute | solution.py:30
  10.5 6.0 %collective-permute-start.3 = (bf16[32,16,128]{2,1,0:T(8,128)(2,1)S(1)}, bf16[32,16,128]{2,1,0:T(8,128)(2,1)S(1)}, u32[]{:S(2)}, u32[]{:S(2)}) collective-permute-start(bf16[32,16,128]{2,1,0:T(8,128)(2,1)S(1)} %get-tuple-element.38), channel_id=1, source_target_pairs={{0,1},{2,0},{3,2},{1,3},{4,5},{6,4},{7,6},{5,7},{8,9},{10,8},{11,1... | collective-permute-start | bytes 393224 | tf_op jit(solution)/shard_map/ppermute | solution.py:30
  13.2 6.1 %collective-permute-start.5 = (bf16[32,16,128]{2,1,0:T(8,128)(2,1)S(1)}, bf16[32,16,128]{2,1,0:T(8,128)(2,1)S(1)}, u32[]{:S(2)}, u32[]{:S(2)}) collective-permute-start(bf16[32,16,128]{2,1,0:T(8,128)(2,1)S(1)} %add.6), channel_id=1, source_target_pairs={{0,2},{2,3},{3,1},{1,0},{4,6},{6,7},{7,5},{5,4},{8,10},{10,11},{11... | collective-permute-start | bytes 393224 | tf_op jit(solution)/shard_map/ppermute | solution.py:30
  13.5 10.0 %collective-permute-start.1 = (bf16[32,16,128]{2,1,0:T(8,128)(2,1)S(1)}, bf16[32,16,128]{2,1,0:T(8,128)(2,1)S(1)}, u32[]{:S(2)}, u32[]{:S(2)}) collective-permute-start(bf16[32,16,128]{2,1,0:T(8,128)(2,1)S(1)} %get-tuple-element.36), channel_id=1, source_target_pairs={{0,1},{2,0},{3,2},{1,3},{4,5},{6,4},{7,6},{5,7},{8,9},{10,8},{11,1... | collective-permute-start | bytes 393224 | tf_op jit(solution)/shard_map/ppermute | solution.py:30
  15.9 11.3 %collective-permute-start.6 = (bf16[32,16,128]{2,1,0:T(8,128)(2,1)S(1)}, bf16[32,16,128]{2,1,0:T(8,128)(2,1)S(1)}, u32[]{:S(2)}, u32[]{:S(2)}) collective-permute-start(bf16[32,16,128]{2,1,0:T(8,128)(2,1)S(1)} %get-tuple-element.46), channel_id=1, source_target_pairs={{0,2},{2,3},{3,1},{1,0},{4,6},{6,7},{7,5},{5,4},{8,10},{10,11},{11... | collective-permute-start | bytes 393224 | tf_op jit(solution)/shard_map/ppermute | solution.py:30
  19.4 9.7 %collective-permute-start.7 = (bf16[32,16,128]{2,1,0:T(8,128)(2,1)S(1)}, bf16[32,16,128]{2,1,0:T(8,128)(2,1)S(1)}, u32[]{:S(2)}, u32[]{:S(2)}) collective-permute-start(bf16[32,16,128]{2,1,0:T(8,128)(2,1)S(1)} %add.7), channel_id=1, source_target_pairs={{0,1},{2,0},{3,2},{1,3},{4,5},{6,4},{7,6},{5,7},{8,9},{10,8},{11,1... | collective-permute-start | bytes 393224 | tf_op jit(solution)/shard_map/ppermute | solution.py:30
  23.7 11.9 %collective-permute-start.9 = (bf16[32,16,128]{2,1,0:T(8,128)(2,1)S(1)}, bf16[32,16,128]{2,1,0:T(8,128)(2,1)S(1)}, u32[]{:S(2)}, u32[]{:S(2)}) collective-permute-start(bf16[32,16,128]{2,1,0:T(8,128)(2,1)S(1)} %get-tuple-element.54.refs_3_.refs_5_), channel_id=1, source_target_pairs={{0,2},{2,3},{3,1},{1,0},{4,6},{6,7},{7,5},{5,4},{8,10},{10,11},{11... | collective-permute-start | bytes 393224 | tf_op jit(solution)/shard_map/ppermute | solution.py:30
  23.8 11.8 %collective-permute-start.10 = (bf16[32,16,128]{2,1,0:T(8,128)(2,1)S(1)}, bf16[32,16,128]{2,1,0:T(8,128)(2,1)S(1)}, u32[]{:S(2)}, u32[]{:S(2)}) collective-permute-start(bf16[32,16,128]{2,1,0:T(8,128)(2,1)S(1)} %get-tuple-element.54.refs_3_.refs_5_), channel_id=1, source_target_pairs={{0,1},{2,0},{3,2},{1,3},{4,5},{6,4},{7,6},{5,7},{8,9},{10,8},{11,1... | collective-permute-start | bytes 393224 | tf_op jit(solution)/shard_map/ppermute | solution.py:30
  29.3 9.3 %collective-permute-start.13 = (bf16[32,16,128]{2,1,0:T(8,128)(2,1)S(1)}, bf16[32,16,128]{2,1,0:T(8,128)(2,1)S(1)}, u32[]{:S(2)}, u32[]{:S(2)}) collective-permute-start(bf16[32,16,128]{2,1,0:T(8,128)(2,1)S(1)} %get-tuple-element.51.refs_9_), channel_id=1, source_target_pairs={{0,1},{2,0},{3,2},{1,3},{4,5},{6,4},{7,6},{5,7},{8,9},{10,8},{11,1... | collective-permute-start | bytes 393224 | tf_op jit(solution)/shard_map/ppermute | solution.py:30
  32.6 8.7 %collective-permute-start.12 = (bf16[32,16,128]{2,1,0:T(8,128)(2,1)S(1)}, bf16[32,16,128]{2,1,0:T(8,128)(2,1)S(1)}, u32[]{:S(2)}, u32[]{:S(2)}) collective-permute-start(bf16[32,16,128]{2,1,0:T(8,128)(2,1)S(1)} %get-tuple-element.51.refs_9_), channel_id=1, source_target_pairs={{0,2},{2,3},{3,1},{1,0},{4,6},{6,7},{7,5},{5,4},{8,10},{10,11},{11... | collective-permute-start | bytes 393224 | tf_op jit(solution)/shard_map/ppermute | solution.py:30
  32.7 20.7 %collective-permute-start.8 = (bf16[64,16,128]{2,1,0:T(8,128)(2,1)S(1)}, bf16[64,16,128]{2,1,0:T(8,128)(2,1)S(1)}, u32[]{:S(2)}, u32[]{:S(2)}) collective-permute-start(bf16[64,16,128]{2,1,0:T(8,128)(2,1)S(1)} %pad_maximum_fusion.1), channel_id=1, source_target_pairs={{0,28},{4,0},{8,4},{12,8},{16,12},{20,16},{24,20},{28,24},{1,29},{... | collective-permute-start | bytes 786440 | tf_op jit(solution)/shard_map/ppermute | solution.py:30
  35.6 10.9 %collective-permute-start.15 = (bf16[32,16,128]{2,1,0:T(8,128)(2,1)S(1)}, bf16[32,16,128]{2,1,0:T(8,128)(2,1)S(1)}, u32[]{:S(2)}, u32[]{:S(2)}) collective-permute-start(bf16[32,16,128]{2,1,0:T(8,128)(2,1)S(1)} %collective-permute-done.9.refs_4_.refs_6_), channel_id=1, source_target_pairs={{0,2},{2,3},{3,1},{1,0},{4,6},{6,7},{7,5},{5,4},{8,10},{10,11},{11... | collective-permute-start | bytes 393224 | tf_op jit(solution)/shard_map/ppermute | solution.py:30
  36.9 16.5 %collective-permute-start.11 = (bf16[64,16,128]{2,1,0:T(8,128)(2,1)S(1)}, bf16[64,16,128]{2,1,0:T(8,128)(2,1)S(1)}, u32[]{:S(2)}, u32[]{:S(2)}) collective-permute-start(bf16[64,16,128]{2,1,0:T(8,128)(2,1)S(1)} %pad_maximum_fusion.2), channel_id=1, source_target_pairs={{0,28},{4,0},{8,4},{12,8},{16,12},{20,16},{24,20},{28,24},{1,29},{... | collective-permute-start | bytes 786440 | tf_op jit(solution)/shard_map/ppermute | solution.py:30
  38.6 8.0 %collective-permute-start.17 = (bf16[32,16,128]{2,1,0:T(8,128)(2,1)S(1)}, bf16[32,16,128]{2,1,0:T(8,128)(2,1)S(1)}, u32[]{:S(2)}, u32[]{:S(2)}) collective-permute-start(bf16[32,16,128]{2,1,0:T(8,128)(2,1)S(1)} %collective-permute-done.13.refs_12_), channel_id=1, source_target_pairs={{0,1},{2,0},{3,2},{1,3},{4,5},{6,4},{7,6},{5,7},{8,9},{10,8},{11,1... | collective-permute-start | bytes 393224 | tf_op jit(solution)/shard_map/ppermute | solution.py:30
  41.4 13.4 %collective-permute-start.14 = (bf16[64,16,128]{2,1,0:T(8,128)(2,1)S(1)}, bf16[64,16,128]{2,1,0:T(8,128)(2,1)S(1)}, u32[]{:S(2)}, u32[]{:S(2)}) collective-permute-start(bf16[64,16,128]{2,1,0:T(8,128)(2,1)S(1)} %pad_maximum_fusion.3), channel_id=1, source_target_pairs={{0,28},{4,0},{8,4},{12,8},{16,12},{20,16},{24,20},{28,24},{1,29},{... | collective-permute-start | bytes 786440 | tf_op jit(solution)/shard_map/ppermute | solution.py:30
  46.5 6.9 %collective-permute-start.16 = (bf16[32,16,128]{2,1,0:T(8,128)(2,1)S(1)}, bf16[32,16,128]{2,1,0:T(8,128)(2,1)S(1)}, u32[]{:S(2)}, u32[]{:S(2)}) collective-permute-start(bf16[32,16,128]{2,1,0:T(8,128)(2,1)S(1)} %collective-permute-done.15.refs_5_.refs_7_), channel_id=1, source_target_pairs={{0,28},{4,0},{8,4},{12,8},{16,12},{20,16},{24,20},{28,24},{1,29},{... | collective-permute-start | bytes 393224 | tf_op jit(solution)/shard_map/ppermute | solution.py:30
  46.6 8.2 %collective-permute-start.18 = (bf16[32,16,128]{2,1,0:T(8,128)(2,1)S(1)}, bf16[32,16,128]{2,1,0:T(8,128)(2,1)S(1)}, u32[]{:S(2)}, u32[]{:S(2)}) collective-permute-start(bf16[32,16,128]{2,1,0:T(8,128)(2,1)S(1)} %collective-permute-done.17.refs_11_), channel_id=1, source_target_pairs={{0,28},{4,0},{8,4},{12,8},{16,12},{20,16},{24,20},{28,24},{1,29},{... | collective-permute-start | bytes 393224 | tf_op jit(solution)/shard_map/ppermute | solution.py:30

commit v7 on v6

--- a/solution.py
+++ b/solution.py
@@ -113,18 +113,16 @@
         blocks += [(rows_of(halo_refs[0], (), 0), 0, 8, 1 + 8 * upper)]
     fill_taps(blocks, chans, span_z, taps_ref, 0)
     weights = weight_ref[...]
-    count, rows, _ = part_refs[0].shape
+    rows = part_refs[0].shape[0]
+    count = part_refs[0].shape[1] // half_z
     width = 8 * half_z
     base = part * (acc_ref.shape[1] - count * half_z)
     for step in range(count // 8):
         lane = step * width
         sums = acc_ref[:, base + lane : base + lane + width]
         sums = (sums + tap_sums(weights, taps_ref, lane, width, half_z)).astype(BF16)
-        for j in range(8):
-            for peer, ref in enumerate(part_refs):
-                ref[step * 8 + j] = sums[
-                    peer * rows : (peer + 1) * rows, j * half_z : (j + 1) * half_z
-                ]
+        for peer, ref in enumerate(part_refs):
+            ref[:, lane : lane + width] = sums[peer * rows : (peer + 1) * rows]
 
 
 def add_kernel(one_ref, two_ref, sum_ref):
@@ -143,15 +141,13 @@
     masked_ref[...] = (cot_ref[...].astype(F32) * (0.3 + 0.7 * gate)).astype(BF16)
 
 
-def grad_blocks(held_ref, weights, blocks, chans, span_z, store):
+def grad_blocks(here, after, weights, blocks, chans, span_z, store):
     half_z = span_z // 2
     size = chans * ROWS
     swap = one_hot((size, size), lambda r, c: c == (r % ROWS) * chans + r // ROWS)
     weave = one_hot((span_z, span_z), lambda m, z: z == 2 * (m % half_z) + m // half_z)
     pair = 2 * chans
-    width = blocks * 8 * half_z
-    here, after = held_ref[:, :width], held_ref[:, half_z : half_z + width]
-    sums = dot(weights, jnp.concatenate([here, after], axis=0))
+    sums = dot(weights, jnp.concatenate(here + after, axis=0))
     beside = []
     for step in range(blocks):
         for parity_x in range(2):
@@ -173,39 +169,47 @@
                 store(chan, parity_x, step, woven[first : first + ROWS])
 
 
+def lanes_of(ref, at, first, last):
+    row, lane = at
+    return ref[row : row + ROWS, lane + first : lane + last]
+
+
 def lower_grad_kernel(pieces, *refs):
-    *piece_refs, weight_ref, grad_ref, held_ref = refs
+    *piece_refs, weight_ref, grad_ref = refs
     chans, _, span_y, span_z = grad_ref.shape
     half_z = span_z // 2
-    for index, ((number, first), _) in enumerate(pieces):
-        row = index * ROWS
-        for j in range(span_y // 2 + 1):
-            held_ref[row : row + ROWS, j * half_z : (j + 1) * half_z] = piece_refs[number][first + j]
+    width = span_y // 2 * half_z
+    low = [(piece_refs[number], at) for (number, at), _ in pieces]
+    here = [lanes_of(*piece, 0, width) for piece in low]
+    after = [lanes_of(*piece, half_z, half_z + width) for piece in low]
 
     def store(chan, parity_x, step, values):
         grad_ref[chan, parity_x, step * ROWS : (step + 1) * ROWS, :] = values
 
-    grad_blocks(held_ref, weight_ref[...], span_y // ROWS, chans, span_z, store)
+    grad_blocks(here, after, weight_ref[...], span_y // ROWS, chans, span_z, store)
 
 
 def upper_grad_kernel(pieces, counts, *refs):
-    *piece_refs, weight_ref, lower_ref, grad_ref, held_ref = refs
+    *piece_refs, weight_ref, lower_ref, grad_ref = refs
     chans, _, span_y, span_z = grad_ref.shape
     half_z = span_z // 2
     done = lower_ref.shape[2]
     grad_ref[:, :, :done, :] = lower_ref[...]
-    for index, ((low, low_first), (high, high_first)) in enumerate(pieces):
-        row = index * ROWS
-        tiles = [(low, low_first + j) for j in range(done // 2, counts[0])]
-        tiles += [(high, high_first + j) for j in range(counts[1])] + [(low, low_first)]
-        for place, (number, j) in enumerate(tiles):
-            held_ref[row : row + ROWS, place * half_z : (place + 1) * half_z] = piece_refs[number][j]
+    first, low_end, high_end = done // 2 * half_z, counts[0] * half_z, counts[1] * half_z
+    here, after = [], []
+    for (low, low_at), (high, high_at) in pieces:
+        upper = lanes_of(piece_refs[high], high_at, 0, high_end)
+        low_ref = piece_refs[low]
+        here.append(jnp.concatenate([lanes_of(low_ref, low_at, first, low_end), upper], axis=1))
+        rest = lanes_of(low_ref, low_at, first + half_z, low_end)
+        wrapped = lanes_of(low_ref, low_at, 0, half_z)
+        after.append(jnp.concatenate([rest, upper, wrapped], axis=1))
 
     def store(chan, parity_x, step, values):
-        first = done + step * ROWS
-        grad_ref[chan, parity_x, first : first + ROWS, :] = values
-
-    grad_blocks(held_ref, weight_ref[...], (span_y - done) // ROWS, chans, span_z, store)
+        place = done + step * ROWS
+        grad_ref[chan, parity_x, place : place + ROWS, :] = values
+
+    grad_blocks(here, after, weight_ref[...], (span_y - done) // ROWS, chans, span_z, store)
 
 
 def weights_kernel(peers, me_ref, own_ref, local_ref, halo_ref, back_ref):
@@ -321,7 +325,7 @@
         bytes_accessed=1 << 22,
     )
     halos = [jnp.pad(halo, (fill_c, (0, 0), (0, 0))) for halo in halos]
-    shapes = [jax.ShapeDtypeStruct((count, rows, half_z), BF16) for count in counts]
+    shapes = [jax.ShapeDtypeStruct((rows, count * half_z), BF16) for count in counts]
     parts = []
     for part in range(2):
         if part:
@@ -355,20 +359,20 @@
         joined = call(add_kernel, "add", shapes[h], (relayed[h], parts[h][steps[h]]))
         arrived[h].append(shifted(joined, "col", steps[h]))
 
-    bias_p = jnp.broadcast_to(jnp.pad(bias, fill_o)[None, :, None], (1, rows, half_z))
-    cot = jnp.pad(jnp.transpose(cotangent[:, 0], (1, 0, 2)), ((0, 0), fill_o, (0, 0)))
+    bias_p = [jnp.broadcast_to(jnp.pad(bias, fill_o)[:, None], shape.shape) for shape in shapes]
+    cot = jnp.pad(cotangent.reshape(cout, points), (fill_o, (0, 0)))
     acts = [
         call(
             act_kernel,
             "activation",
             (shapes[h], shapes[h]),
-            (*arrived[h], bias_p, cot[starts[h] : starts[h] + counts[h]]),
+            (*arrived[h], bias_p[h], cot[:, starts[h] * half_z : (starts[h] + counts[h]) * half_z]),
             transcendentals=3 * counts[h] * rows * half_z,
         )
         for h in range(2)
     ]
-    out = jnp.concatenate([out for out, _ in acts], axis=0)
-    out_act = jnp.transpose(out[:, :cout], (1, 0, 2))[:, None]
+    out = jnp.concatenate([out for out, _ in acts], axis=1)
+    out_act = out[:cout].reshape(cout, 1, half_y, half_z)
 
     masked = [masked for _, masked in acts]
     near = [r for r in range(1, peers) if r != far]
@@ -380,19 +384,19 @@
         arrays.append(value)
         return len(arrays) - 1
 
-    whole = place_of(shifted(jnp.concatenate(masked, axis=0), "gx", -1))
+    whole = place_of(shifted(jnp.concatenate(masked, axis=1), "gx", -1))
     for h in range(2):
-        above[h][0] = (whole, starts[h])
+        above[h][0] = (whole, (0, starts[h] * half_z))
     gathered[0] = lax.optimization_barrier(gathered[0])
     for h in range(2):
         joined = jnp.concatenate([gathered[h][r] for r in near], axis=0)
         number = place_of(shifted(joined, "gx", -1))
         for i, r in enumerate(near):
-            above[h][r] = (number, i * counts[h])
+            above[h][r] = (number, (i * rows, 0))
     for h in range(2):
         gathered[h][far] = shifted(gathered[h][steps[h]], "col", steps[h])
-        above[h][far] = (place_of(shifted(gathered[h][far], "gx", -1)), 0)
-    mine = [{r: (place_of(gathered[h][r]), 0) for r in range(peers)} for h in range(2)]
+        above[h][far] = (place_of(shifted(gathered[h][far], "gx", -1)), (0, 0))
+    mine = [{r: (place_of(gathered[h][r]), (0, 0)) for r in range(peers)} for h in range(2)]
     order = [[places[h][r] for h in range(2)] for places in (mine, above) for r in range(peers)]
 
     def grad_call(kernel, name, shape, used, extra, blocks):
@@ -403,9 +407,6 @@
             name,
             shape,
             (*[arrays[n] for n in used], weights_back, *extra),
-            [
-                pltpu.VMEM((2 * total, (1 + 8 * blocks) * half_z), BF16),
-            ],
             flops=8 * total * 12 * chans * 8 * blocks * half_z,
         )
 

time: 57.1 us -> 56.8 us (level)
  no operation moved by 1% of the time
where the time goes in v7:
time: 56.8 us; the launch traced here: 56.7 us
  starting transfers between devices  31.1 us (55%)
  waiting for transfers between devices  15.3 us (27%)
  Pallas kernels  6.33 us (11%)
  local copies, waits for them, and re-layouts  2.25 us (4%)
  other arithmetic  0.92 us (2%)
  between operations  0.81 us (1%)
    ppermute x19, starting transfers between devices, shifted(): lax.ppermute(block, axis, [(ring[i], ring[(i + distance) % count]) for i...  31.1 us
    ppermute x19, waiting for transfers between devices, shifted(): lax.ppermute(block, axis, [(ring[i], ring[(i + distance) % count]) for i...  15.3 us
    pallas_call x9, Pallas kernels, call(): pl.pallas_call(kernel, out_shape=out_shape, scratch_shapes=list(scratch),...  6.1 us
    squeeze x1, local copies, waits for them, and re-layouts, on_device(): plane = lax.optimization_barrier(field[:, planes - 1])  1.17 us
  transfers between devices with their start and end apart: 19, of which 9 were waited for; matrix products, arithmetic and copies ran while one was open for 3% of the time, Pallas kernels for 8%

profile of v7, /device:TPU:11, one launch (start us, length us, event | category | flops | bytes accessed | tf_op | source)
XLA Modules:
  0.0 56.7 jit_solution(14580378799489628093)
XLA Ops:
  0.6 1.2 %slice_bitcast_fusion = bf16[8,128,256]{2,1,0:T(8,128)(2,1)S(1)} fusion(bf16[8,2,128,256]{3,2,1,0:T(8,128)(2,1)} %field_ref.1), kind=kLoop, calls=%fused_computation | loop fusion | bytes 1048576 | tf_op jit(solution)/shard_map/squeeze | solution.py:288
  1.9 1.8 %collective-permute-start = (bf16[8,80,256]{2,1,0:T(8,128)(2,1)S(1)}, bf16[8,80,256]{2,1,0:T(8,128)(2,1)S(1)}, u32[]{:S(2)}, u32[]{:S(2)}) collective-permute-start(bf16[8,80,256]{2,1,0:T(8,128)(2,1)S(1)} %pad_maximum_fusion), channel_id=1, source_target_pairs={{0,4},{4,8},{8,12},{12,16},{16,20},{20,24},{24,28},{28,0},{1,5},{5... | collective-permute-start | bytes 983048 | tf_op jit(solution)/shard_map/ppermute | solution.py:30
  3.7 0.1 collective-permute-start.2
  3.8 0.8 %dynamic-slice_convert_fusion = f32[64,8,3,3,3]{0,1,4,3,2:T(8,128)S(1)} fusion(bf16[64,32,3,3,3]{0,1,4,3,2:T(8,128)(2,1)} %param.5, s32[]{:T(128)S(6)} %select_n.3), kind=kLoop, calls=%fused_computation.7 | loop fusion | flops 13824 | bytes 82948 | tf_op jit(solution)/shard_map/convert_element_type | solution.py:300
  4.6 0.2 weights.1
  4.9 1.5 %local_planes.1.refs_2_.refs_3_ = f32[64,8192]{1,0:T(8,128)S(1)} custom-call(bf16[8,2,128,256]{3,2,1,0:T(8,128)(2,1)S(1)} %copy-done, bf16[64,192]{1,0:T(8,128)(2,1)S(1)} %get-tuple-element.30.weight_ref), custom_call_target="tpu_custom_call" | custom-call | flops 201326592 | bytes 4194304 | tf_op jit(solution)/shard_map/local_planes/pallas_call | solution.py:265
  6.4 1.3 %collective-permute-done.refs_0_ = bf16[8,80,256]{2,1,0:T(8,128)(2,1)S(1)} collective-permute-done((bf16[8,80,256]{2,1,0:T(8,128)(2,1)S(1)}, bf16[8,80,256]{2,1,0:T(8,128)(2,1)S(1)}, u32[]{:S(2)}, u32[]{:S(2)}) %collective-permute-start) | collective-permute-done | bytes 327712 | tf_op jit(solution)/shard_map/ppermute | solution.py:30
  7.7 0.6 %halo_plane.2 = (bf16[16,4096]{1,0:T(8,128)(2,1)S(1)}, bf16[16,4096]{1,0:T(8,128)(2,1)S(1)}, bf16[16,4096]{1,0:T(8,128)(2,1)S(1)}, bf16[16,4096]{1,0:T(8,128)(2,1)S(1)}) custom-call(bf16[8,80,256]{2,1,0:T(8,128)(2,1)S(1)} %collective-permute-done.refs_0_, bf16[64,96]{1,0:T(8,128)(2,1)S(1)} %get-tuple-element.37.refs_1_.refs_2_, ...), custom_call_target="tpu_custom_call" | custom-call | flops 50331648 | bytes 2097152 | tf_op jit(solution)/shard_map/halo_plane/pallas_call | solution.py:265
  8.4 0.0 copy-start.1
  8.4 0.0 copy-start.2
  8.4 0.2 collective-permute-start.4
  8.6 1.2 %collective-permute-done.2.refs_1_ = bf16[8,48,256]{2,1,0:T(8,128)(2,1)S(1)} collective-permute-done((bf16[8,48,256]{2,1,0:T(8,128)(2,1)S(1)}, bf16[8,48,256]{2,1,0:T(8,128)(2,1)S(1)}, u32[]{:S(2)}, u32[]{:S(2)}) %collective-permute-start.2) | collective-permute-done | bytes 196640 | tf_op jit(solution)/shard_map/ppermute | solution.py:30
  9.8 0.6 %halo_plane.3 = (bf16[16,4096]{1,0:T(8,128)(2,1)S(1)}, bf16[16,4096]{1,0:T(8,128)(2,1)S(1)}, bf16[16,4096]{1,0:T(8,128)(2,1)S(1)}, bf16[16,4096]{1,0:T(8,128)(2,1)S(1)}) custom-call(bf16[8,80,256]{2,1,0:T(8,128)(2,1)S(1)} %collective-permute-done.refs_0_, bf16[8,48,256]{2,1,0:T(8,128)(2,1)S(1)} %collective-permute-done.2.refs_1_, ...), custom_call_target="tpu_custom_call" | custom-call | flops 50331648 | bytes 2097152 | tf_op jit(solution)/shard_map/halo_plane/pallas_call | solution.py:265
  10.5 2.4 %collective-permute-start.3 = (bf16[16,4096]{1,0:T(8,128)(2,1)S(1)}, bf16[16,4096]{1,0:T(8,128)(2,1)S(1)}, u32[]{:S(2)}, u32[]{:S(2)}) collective-permute-start(bf16[16,4096]{1,0:T(8,128)(2,1)S(1)} %get-tuple-element.38), channel_id=1, source_target_pairs={{0,1},{2,0},{3,2},{1,3},{4,5},{6,4},{7,6},{5,7},{8,9},{10,8},{11,1... | collective-permute-start | bytes 393224 | tf_op jit(solution)/shard_map/ppermute | solution.py:30
  12.8 0.3 collective-permute-done.4.one_ref
  13.2 0.1 collective-permute-start.5
  13.3 0.2 copy.12
  13.5 2.4 %collective-permute-start.1 = (bf16[16,4096]{1,0:T(8,128)(2,1)S(1)}, bf16[16,4096]{1,0:T(8,128)(2,1)S(1)}, u32[]{:S(2)}, u32[]{:S(2)}) collective-permute-start(bf16[16,4096]{1,0:T(8,128)(2,1)S(1)} %get-tuple-element.36), channel_id=1, source_target_pairs={{0,1},{2,0},{3,2},{1,3},{4,5},{6,4},{7,6},{5,7},{8,9},{10,8},{11,1... | collective-permute-start | bytes 393224 | tf_op jit(solution)/shard_map/ppermute | solution.py:30
  15.9 0.2 collective-permute-start.6
  16.1 0.4 collective-permute-done.3.one_ref
  16.5 2.9 %collective-permute-done.5.refs_2_ = bf16[16,4096]{1,0:T(8,128)(2,1)S(1)} collective-permute-done((bf16[16,4096]{1,0:T(8,128)(2,1)S(1)}, bf16[16,4096]{1,0:T(8,128)(2,1)S(1)}, u32[]{:S(2)}, u32[]{:S(2)}) %collective-permute-start.5) | collective-permute-done | bytes 131104 | tf_op jit(solution)/shard_map/ppermute | solution.py:30
  19.4 1.1 %collective-permute-start.7 = (bf16[16,4096]{1,0:T(8,128)(2,1)S(1)}, bf16[16,4096]{1,0:T(8,128)(2,1)S(1)}, u32[]{:S(2)}, u32[]{:S(2)}) collective-permute-start(bf16[16,4096]{1,0:T(8,128)(2,1)S(1)} %add.7), channel_id=1, source_target_pairs={{0,1},{2,0},{3,2},{1,3},{4,5},{6,4},{7,6},{5,7},{8,9},{10,8},{11,1... | collective-permute-start | bytes 393224 | tf_op jit(solution)/shard_map/ppermute | solution.py:30
  20.4 3.0 %collective-permute-done.1.refs_1_ = bf16[16,4096]{1,0:T(8,128)(2,1)S(1)} collective-permute-done((bf16[16,4096]{1,0:T(8,128)(2,1)S(1)}, bf16[16,4096]{1,0:T(8,128)(2,1)S(1)}, u32[]{:S(2)}, u32[]{:S(2)}) %collective-permute-start.1) | collective-permute-done | bytes 131104 | tf_op jit(solution)/shard_map/ppermute | solution.py:30
  23.4 0.1 broadcast_in_dim.2.refs_3_
  23.5 0.2 activation.2
  23.8 0.1 collective-permute-start.9
  23.8 3.3 %collective-permute-start.10 = (bf16[16,4096]{1,0:T(8,128)(2,1)S(1)}, bf16[16,4096]{1,0:T(8,128)(2,1)S(1)}, u32[]{:S(2)}, u32[]{:S(2)}) collective-permute-start(bf16[16,4096]{1,0:T(8,128)(2,1)S(1)} %get-tuple-element.54.refs_3_.refs_5_), channel_id=1, source_target_pairs={{0,1},{2,0},{3,2},{1,3},{4,5},{6,4},{7,6},{5,7},{8,9},{10,8},{11,1... | collective-permute-start | bytes 393224 | tf_op jit(solution)/shard_map/ppermute | solution.py:30
  27.1 0.0 collective-permute-done.6.refs_1_
  27.1 2.0 %collective-permute-done.7.refs_2_ = bf16[16,4096]{1,0:T(8,128)(2,1)S(1)} collective-permute-done((bf16[16,4096]{1,0:T(8,128)(2,1)S(1)}, bf16[16,4096]{1,0:T(8,128)(2,1)S(1)}, u32[]{:S(2)}, u32[]{:S(2)}) %collective-permute-start.7) | collective-permute-done | bytes 131104 | tf_op jit(solution)/shard_map/ppermute | solution.py:30
  29.1 0.2 activation.3
  29.3 3.3 %collective-permute-start.13 = (bf16[16,4096]{1,0:T(8,128)(2,1)S(1)}, bf16[16,4096]{1,0:T(8,128)(2,1)S(1)}, u32[]{:S(2)}, u32[]{:S(2)}) collective-permute-start(bf16[16,4096]{1,0:T(8,128)(2,1)S(1)} %get-tuple-element.51.refs_9_), channel_id=1, source_target_pairs={{0,1},{2,0},{3,2},{1,3},{4,5},{6,4},{7,6},{5,7},{8,9},{10,8},{11,1... | collective-permute-start | bytes 393224 | tf_op jit(solution)/shard_map/ppermute | solution.py:30
  32.6 0.0 collective-permute-start.12
  32.6 2.9 %collective-permute-start.8 = (bf16[16,8192]{1,0:T(8,128)(2,1)S(1)}, bf16[16,8192]{1,0:T(8,128)(2,1)S(1)}, u32[]{:S(2)}, u32[]{:S(2)}) collective-permute-start(bf16[16,8192]{1,0:T(8,128)(2,1)S(1)} %pad_maximum_fusion.1), channel_id=1, source_target_pairs={{0,28},{4,0},{8,4},{12,8},{16,12},{20,16},{24,20},{28,24},{1,29},{... | collective-permute-start | bytes 786440 | tf_op jit(solution)/shard_map/ppermute | solution.py:30
  35.6 0.0 collective-permute-done.10.refs_6_.refs_8_
  35.6 1.2 %collective-permute-start.15 = (bf16[16,4096]{1,0:T(8,128)(2,1)S(1)}, bf16[16,4096]{1,0:T(8,128)(2,1)S(1)}, u32[]{:S(2)}, u32[]{:S(2)}) collective-permute-start(bf16[16,4096]{1,0:T(8,128)(2,1)S(1)} %collective-permute-done.9.refs_4_.refs_6_), channel_id=1, source_target_pairs={{0,2},{2,3},{3,1},{1,0},{4,6},{6,7},{7,5},{5,4},{8,10},{10,11},{11... | collective-permute-start | bytes 393224 | tf_op jit(solution)/shard_map/ppermute | solution.py:30
  36.8 1.8 %collective-permute-start.11 = (bf16[32,4096]{1,0:T(8,128)(2,1)S(1)}, bf16[32,4096]{1,0:T(8,128)(2,1)S(1)}, u32[]{:S(2)}, u32[]{:S(2)}) collective-permute-start(bf16[32,4096]{1,0:T(8,128)(2,1)S(1)} %pad_maximum_fusion.2), channel_id=1, source_target_pairs={{0,28},{4,0},{8,4},{12,8},{16,12},{20,16},{24,20},{28,24},{1,29},{... | collective-permute-start | bytes 786440 | tf_op jit(solution)/shard_map/ppermute | solution.py:30
  38.6 2.8 %collective-permute-start.17 = (bf16[16,4096]{1,0:T(8,128)(2,1)S(1)}, bf16[16,4096]{1,0:T(8,128)(2,1)S(1)}, u32[]{:S(2)}, u32[]{:S(2)}) collective-permute-start(bf16[16,4096]{1,0:T(8,128)(2,1)S(1)} %collective-permute-done.13.refs_12_), channel_id=1, source_target_pairs={{0,1},{2,0},{3,2},{1,3},{4,5},{6,4},{7,6},{5,7},{8,9},{10,8},{11,1... | collective-permute-start | bytes 393224 | tf_op jit(solution)/shard_map/ppermute | solution.py:30
  41.4 0.0 collective-permute-done.12.refs_10_
  41.4 5.1 %collective-permute-start.14 = (bf16[32,4096]{1,0:T(8,128)(2,1)S(1)}, bf16[32,4096]{1,0:T(8,128)(2,1)S(1)}, u32[]{:S(2)}, u32[]{:S(2)}) collective-permute-start(bf16[32,4096]{1,0:T(8,128)(2,1)S(1)} %pad_maximum_fusion.3), channel_id=1, source_target_pairs={{0,28},{4,0},{8,4},{12,8},{16,12},{20,16},{24,20},{28,24},{1,29},{... | collective-permute-start | bytes 786440 | tf_op jit(solution)/shard_map/ppermute | solution.py:30
  46.5 0.0 collective-permute-done.15.refs_5_.refs_7_
  46.5 0.1 collective-permute-start.16
  46.6 0.0 collective-permute-done.17.refs_11_
  46.6 2.4 %collective-permute-start.18 = (bf16[16,4096]{1,0:T(8,128)(2,1)S(1)}, bf16[16,4096]{1,0:T(8,128)(2,1)S(1)}, u32[]{:S(2)}, u32[]{:S(2)}) collective-permute-start(bf16[16,4096]{1,0:T(8,128)(2,1)S(1)} %collective-permute-done.17.refs_11_), channel_id=1, source_target_pairs={{0,28},{4,0},{8,4},{12,8},{16,12},{20,16},{24,20},{28,24},{1,29},{... | collective-permute-start | bytes 393224 | tf_op jit(solution)/shard_map/ppermute | solution.py:30
  48.9 0.8 %copy.10 = bf16[2,8,64,128]{3,2,1,0:T(8,128)(2,1)} copy(bf16[2,8,64,128]{3,1,2,0:T(8,128)(2,1)S(1)} %maximum_bitcast_fusion) | data formatting | bytes 524288
  49.7 3.6 %collective-permute-done.16.refs_2_.refs_3_ = bf16[16,4096]{1,0:T(8,128)(2,1)S(1)} collective-permute-done((bf16[16,4096]{1,0:T(8,128)(2,1)S(1)}, bf16[16,4096]{1,0:T(8,128)(2,1)S(1)}, u32[]{:S(2)}, u32[]{:S(2)}) %collective-permute-start.16) | collective-permute-done | bytes 131104 | tf_op jit(solution)/shard_map/ppermute | solution.py:30
  53.3 0.8 %lower_grad.1.refs_14_ = bf16[8,2,48,256]{3,2,1,0:T(8,128)(2,1)S(1)} custom-call(bf16[16,8192]{1,0:T(8,128)(2,1)S(1)} %collective-permute-done.8.refs_0_, bf16[32,4096]{1,0:T(8,128)(2,1)S(1)} %collective-permute-done.11.refs_1_, bf16[16,4096]{1,0:T(8,128)(2,1)S(1)} %collective-permute-done.16.refs_2_.refs_3_, ...), custom_call_target="tpu_custom_call" | custom-call | flops 150994944 | bytes 1048576 | tf_op jit(solution)/shard_map/lower_grad/pallas_call | solution.py:265
  54.1 0.6 %collective-permute-done.18.refs_4_ = bf16[16,4096]{1,0:T(8,128)(2,1)S(1)} collective-permute-done((bf16[16,4096]{1,0:T(8,128)(2,1)S(1)}, bf16[16,4096]{1,0:T(8,128)(2,1)S(1)}, u32[]{:S(2)}, u32[]{:S(2)}) %collective-permute-start.18) | collective-permute-done | bytes 131104 | tf_op jit(solution)/shard_map/ppermute | solution.py:30
  54.7 2.0 %upper_grad.1 = bf16[8,2,128,256]{3,2,1,0:T(8,128)(2,1)} custom-call(bf16[16,8192]{1,0:T(8,128)(2,1)S(1)} %collective-permute-done.8.refs_0_, bf16[32,4096]{1,0:T(8,128)(2,1)S(1)} %collective-permute-done.11.refs_1_, bf16[32,4096]{1,0:T(8,128)(2,1)S(1)} %collective-permute-done.14.refs_2_, bf16[16,4096]{1,0:T(8,128)(2,1)S(1)} %collective-permute-done.16.refs_2_.refs_3_, ...), custom_call_target="tpu_custom_call" | custom-call | flops 251658240 | bytes 1048576 | tf_op jit(solution)/shard_map/upper_grad/pallas_call | solution.py:265
  (20 shorter events, 0.2 us)
Async XLA Ops:
  0.6 4.2 %copy-start = (bf16[8,2,128,256]{3,2,1,0:T(8,128)(2,1)S(1)}, bf16[8,2,128,256]{3,2,1,0:T(8,128)(2,1)}, u32[]{:S(2)}) copy-start(bf16[8,2,128,256]{3,2,1,0:T(8,128)(2,1)} %field_ref.1) | copy-start | bytes 3145732
  1.9 5.8 %collective-permute-start = (bf16[8,80,256]{2,1,0:T(8,128)(2,1)S(1)}, bf16[8,80,256]{2,1,0:T(8,128)(2,1)S(1)}, u32[]{:S(2)}, u32[]{:S(2)}) collective-permute-start(bf16[8,80,256]{2,1,0:T(8,128)(2,1)S(1)} %pad_maximum_fusion), channel_id=1, source_target_pairs={{0,4},{4,8},{8,12},{12,16},{16,20},{20,24},{24,28},{28,0},{1,5},{5... | collective-permute-start | bytes 983048 | tf_op jit(solution)/shard_map/ppermute | solution.py:30
  3.7 6.1 %collective-permute-start.2 = (bf16[8,48,256]{2,1,0:T(8,128)(2,1)S(1)}, bf16[8,48,256]{2,1,0:T(8,128)(2,1)S(1)}, u32[]{:S(2)}, u32[]{:S(2)}) collective-permute-start(bf16[8,48,256]{2,1,0:T(8,128)(2,1)S(1)} %slice.26), channel_id=1, source_target_pairs={{0,4},{4,8},{8,12},{12,16},{16,20},{20,24},{24,28},{28,0},{1,5},{5... | collective-permute-start | bytes 589832 | tf_op jit(solution)/shard_map/ppermute | solution.py:30
  8.4 4.9 %copy-start.1 = (bf16[16,1,64,128]{3,2,1,0:T(8,128)(2,1)S(1)}, bf16[16,1,64,128]{3,2,1,0:T(8,128)(2,1)}, u32[]{:S(2)}) copy-start(bf16[16,1,64,128]{3,2,1,0:T(8,128)(2,1)} %param.7) | copy-start | bytes 786436
  8.4 15.0 %copy-start.2 = (f32[16]{0:T(128)S(1)}, f32[16]{0:T(128)}, u32[]{:S(2)}) copy-start(f32[16]{0:T(128)} %param.6) | copy-start | bytes 196
  8.4 4.8 %collective-permute-start.4 = (bf16[16,4096]{1,0:T(8,128)(2,1)S(1)}, bf16[16,4096]{1,0:T(8,128)(2,1)S(1)}, u32[]{:S(2)}, u32[]{:S(2)}) collective-permute-start(bf16[16,4096]{1,0:T(8,128)(2,1)S(1)} %get-tuple-element.40), channel_id=1, source_target_pairs={{0,2},{2,3},{3,1},{1,0},{4,6},{6,7},{7,5},{5,4},{8,10},{10,11},{11... | collective-permute-start | bytes 393224 | tf_op jit(solution)/shard_map/ppermute | solution.py:30
  10.5 6.0 %collective-permute-start.3 = (bf16[16,4096]{1,0:T(8,128)(2,1)S(1)}, bf16[16,4096]{1,0:T(8,128)(2,1)S(1)}, u32[]{:S(2)}, u32[]{:S(2)}) collective-permute-start(bf16[16,4096]{1,0:T(8,128)(2,1)S(1)} %get-tuple-element.38), channel_id=1, source_target_pairs={{0,1},{2,0},{3,2},{1,3},{4,5},{6,4},{7,6},{5,7},{8,9},{10,8},{11,1... | collective-permute-start | bytes 393224 | tf_op jit(solution)/shard_map/ppermute | solution.py:30
  13.2 6.1 %collective-permute-start.5 = (bf16[16,4096]{1,0:T(8,128)(2,1)S(1)}, bf16[16,4096]{1,0:T(8,128)(2,1)S(1)}, u32[]{:S(2)}, u32[]{:S(2)}) collective-permute-start(bf16[16,4096]{1,0:T(8,128)(2,1)S(1)} %add.6), channel_id=1, source_target_pairs={{0,2},{2,3},{3,1},{1,0},{4,6},{6,7},{7,5},{5,4},{8,10},{10,11},{11... | collective-permute-start | bytes 393224 | tf_op jit(solution)/shard_map/ppermute | solution.py:30
  13.5 10.0 %collective-permute-start.1 = (bf16[16,4096]{1,0:T(8,128)(2,1)S(1)}, bf16[16,4096]{1,0:T(8,128)(2,1)S(1)}, u32[]{:S(2)}, u32[]{:S(2)}) collective-permute-start(bf16[16,4096]{1,0:T(8,128)(2,1)S(1)} %get-tuple-element.36), channel_id=1, source_target_pairs={{0,1},{2,0},{3,2},{1,3},{4,5},{6,4},{7,6},{5,7},{8,9},{10,8},{11,1... | collective-permute-start | bytes 393224 | tf_op jit(solution)/shard_map/ppermute | solution.py:30
  15.9 11.3 %collective-permute-start.6 = (bf16[16,4096]{1,0:T(8,128)(2,1)S(1)}, bf16[16,4096]{1,0:T(8,128)(2,1)S(1)}, u32[]{:S(2)}, u32[]{:S(2)}) collective-permute-start(bf16[16,4096]{1,0:T(8,128)(2,1)S(1)} %get-tuple-element.46), channel_id=1, source_target_pairs={{0,2},{2,3},{3,1},{1,0},{4,6},{6,7},{7,5},{5,4},{8,10},{10,11},{11... | collective-permute-start | bytes 393224 | tf_op jit(solution)/shard_map/ppermute | solution.py:30
  19.4 9.7 %collective-permute-start.7 = (bf16[16,4096]{1,0:T(8,128)(2,1)S(1)}, bf16[16,4096]{1,0:T(8,128)(2,1)S(1)}, u32[]{:S(2)}, u32[]{:S(2)}) collective-permute-start(bf16[16,4096]{1,0:T(8,128)(2,1)S(1)} %add.7), channel_id=1, source_target_pairs={{0,1},{2,0},{3,2},{1,3},{4,5},{6,4},{7,6},{5,7},{8,9},{10,8},{11,1... | collective-permute-start | bytes 393224 | tf_op jit(solution)/shard_map/ppermute | solution.py:30
  23.8 11.8 %collective-permute-start.9 = (bf16[16,4096]{1,0:T(8,128)(2,1)S(1)}, bf16[16,4096]{1,0:T(8,128)(2,1)S(1)}, u32[]{:S(2)}, u32[]{:S(2)}) collective-permute-start(bf16[16,4096]{1,0:T(8,128)(2,1)S(1)} %get-tuple-element.54.refs_3_.refs_5_), channel_id=1, source_target_pairs={{0,2},{2,3},{3,1},{1,0},{4,6},{6,7},{7,5},{5,4},{8,10},{10,11},{11... | collective-permute-start | bytes 393224 | tf_op jit(solution)/shard_map/ppermute | solution.py:30
  23.8 11.8 %collective-permute-start.10 = (bf16[16,4096]{1,0:T(8,128)(2,1)S(1)}, bf16[16,4096]{1,0:T(8,128)(2,1)S(1)}, u32[]{:S(2)}, u32[]{:S(2)}) collective-permute-start(bf16[16,4096]{1,0:T(8,128)(2,1)S(1)} %get-tuple-element.54.refs_3_.refs_5_), channel_id=1, source_target_pairs={{0,1},{2,0},{3,2},{1,3},{4,5},{6,4},{7,6},{5,7},{8,9},{10,8},{11,1... | collective-permute-start | bytes 393224 | tf_op jit(solution)/shard_map/ppermute | solution.py:30
  29.3 9.3 %collective-permute-start.13 = (bf16[16,4096]{1,0:T(8,128)(2,1)S(1)}, bf16[16,4096]{1,0:T(8,128)(2,1)S(1)}, u32[]{:S(2)}, u32[]{:S(2)}) collective-permute-start(bf16[16,4096]{1,0:T(8,128)(2,1)S(1)} %get-tuple-element.51.refs_9_), channel_id=1, source_target_pairs={{0,1},{2,0},{3,2},{1,3},{4,5},{6,4},{7,6},{5,7},{8,9},{10,8},{11,1... | collective-permute-start | bytes 393224 | tf_op jit(solution)/shard_map/ppermute | solution.py:30
  32.6 8.7 %collective-permute-start.12 = (bf16[16,4096]{1,0:T(8,128)(2,1)S(1)}, bf16[16,4096]{1,0:T(8,128)(2,1)S(1)}, u32[]{:S(2)}, u32[]{:S(2)}) collective-permute-start(bf16[16,4096]{1,0:T(8,128)(2,1)S(1)} %get-tuple-element.51.refs_9_), channel_id=1, source_target_pairs={{0,2},{2,3},{3,1},{1,0},{4,6},{6,7},{7,5},{5,4},{8,10},{10,11},{11... | collective-permute-start | bytes 393224 | tf_op jit(solution)/shard_map/ppermute | solution.py:30
  32.6 20.6 %collective-permute-start.8 = (bf16[16,8192]{1,0:T(8,128)(2,1)S(1)}, bf16[16,8192]{1,0:T(8,128)(2,1)S(1)}, u32[]{:S(2)}, u32[]{:S(2)}) collective-permute-start(bf16[16,8192]{1,0:T(8,128)(2,1)S(1)} %pad_maximum_fusion.1), channel_id=1, source_target_pairs={{0,28},{4,0},{8,4},{12,8},{16,12},{20,16},{24,20},{28,24},{1,29},{... | collective-permute-start | bytes 786440 | tf_op jit(solution)/shard_map/ppermute | solution.py:30
  35.6 10.9 %collective-permute-start.15 = (bf16[16,4096]{1,0:T(8,128)(2,1)S(1)}, bf16[16,4096]{1,0:T(8,128)(2,1)S(1)}, u32[]{:S(2)}, u32[]{:S(2)}) collective-permute-start(bf16[16,4096]{1,0:T(8,128)(2,1)S(1)} %collective-permute-done.9.refs_4_.refs_6_), channel_id=1, source_target_pairs={{0,2},{2,3},{3,1},{1,0},{4,6},{6,7},{7,5},{5,4},{8,10},{10,11},{11... | collective-permute-start | bytes 393224 | tf_op jit(solution)/shard_map/ppermute | solution.py:30
  36.8 16.5 %collective-permute-start.11 = (bf16[32,4096]{1,0:T(8,128)(2,1)S(1)}, bf16[32,4096]{1,0:T(8,128)(2,1)S(1)}, u32[]{:S(2)}, u32[]{:S(2)}) collective-permute-start(bf16[32,4096]{1,0:T(8,128)(2,1)S(1)} %pad_maximum_fusion.2), channel_id=1, source_target_pairs={{0,28},{4,0},{8,4},{12,8},{16,12},{20,16},{24,20},{28,24},{1,29},{... | collective-permute-start | bytes 786440 | tf_op jit(solution)/shard_map/ppermute | solution.py:30
  38.6 8.0 %collective-permute-start.17 = (bf16[16,4096]{1,0:T(8,128)(2,1)S(1)}, bf16[16,4096]{1,0:T(8,128)(2,1)S(1)}, u32[]{:S(2)}, u32[]{:S(2)}) collective-permute-start(bf16[16,4096]{1,0:T(8,128)(2,1)S(1)} %collective-permute-done.13.refs_12_), channel_id=1, source_target_pairs={{0,1},{2,0},{3,2},{1,3},{4,5},{6,4},{7,6},{5,7},{8,9},{10,8},{11,1... | collective-permute-start | bytes 393224 | tf_op jit(solution)/shard_map/ppermute | solution.py:30
  41.4 13.3 %collective-permute-start.14 = (bf16[32,4096]{1,0:T(8,128)(2,1)S(1)}, bf16[32,4096]{1,0:T(8,128)(2,1)S(1)}, u32[]{:S(2)}, u32[]{:S(2)}) collective-permute-start(bf16[32,4096]{1,0:T(8,128)(2,1)S(1)} %pad_maximum_fusion.3), channel_id=1, source_target_pairs={{0,28},{4,0},{8,4},{12,8},{16,12},{20,16},{24,20},{28,24},{1,29},{... | collective-permute-start | bytes 786440 | tf_op jit(solution)/shard_map/ppermute | solution.py:30
  46.5 6.8 %collective-permute-start.16 = (bf16[16,4096]{1,0:T(8,128)(2,1)S(1)}, bf16[16,4096]{1,0:T(8,128)(2,1)S(1)}, u32[]{:S(2)}, u32[]{:S(2)}) collective-permute-start(bf16[16,4096]{1,0:T(8,128)(2,1)S(1)} %collective-permute-done.15.refs_5_.refs_7_), channel_id=1, source_target_pairs={{0,28},{4,0},{8,4},{12,8},{16,12},{20,16},{24,20},{28,24},{1,29},{... | collective-permute-start | bytes 393224 | tf_op jit(solution)/shard_map/ppermute | solution.py:30
  46.6 8.1 %collective-permute-start.18 = (bf16[16,4096]{1,0:T(8,128)(2,1)S(1)}, bf16[16,4096]{1,0:T(8,128)(2,1)S(1)}, u32[]{:S(2)}, u32[]{:S(2)}) collective-permute-start(bf16[16,4096]{1,0:T(8,128)(2,1)S(1)} %collective-permute-done.17.refs_11_), channel_id=1, source_target_pairs={{0,28},{4,0},{8,4},{12,8},{16,12},{20,16},{24,20},{28,24},{1,29},{... | collective-permute-start | bytes 393224 | tf_op jit(solution)/shard_map/ppermute | solution.py:30

commit v8 on v7

--- a/solution.py
+++ b/solution.py
@@ -190,11 +190,12 @@
 
 
 def upper_grad_kernel(pieces, counts, *refs):
-    *piece_refs, weight_ref, lower_ref, grad_ref = refs
+    *piece_refs, weight_ref, lower_ref, grad_ref, stage_ref, sems = refs
     chans, _, span_y, span_z = grad_ref.shape
     half_z = span_z // 2
     done = lower_ref.shape[2]
-    grad_ref[:, :, :done, :] = lower_ref[...]
+    lower_copy = pltpu.make_async_copy(lower_ref, grad_ref.at[:, :, pl.ds(0, done)], sems.at[0])
+    lower_copy.start()
     first, low_end, high_end = done // 2 * half_z, counts[0] * half_z, counts[1] * half_z
     here, after = [], []
     for (low, low_at), (high, high_at) in pieces:
@@ -206,10 +207,14 @@
         after.append(jnp.concatenate([rest, upper, wrapped], axis=1))
 
     def store(chan, parity_x, step, values):
-        place = done + step * ROWS
-        grad_ref[chan, parity_x, place : place + ROWS, :] = values
+        stage_ref[chan, parity_x, step * ROWS : (step + 1) * ROWS, :] = values
 
     grad_blocks(here, after, weight_ref[...], (span_y - done) // ROWS, chans, span_z, store)
+    upper_rows = pl.ds(done, span_y - done)
+    upper_copy = pltpu.make_async_copy(stage_ref, grad_ref.at[:, :, upper_rows], sems.at[1])
+    upper_copy.start()
+    lower_copy.wait()
+    upper_copy.wait()
 
 
 def weights_kernel(peers, me_ref, own_ref, local_ref, halo_ref, back_ref):
@@ -419,14 +424,25 @@
         (),
         done // ROWS,
     )
-    in_grad = grad_call(
-        lambda pieces, *refs: upper_grad_kernel(pieces, counts, *refs),
-        "upper_grad",
-        jax.ShapeDtypeStruct((chans, planes, span_y, span_z), BF16),
-        {n for both in order for n, _ in both},
-        (lower,),
-        (span_y - done) // ROWS,
-    )
+    used = sorted({n for both in order for n, _ in both})
+    renamed = [[(used.index(n), at) for n, at in both] for both in order]
+    in_grad = pl.pallas_call(
+        functools.partial(upper_grad_kernel, renamed, counts),
+        out_shape=jax.ShapeDtypeStruct((chans, planes, span_y, span_z), BF16),
+        in_specs=[vmem] * (len(used) + 2),
+        out_specs=pl.BlockSpec(memory_space=pl.ANY),
+        scratch_shapes=[
+            pltpu.VMEM((chans, planes, span_y - done, span_z), BF16),
+            pltpu.SemaphoreType.DMA((2,)),
+        ],
+        compiler_params=PARAMS,
+        cost_estimate=pl.CostEstimate(
+            flops=4 * total * 12 * chans * (span_y - done) * half_z,
+            bytes_accessed=1 << 20,
+            transcendentals=0,
+        ),
+        name="upper_grad",
+    )(*[arrays[n] for n in used], weights_back, lower)
     return out_act, in_grad[:cin]
 
 

time: 56.8 us -> 56.7 us (level)
    pallas_call x9 -> x8, Pallas kernels: 6.1 us -> 4.14 us  [call(): pl.pallas_call(kernel, out_shape=out_shape, scratch_shapes=list(scratch),...]
    pallas_call x0 -> x1, Pallas kernels: none -> 1.84 us  [on_device(): pl.pallas_call(functools.partial(upper_grad_kernel, renamed, counts), out...]
where the time goes in v8:
time: 56.7 us; the launch traced here: 56.5 us
  starting transfers between devices  31.1 us (55%)
  waiting for transfers between devices  15.3 us (27%)
  Pallas kernels  6.22 us (11%)
  local copies, waits for them, and re-layouts  2.25 us (4%)
  other arithmetic  0.92 us (2%)
  between operations  0.81 us (1%)
    ppermute x19, starting transfers between devices, shifted(): lax.ppermute(block, axis, [(ring[i], ring[(i + distance) % count]) for i...  31.1 us
    ppermute x19, waiting for transfers between devices, shifted(): lax.ppermute(block, axis, [(ring[i], ring[(i + distance) % count]) for i...  15.3 us
    pallas_call x8, Pallas kernels, call(): pl.pallas_call(kernel, out_shape=out_shape, scratch_shapes=list(scratch),...  4.14 us
    pallas_call x1, Pallas kernels, on_device(): pl.pallas_call(functools.partial(upper_grad_kernel, renamed, counts), out...  1.84 us
    squeeze x1, local copies, waits for them, and re-layouts, on_device(): plane = lax.optimization_barrier(field[:, planes - 1])  1.17 us
  transfers between devices with their start and end apart: 19, of which 9 were waited for; matrix products, arithmetic and copies ran while one was open for 3% of the time, Pallas kernels for 8%

profile of v8, /device:TPU:11, one launch (start us, length us, event | category | flops | bytes accessed | tf_op | source)
XLA Modules:
  0.0 56.5 jit_solution(10335397912807802421)
XLA Ops:
  0.6 1.2 %slice_bitcast_fusion = bf16[8,128,256]{2,1,0:T(8,128)(2,1)S(1)} fusion(bf16[8,2,128,256]{3,2,1,0:T(8,128)(2,1)} %field_ref.1), kind=kLoop, calls=%fused_computation | loop fusion | bytes 1048576 | tf_op jit(solution)/shard_map/squeeze | solution.py:293
  1.9 1.8 %collective-permute-start = (bf16[8,80,256]{2,1,0:T(8,128)(2,1)S(1)}, bf16[8,80,256]{2,1,0:T(8,128)(2,1)S(1)}, u32[]{:S(2)}, u32[]{:S(2)}) collective-permute-start(bf16[8,80,256]{2,1,0:T(8,128)(2,1)S(1)} %pad_maximum_fusion), channel_id=1, source_target_pairs={{0,4},{4,8},{8,12},{12,16},{16,20},{20,24},{24,28},{28,0},{1,5},{5... | collective-permute-start | bytes 983048 | tf_op jit(solution)/shard_map/ppermute | solution.py:30
  3.7 0.1 collective-permute-start.2
  3.8 0.8 %dynamic-slice_convert_fusion = f32[64,8,3,3,3]{0,1,4,3,2:T(8,128)S(1)} fusion(bf16[64,32,3,3,3]{0,1,4,3,2:T(8,128)(2,1)} %param.5, s32[]{:T(128)S(6)} %select_n.3), kind=kLoop, calls=%fused_computation.7 | loop fusion | flops 13824 | bytes 82948 | tf_op jit(solution)/shard_map/convert_element_type | solution.py:305
  4.6 0.2 weights.1
  4.9 1.5 %local_planes.1.refs_2_.refs_3_ = f32[64,8192]{1,0:T(8,128)S(1)} custom-call(bf16[8,2,128,256]{3,2,1,0:T(8,128)(2,1)S(1)} %copy-done, bf16[64,192]{1,0:T(8,128)(2,1)S(1)} %get-tuple-element.30.weight_ref), custom_call_target="tpu_custom_call" | custom-call | flops 201326592 | bytes 4194304 | tf_op jit(solution)/shard_map/local_planes/pallas_call | solution.py:270
  6.4 1.3 %collective-permute-done.refs_0_ = bf16[8,80,256]{2,1,0:T(8,128)(2,1)S(1)} collective-permute-done((bf16[8,80,256]{2,1,0:T(8,128)(2,1)S(1)}, bf16[8,80,256]{2,1,0:T(8,128)(2,1)S(1)}, u32[]{:S(2)}, u32[]{:S(2)}) %collective-permute-start) | collective-permute-done | bytes 327712 | tf_op jit(solution)/shard_map/ppermute | solution.py:30
  7.7 0.6 %halo_plane.2 = (bf16[16,4096]{1,0:T(8,128)(2,1)S(1)}, bf16[16,4096]{1,0:T(8,128)(2,1)S(1)}, bf16[16,4096]{1,0:T(8,128)(2,1)S(1)}, bf16[16,4096]{1,0:T(8,128)(2,1)S(1)}) custom-call(bf16[8,80,256]{2,1,0:T(8,128)(2,1)S(1)} %collective-permute-done.refs_0_, bf16[64,96]{1,0:T(8,128)(2,1)S(1)} %get-tuple-element.37.refs_1_.refs_2_, ...), custom_call_target="tpu_custom_call" | custom-call | flops 50331648 | bytes 2097152 | tf_op jit(solution)/shard_map/halo_plane/pallas_call | solution.py:270
  8.4 0.0 copy-start.1
  8.4 0.0 copy-start.2
  8.4 0.2 collective-permute-start.4
  8.6 1.2 %collective-permute-done.2.refs_1_ = bf16[8,48,256]{2,1,0:T(8,128)(2,1)S(1)} collective-permute-done((bf16[8,48,256]{2,1,0:T(8,128)(2,1)S(1)}, bf16[8,48,256]{2,1,0:T(8,128)(2,1)S(1)}, u32[]{:S(2)}, u32[]{:S(2)}) %collective-permute-start.2) | collective-permute-done | bytes 196640 | tf_op jit(solution)/shard_map/ppermute | solution.py:30
  9.8 0.6 %halo_plane.3 = (bf16[16,4096]{1,0:T(8,128)(2,1)S(1)}, bf16[16,4096]{1,0:T(8,128)(2,1)S(1)}, bf16[16,4096]{1,0:T(8,128)(2,1)S(1)}, bf16[16,4096]{1,0:T(8,128)(2,1)S(1)}) custom-call(bf16[8,80,256]{2,1,0:T(8,128)(2,1)S(1)} %collective-permute-done.refs_0_, bf16[8,48,256]{2,1,0:T(8,128)(2,1)S(1)} %collective-permute-done.2.refs_1_, ...), custom_call_target="tpu_custom_call" | custom-call | flops 50331648 | bytes 2097152 | tf_op jit(solution)/shard_map/halo_plane/pallas_call | solution.py:270
  10.5 2.4 %collective-permute-start.3 = (bf16[16,4096]{1,0:T(8,128)(2,1)S(1)}, bf16[16,4096]{1,0:T(8,128)(2,1)S(1)}, u32[]{:S(2)}, u32[]{:S(2)}) collective-permute-start(bf16[16,4096]{1,0:T(8,128)(2,1)S(1)} %get-tuple-element.38), channel_id=1, source_target_pairs={{0,1},{2,0},{3,2},{1,3},{4,5},{6,4},{7,6},{5,7},{8,9},{10,8},{11,1... | collective-permute-start | bytes 393224 | tf_op jit(solution)/shard_map/ppermute | solution.py:30
  12.8 0.3 collective-permute-done.4.one_ref
  13.2 0.1 collective-permute-start.5
  13.3 0.2 copy.12
  13.5 2.4 %collective-permute-start.1 = (bf16[16,4096]{1,0:T(8,128)(2,1)S(1)}, bf16[16,4096]{1,0:T(8,128)(2,1)S(1)}, u32[]{:S(2)}, u32[]{:S(2)}) collective-permute-start(bf16[16,4096]{1,0:T(8,128)(2,1)S(1)} %get-tuple-element.36), channel_id=1, source_target_pairs={{0,1},{2,0},{3,2},{1,3},{4,5},{6,4},{7,6},{5,7},{8,9},{10,8},{11,1... | collective-permute-start | bytes 393224 | tf_op jit(solution)/shard_map/ppermute | solution.py:30
  15.9 0.2 collective-permute-start.6
  16.1 0.4 collective-permute-done.3.one_ref
  16.5 2.9 %collective-permute-done.5.refs_2_ = bf16[16,4096]{1,0:T(8,128)(2,1)S(1)} collective-permute-done((bf16[16,4096]{1,0:T(8,128)(2,1)S(1)}, bf16[16,4096]{1,0:T(8,128)(2,1)S(1)}, u32[]{:S(2)}, u32[]{:S(2)}) %collective-permute-start.5) | collective-permute-done | bytes 131104 | tf_op jit(solution)/shard_map/ppermute | solution.py:30
  19.4 1.1 %collective-permute-start.7 = (bf16[16,4096]{1,0:T(8,128)(2,1)S(1)}, bf16[16,4096]{1,0:T(8,128)(2,1)S(1)}, u32[]{:S(2)}, u32[]{:S(2)}) collective-permute-start(bf16[16,4096]{1,0:T(8,128)(2,1)S(1)} %add.7), channel_id=1, source_target_pairs={{0,1},{2,0},{3,2},{1,3},{4,5},{6,4},{7,6},{5,7},{8,9},{10,8},{11,1... | collective-permute-start | bytes 393224 | tf_op jit(solution)/shard_map/ppermute | solution.py:30
  20.4 3.0 %collective-permute-done.1.refs_1_ = bf16[16,4096]{1,0:T(8,128)(2,1)S(1)} collective-permute-done((bf16[16,4096]{1,0:T(8,128)(2,1)S(1)}, bf16[16,4096]{1,0:T(8,128)(2,1)S(1)}, u32[]{:S(2)}, u32[]{:S(2)}) %collective-permute-start.1) | collective-permute-done | bytes 131104 | tf_op jit(solution)/shard_map/ppermute | solution.py:30
  23.4 0.1 broadcast_in_dim.2.refs_3_
  23.5 0.2 activation.2
  23.8 0.1 collective-permute-start.9
  23.8 3.3 %collective-permute-start.10 = (bf16[16,4096]{1,0:T(8,128)(2,1)S(1)}, bf16[16,4096]{1,0:T(8,128)(2,1)S(1)}, u32[]{:S(2)}, u32[]{:S(2)}) collective-permute-start(bf16[16,4096]{1,0:T(8,128)(2,1)S(1)} %get-tuple-element.54.refs_3_.refs_5_), channel_id=1, source_target_pairs={{0,1},{2,0},{3,2},{1,3},{4,5},{6,4},{7,6},{5,7},{8,9},{10,8},{11,1... | collective-permute-start | bytes 393224 | tf_op jit(solution)/shard_map/ppermute | solution.py:30
  27.1 0.0 collective-permute-done.6.refs_1_
  27.1 2.0 %collective-permute-done.7.refs_2_ = bf16[16,4096]{1,0:T(8,128)(2,1)S(1)} collective-permute-done((bf16[16,4096]{1,0:T(8,128)(2,1)S(1)}, bf16[16,4096]{1,0:T(8,128)(2,1)S(1)}, u32[]{:S(2)}, u32[]{:S(2)}) %collective-permute-start.7) | collective-permute-done | bytes 131104 | tf_op jit(solution)/shard_map/ppermute | solution.py:30
  29.1 0.2 activation.3
  29.3 3.3 %collective-permute-start.13 = (bf16[16,4096]{1,0:T(8,128)(2,1)S(1)}, bf16[16,4096]{1,0:T(8,128)(2,1)S(1)}, u32[]{:S(2)}, u32[]{:S(2)}) collective-permute-start(bf16[16,4096]{1,0:T(8,128)(2,1)S(1)} %get-tuple-element.51.refs_9_), channel_id=1, source_target_pairs={{0,1},{2,0},{3,2},{1,3},{4,5},{6,4},{7,6},{5,7},{8,9},{10,8},{11,1... | collective-permute-start | bytes 393224 | tf_op jit(solution)/shard_map/ppermute | solution.py:30
  32.6 0.0 collective-permute-start.12
  32.6 2.9 %collective-permute-start.8 = (bf16[16,8192]{1,0:T(8,128)(2,1)S(1)}, bf16[16,8192]{1,0:T(8,128)(2,1)S(1)}, u32[]{:S(2)}, u32[]{:S(2)}) collective-permute-start(bf16[16,8192]{1,0:T(8,128)(2,1)S(1)} %pad_maximum_fusion.1), channel_id=1, source_target_pairs={{0,28},{4,0},{8,4},{12,8},{16,12},{20,16},{24,20},{28,24},{1,29},{... | collective-permute-start | bytes 786440 | tf_op jit(solution)/shard_map/ppermute | solution.py:30
  35.6 0.0 collective-permute-done.9.refs_4_.refs_6_
  35.6 0.0 collective-permute-done.10.refs_6_.refs_8_
  35.6 1.2 %collective-permute-start.15 = (bf16[16,4096]{1,0:T(8,128)(2,1)S(1)}, bf16[16,4096]{1,0:T(8,128)(2,1)S(1)}, u32[]{:S(2)}, u32[]{:S(2)}) collective-permute-start(bf16[16,4096]{1,0:T(8,128)(2,1)S(1)} %collective-permute-done.9.refs_4_.refs_6_), channel_id=1, source_target_pairs={{0,2},{2,3},{3,1},{1,0},{4,6},{6,7},{7,5},{5,4},{8,10},{10,11},{11... | collective-permute-start | bytes 393224 | tf_op jit(solution)/shard_map/ppermute | solution.py:30
  36.8 1.8 %collective-permute-start.11 = (bf16[32,4096]{1,0:T(8,128)(2,1)S(1)}, bf16[32,4096]{1,0:T(8,128)(2,1)S(1)}, u32[]{:S(2)}, u32[]{:S(2)}) collective-permute-start(bf16[32,4096]{1,0:T(8,128)(2,1)S(1)} %pad_maximum_fusion.2), channel_id=1, source_target_pairs={{0,28},{4,0},{8,4},{12,8},{16,12},{20,16},{24,20},{28,24},{1,29},{... | collective-permute-start | bytes 786440 | tf_op jit(solution)/shard_map/ppermute | solution.py:30
  38.6 0.0 collective-permute-done.13.refs_12_
  38.6 2.8 %collective-permute-start.17 = (bf16[16,4096]{1,0:T(8,128)(2,1)S(1)}, bf16[16,4096]{1,0:T(8,128)(2,1)S(1)}, u32[]{:S(2)}, u32[]{:S(2)}) collective-permute-start(bf16[16,4096]{1,0:T(8,128)(2,1)S(1)} %collective-permute-done.13.refs_12_), channel_id=1, source_target_pairs={{0,1},{2,0},{3,2},{1,3},{4,5},{6,4},{7,6},{5,7},{8,9},{10,8},{11,1... | collective-permute-start | bytes 393224 | tf_op jit(solution)/shard_map/ppermute | solution.py:30
  41.4 5.1 %collective-permute-start.14 = (bf16[32,4096]{1,0:T(8,128)(2,1)S(1)}, bf16[32,4096]{1,0:T(8,128)(2,1)S(1)}, u32[]{:S(2)}, u32[]{:S(2)}) collective-permute-start(bf16[32,4096]{1,0:T(8,128)(2,1)S(1)} %pad_maximum_fusion.3), channel_id=1, source_target_pairs={{0,28},{4,0},{8,4},{12,8},{16,12},{20,16},{24,20},{28,24},{1,29},{... | collective-permute-start | bytes 786440 | tf_op jit(solution)/shard_map/ppermute | solution.py:30
  46.5 0.1 collective-permute-start.16
  46.6 2.4 %collective-permute-start.18 = (bf16[16,4096]{1,0:T(8,128)(2,1)S(1)}, bf16[16,4096]{1,0:T(8,128)(2,1)S(1)}, u32[]{:S(2)}, u32[]{:S(2)}) collective-permute-start(bf16[16,4096]{1,0:T(8,128)(2,1)S(1)} %collective-permute-done.17.refs_11_), channel_id=1, source_target_pairs={{0,28},{4,0},{8,4},{12,8},{16,12},{20,16},{24,20},{28,24},{1,29},{... | collective-permute-start | bytes 393224 | tf_op jit(solution)/shard_map/ppermute | solution.py:30
  48.9 0.8 %copy.10 = bf16[2,8,64,128]{3,2,1,0:T(8,128)(2,1)} copy(bf16[2,8,64,128]{3,1,2,0:T(8,128)(2,1)S(1)} %maximum_bitcast_fusion) | data formatting | bytes 524288
  49.7 3.6 %collective-permute-done.16.refs_2_.refs_3_ = bf16[16,4096]{1,0:T(8,128)(2,1)S(1)} collective-permute-done((bf16[16,4096]{1,0:T(8,128)(2,1)S(1)}, bf16[16,4096]{1,0:T(8,128)(2,1)S(1)}, u32[]{:S(2)}, u32[]{:S(2)}) %collective-permute-start.16) | collective-permute-done | bytes 131104 | tf_op jit(solution)/shard_map/ppermute | solution.py:30
  53.3 0.0 collective-permute-done.8.refs_0_
  53.3 0.8 %lower_grad.1.refs_14_ = bf16[8,2,48,256]{3,2,1,0:T(8,128)(2,1)S(1)} custom-call(bf16[16,8192]{1,0:T(8,128)(2,1)S(1)} %collective-permute-done.8.refs_0_, bf16[32,4096]{1,0:T(8,128)(2,1)S(1)} %collective-permute-done.11.refs_1_, bf16[16,4096]{1,0:T(8,128)(2,1)S(1)} %collective-permute-done.16.refs_2_.refs_3_, ...), custom_call_target="tpu_custom_call" | custom-call | flops 150994944 | bytes 1048576 | tf_op jit(solution)/shard_map/lower_grad/pallas_call | solution.py:270
  54.1 0.6 %collective-permute-done.18.refs_4_ = bf16[16,4096]{1,0:T(8,128)(2,1)S(1)} collective-permute-done((bf16[16,4096]{1,0:T(8,128)(2,1)S(1)}, bf16[16,4096]{1,0:T(8,128)(2,1)S(1)}, u32[]{:S(2)}, u32[]{:S(2)}) %collective-permute-start.18) | collective-permute-done | bytes 131104 | tf_op jit(solution)/shard_map/ppermute | solution.py:30
  54.7 1.8 %upper_grad.1 = bf16[8,2,128,256]{3,2,1,0:T(8,128)(2,1)} custom-call(bf16[16,8192]{1,0:T(8,128)(2,1)S(1)} %collective-permute-done.8.refs_0_, bf16[32,4096]{1,0:T(8,128)(2,1)S(1)} %collective-permute-done.11.refs_1_, bf16[32,4096]{1,0:T(8,128)(2,1)S(1)} %collective-permute-done.14.refs_2_, bf16[16,4096]{1,0:T(8,128)(2,1)S(1)} %collective-permute-done.16.refs_2_.refs_3_, ...), custom_call_target="tpu_custom_call" | custom-call | flops 251658240 | bytes 1048576 | tf_op jit(solution)/shard_map/upper_grad/pallas_call | solution.py:429
  (20 shorter events, 0.2 us)
Async XLA Ops:
  0.6 4.2 %copy-start = (bf16[8,2,128,256]{3,2,1,0:T(8,128)(2,1)S(1)}, bf16[8,2,128,256]{3,2,1,0:T(8,128)(2,1)}, u32[]{:S(2)}) copy-start(bf16[8,2,128,256]{3,2,1,0:T(8,128)(2,1)} %field_ref.1) | copy-start | bytes 3145732
  1.9 5.8 %collective-permute-start = (bf16[8,80,256]{2,1,0:T(8,128)(2,1)S(1)}, bf16[8,80,256]{2,1,0:T(8,128)(2,1)S(1)}, u32[]{:S(2)}, u32[]{:S(2)}) collective-permute-start(bf16[8,80,256]{2,1,0:T(8,128)(2,1)S(1)} %pad_maximum_fusion), channel_id=1, source_target_pairs={{0,4},{4,8},{8,12},{12,16},{16,20},{20,24},{24,28},{28,0},{1,5},{5... | collective-permute-start | bytes 983048 | tf_op jit(solution)/shard_map/ppermute | solution.py:30
  3.7 6.1 %collective-permute-start.2 = (bf16[8,48,256]{2,1,0:T(8,128)(2,1)S(1)}, bf16[8,48,256]{2,1,0:T(8,128)(2,1)S(1)}, u32[]{:S(2)}, u32[]{:S(2)}) collective-permute-start(bf16[8,48,256]{2,1,0:T(8,128)(2,1)S(1)} %slice.26), channel_id=1, source_target_pairs={{0,4},{4,8},{8,12},{12,16},{16,20},{20,24},{24,28},{28,0},{1,5},{5... | collective-permute-start | bytes 589832 | tf_op jit(solution)/shard_map/ppermute | solution.py:30
  8.4 4.9 %copy-start.1 = (bf16[16,1,64,128]{3,2,1,0:T(8,128)(2,1)S(1)}, bf16[16,1,64,128]{3,2,1,0:T(8,128)(2,1)}, u32[]{:S(2)}) copy-start(bf16[16,1,64,128]{3,2,1,0:T(8,128)(2,1)} %param.7) | copy-start | bytes 786436
  8.4 15.0 %copy-start.2 = (f32[16]{0:T(128)S(1)}, f32[16]{0:T(128)}, u32[]{:S(2)}) copy-start(f32[16]{0:T(128)} %param.6) | copy-start | bytes 196
  8.4 4.8 %collective-permute-start.4 = (bf16[16,4096]{1,0:T(8,128)(2,1)S(1)}, bf16[16,4096]{1,0:T(8,128)(2,1)S(1)}, u32[]{:S(2)}, u32[]{:S(2)}) collective-permute-start(bf16[16,4096]{1,0:T(8,128)(2,1)S(1)} %get-tuple-element.40), channel_id=1, source_target_pairs={{0,2},{2,3},{3,1},{1,0},{4,6},{6,7},{7,5},{5,4},{8,10},{10,11},{11... | collective-permute-start | bytes 393224 | tf_op jit(solution)/shard_map/ppermute | solution.py:30
  10.5 6.0 %collective-permute-start.3 = (bf16[16,4096]{1,0:T(8,128)(2,1)S(1)}, bf16[16,4096]{1,0:T(8,128)(2,1)S(1)}, u32[]{:S(2)}, u32[]{:S(2)}) collective-permute-start(bf16[16,4096]{1,0:T(8,128)(2,1)S(1)} %get-tuple-element.38), channel_id=1, source_target_pairs={{0,1},{2,0},{3,2},{1,3},{4,5},{6,4},{7,6},{5,7},{8,9},{10,8},{11,1... | collective-permute-start | bytes 393224 | tf_op jit(solution)/shard_map/ppermute | solution.py:30
  13.2 6.1 %collective-permute-start.5 = (bf16[16,4096]{1,0:T(8,128)(2,1)S(1)}, bf16[16,4096]{1,0:T(8,128)(2,1)S(1)}, u32[]{:S(2)}, u32[]{:S(2)}) collective-permute-start(bf16[16,4096]{1,0:T(8,128)(2,1)S(1)} %add.6), channel_id=1, source_target_pairs={{0,2},{2,3},{3,1},{1,0},{4,6},{6,7},{7,5},{5,4},{8,10},{10,11},{11... | collective-permute-start | bytes 393224 | tf_op jit(solution)/shard_map/ppermute | solution.py:30
  13.5 10.0 %collective-permute-start.1 = (bf16[16,4096]{1,0:T(8,128)(2,1)S(1)}, bf16[16,4096]{1,0:T(8,128)(2,1)S(1)}, u32[]{:S(2)}, u32[]{:S(2)}) collective-permute-start(bf16[16,4096]{1,0:T(8,128)(2,1)S(1)} %get-tuple-element.36), channel_id=1, source_target_pairs={{0,1},{2,0},{3,2},{1,3},{4,5},{6,4},{7,6},{5,7},{8,9},{10,8},{11,1... | collective-permute-start | bytes 393224 | tf_op jit(solution)/shard_map/ppermute | solution.py:30
  15.9 11.3 %collective-permute-start.6 = (bf16[16,4096]{1,0:T(8,128)(2,1)S(1)}, bf16[16,4096]{1,0:T(8,128)(2,1)S(1)}, u32[]{:S(2)}, u32[]{:S(2)}) collective-permute-start(bf16[16,4096]{1,0:T(8,128)(2,1)S(1)} %get-tuple-element.46), channel_id=1, source_target_pairs={{0,2},{2,3},{3,1},{1,0},{4,6},{6,7},{7,5},{5,4},{8,10},{10,11},{11... | collective-permute-start | bytes 393224 | tf_op jit(solution)/shard_map/ppermute | solution.py:30
  19.4 9.7 %collective-permute-start.7 = (bf16[16,4096]{1,0:T(8,128)(2,1)S(1)}, bf16[16,4096]{1,0:T(8,128)(2,1)S(1)}, u32[]{:S(2)}, u32[]{:S(2)}) collective-permute-start(bf16[16,4096]{1,0:T(8,128)(2,1)S(1)} %add.7), channel_id=1, source_target_pairs={{0,1},{2,0},{3,2},{1,3},{4,5},{6,4},{7,6},{5,7},{8,9},{10,8},{11,1... | collective-permute-start | bytes 393224 | tf_op jit(solution)/shard_map/ppermute | solution.py:30
  23.8 11.8 %collective-permute-start.9 = (bf16[16,4096]{1,0:T(8,128)(2,1)S(1)}, bf16[16,4096]{1,0:T(8,128)(2,1)S(1)}, u32[]{:S(2)}, u32[]{:S(2)}) collective-permute-start(bf16[16,4096]{1,0:T(8,128)(2,1)S(1)} %get-tuple-element.54.refs_3_.refs_5_), channel_id=1, source_target_pairs={{0,2},{2,3},{3,1},{1,0},{4,6},{6,7},{7,5},{5,4},{8,10},{10,11},{11... | collective-permute-start | bytes 393224 | tf_op jit(solution)/shard_map/ppermute | solution.py:30
  23.8 11.8 %collective-permute-start.10 = (bf16[16,4096]{1,0:T(8,128)(2,1)S(1)}, bf16[16,4096]{1,0:T(8,128)(2,1)S(1)}, u32[]{:S(2)}, u32[]{:S(2)}) collective-permute-start(bf16[16,4096]{1,0:T(8,128)(2,1)S(1)} %get-tuple-element.54.refs_3_.refs_5_), channel_id=1, source_target_pairs={{0,1},{2,0},{3,2},{1,3},{4,5},{6,4},{7,6},{5,7},{8,9},{10,8},{11,1... | collective-permute-start | bytes 393224 | tf_op jit(solution)/shard_map/ppermute | solution.py:30
  29.3 9.3 %collective-permute-start.13 = (bf16[16,4096]{1,0:T(8,128)(2,1)S(1)}, bf16[16,4096]{1,0:T(8,128)(2,1)S(1)}, u32[]{:S(2)}, u32[]{:S(2)}) collective-permute-start(bf16[16,4096]{1,0:T(8,128)(2,1)S(1)} %get-tuple-element.51.refs_9_), channel_id=1, source_target_pairs={{0,1},{2,0},{3,2},{1,3},{4,5},{6,4},{7,6},{5,7},{8,9},{10,8},{11,1... | collective-permute-start | bytes 393224 | tf_op jit(solution)/shard_map/ppermute | solution.py:30
  32.6 8.7 %collective-permute-start.12 = (bf16[16,4096]{1,0:T(8,128)(2,1)S(1)}, bf16[16,4096]{1,0:T(8,128)(2,1)S(1)}, u32[]{:S(2)}, u32[]{:S(2)}) collective-permute-start(bf16[16,4096]{1,0:T(8,128)(2,1)S(1)} %get-tuple-element.51.refs_9_), channel_id=1, source_target_pairs={{0,2},{2,3},{3,1},{1,0},{4,6},{6,7},{7,5},{5,4},{8,10},{10,11},{11... | collective-permute-start | bytes 393224 | tf_op jit(solution)/shard_map/ppermute | solution.py:30
  32.6 20.6 %collective-permute-start.8 = (bf16[16,8192]{1,0:T(8,128)(2,1)S(1)}, bf16[16,8192]{1,0:T(8,128)(2,1)S(1)}, u32[]{:S(2)}, u32[]{:S(2)}) collective-permute-start(bf16[16,8192]{1,0:T(8,128)(2,1)S(1)} %pad_maximum_fusion.1), channel_id=1, source_target_pairs={{0,28},{4,0},{8,4},{12,8},{16,12},{20,16},{24,20},{28,24},{1,29},{... | collective-permute-start | bytes 786440 | tf_op jit(solution)/shard_map/ppermute | solution.py:30
  35.6 10.9 %collective-permute-start.15 = (bf16[16,4096]{1,0:T(8,128)(2,1)S(1)}, bf16[16,4096]{1,0:T(8,128)(2,1)S(1)}, u32[]{:S(2)}, u32[]{:S(2)}) collective-permute-start(bf16[16,4096]{1,0:T(8,128)(2,1)S(1)} %collective-permute-done.9.refs_4_.refs_6_), channel_id=1, source_target_pairs={{0,2},{2,3},{3,1},{1,0},{4,6},{6,7},{7,5},{5,4},{8,10},{10,11},{11... | collective-permute-start | bytes 393224 | tf_op jit(solution)/shard_map/ppermute | solution.py:30
  36.8 16.5 %collective-permute-start.11 = (bf16[32,4096]{1,0:T(8,128)(2,1)S(1)}, bf16[32,4096]{1,0:T(8,128)(2,1)S(1)}, u32[]{:S(2)}, u32[]{:S(2)}) collective-permute-start(bf16[32,4096]{1,0:T(8,128)(2,1)S(1)} %pad_maximum_fusion.2), channel_id=1, source_target_pairs={{0,28},{4,0},{8,4},{12,8},{16,12},{20,16},{24,20},{28,24},{1,29},{... | collective-permute-start | bytes 786440 | tf_op jit(solution)/shard_map/ppermute | solution.py:30
  38.6 8.0 %collective-permute-start.17 = (bf16[16,4096]{1,0:T(8,128)(2,1)S(1)}, bf16[16,4096]{1,0:T(8,128)(2,1)S(1)}, u32[]{:S(2)}, u32[]{:S(2)}) collective-permute-start(bf16[16,4096]{1,0:T(8,128)(2,1)S(1)} %collective-permute-done.13.refs_12_), channel_id=1, source_target_pairs={{0,1},{2,0},{3,2},{1,3},{4,5},{6,4},{7,6},{5,7},{8,9},{10,8},{11,1... | collective-permute-start | bytes 393224 | tf_op jit(solution)/shard_map/ppermute | solution.py:30
  41.4 13.3 %collective-permute-start.14 = (bf16[32,4096]{1,0:T(8,128)(2,1)S(1)}, bf16[32,4096]{1,0:T(8,128)(2,1)S(1)}, u32[]{:S(2)}, u32[]{:S(2)}) collective-permute-start(bf16[32,4096]{1,0:T(8,128)(2,1)S(1)} %pad_maximum_fusion.3), channel_id=1, source_target_pairs={{0,28},{4,0},{8,4},{12,8},{16,12},{20,16},{24,20},{28,24},{1,29},{... | collective-permute-start | bytes 786440 | tf_op jit(solution)/shard_map/ppermute | solution.py:30
  46.5 6.8 %collective-permute-start.16 = (bf16[16,4096]{1,0:T(8,128)(2,1)S(1)}, bf16[16,4096]{1,0:T(8,128)(2,1)S(1)}, u32[]{:S(2)}, u32[]{:S(2)}) collective-permute-start(bf16[16,4096]{1,0:T(8,128)(2,1)S(1)} %collective-permute-done.15.refs_5_.refs_7_), channel_id=1, source_target_pairs={{0,28},{4,0},{8,4},{12,8},{16,12},{20,16},{24,20},{28,24},{1,29},{... | collective-permute-start | bytes 393224 | tf_op jit(solution)/shard_map/ppermute | solution.py:30
  46.6 8.1 %collective-permute-start.18 = (bf16[16,4096]{1,0:T(8,128)(2,1)S(1)}, bf16[16,4096]{1,0:T(8,128)(2,1)S(1)}, u32[]{:S(2)}, u32[]{:S(2)}) collective-permute-start(bf16[16,4096]{1,0:T(8,128)(2,1)S(1)} %collective-permute-done.17.refs_11_), channel_id=1, source_target_pairs={{0,28},{4,0},{8,4},{12,8},{16,12},{20,16},{24,20},{28,24},{1,29},{... | collective-permute-start | bytes 393224 | tf_op jit(solution)/shard_map/ppermute | solution.py:30

commit v9 on v8

--- a/solution.py
+++ b/solution.py
@@ -123,10 +123,6 @@
         sums = (sums + tap_sums(weights, taps_ref, lane, width, half_z)).astype(BF16)
         for peer, ref in enumerate(part_refs):
             ref[:, lane : lane + width] = sums[peer * rows : (peer + 1) * rows]
-
-
-def add_kernel(one_ref, two_ref, sum_ref):
-    sum_ref[...] = (one_ref[...].astype(F32) + two_ref[...].astype(F32)).astype(BF16)
 
 
 def act_kernel(*refs):
@@ -361,7 +357,7 @@
     for h in range(2):
         if h:
             relayed[1], arrived[0][-1] = lax.optimization_barrier((relayed[1], arrived[0][-1]))
-        joined = call(add_kernel, "add", shapes[h], (relayed[h], parts[h][steps[h]]))
+        joined = (relayed[h].astype(F32) + parts[h][steps[h]].astype(F32)).astype(BF16)
         arrived[h].append(shifted(joined, "col", steps[h]))
 
     bias_p = [jnp.broadcast_to(jnp.pad(bias, fill_o)[:, None], shape.shape) for shape in shapes]

time: 56.7 us -> 56.8 us (level)
    pallas_call x8 -> x6, Pallas kernels: 4.14 us -> 4.07 us  [call(): pl.pallas_call(kernel, out_shape=out_shape, scratch_shapes=list(scratch),...]
  transfers between devices with their start and end apart: 19 -> 19, of which waited for: 9 -> 9; matrix products, arithmetic and copies ran while one was open for 3% -> 4% of each run, Pallas kernels for 8% -> 8%
where the time goes in v9:
time: 56.8 us; the launch traced here: 56.6 us
  starting transfers between devices  31 us (55%)
  waiting for transfers between devices  15.3 us (27%)
  Pallas kernels  6.15 us (11%)
  local copies, waits for them, and re-layouts  2.25 us (4%)
  other arithmetic  0.99 us (2%)
  between operations  0.81 us (1%)
    ppermute x19, starting transfers between devices, shifted(): lax.ppermute(block, axis, [(ring[i], ring[(i + distance) % count]) for i...  31 us
    ppermute x19, waiting for transfers between devices, shifted(): lax.ppermute(block, axis, [(ring[i], ring[(i + distance) % count]) for i...  15.3 us
    pallas_call x6, Pallas kernels, call(): pl.pallas_call(kernel, out_shape=out_shape, scratch_shapes=list(scratch),...  4.07 us
    pallas_call x1, Pallas kernels, on_device(): pl.pallas_call(functools.partial(upper_grad_kernel, renamed, counts), out...  1.84 us
    squeeze x1, local copies, waits for them, and re-layouts, on_device(): plane = lax.optimization_barrier(field[:, planes - 1])  1.17 us
  transfers between devices with their start and end apart: 19, of which 9 were waited for; matrix products, arithmetic and copies ran while one was open for 4% of the time, Pallas kernels for 8%

profile of v9, /device:TPU:11, one launch (start us, length us, event | category | flops | bytes accessed | tf_op | source)
XLA Modules:
  0.0 56.6 jit_solution(5165719297933103387)
XLA Ops:
  0.6 1.2 %slice_bitcast_fusion = bf16[8,128,256]{2,1,0:T(8,128)(2,1)S(1)} fusion(bf16[8,2,128,256]{3,2,1,0:T(8,128)(2,1)} %field_ref.1), kind=kLoop, calls=%fused_computation | loop fusion | bytes 1048576 | tf_op jit(solution)/shard_map/squeeze | solution.py:289
  1.9 1.8 %collective-permute-start = (bf16[8,80,256]{2,1,0:T(8,128)(2,1)S(1)}, bf16[8,80,256]{2,1,0:T(8,128)(2,1)S(1)}, u32[]{:S(2)}, u32[]{:S(2)}) collective-permute-start(bf16[8,80,256]{2,1,0:T(8,128)(2,1)S(1)} %pad_maximum_fusion), channel_id=1, source_target_pairs={{0,4},{4,8},{8,12},{12,16},{16,20},{20,24},{24,28},{28,0},{1,5},{5... | collective-permute-start | bytes 983048 | tf_op jit(solution)/shard_map/ppermute | solution.py:30
  3.7 0.1 collective-permute-start.2
  3.8 0.8 %dynamic-slice_convert_fusion = f32[64,8,3,3,3]{0,1,4,3,2:T(8,128)S(1)} fusion(bf16[64,32,3,3,3]{0,1,4,3,2:T(8,128)(2,1)} %param.5, s32[]{:T(128)S(6)} %select_n.3), kind=kLoop, calls=%fused_computation.9 | loop fusion | flops 13824 | bytes 82948 | tf_op jit(solution)/shard_map/convert_element_type | solution.py:301
  4.6 0.2 weights.1
  4.9 1.5 %local_planes.1.refs_2_.refs_3_ = f32[64,8192]{1,0:T(8,128)S(1)} custom-call(bf16[8,2,128,256]{3,2,1,0:T(8,128)(2,1)S(1)} %copy-done, bf16[64,192]{1,0:T(8,128)(2,1)S(1)} %get-tuple-element.30.weight_ref), custom_call_target="tpu_custom_call" | custom-call | flops 201326592 | bytes 4194304 | tf_op jit(solution)/shard_map/local_planes/pallas_call | solution.py:266
  6.4 1.3 %collective-permute-done.refs_0_ = bf16[8,80,256]{2,1,0:T(8,128)(2,1)S(1)} collective-permute-done((bf16[8,80,256]{2,1,0:T(8,128)(2,1)S(1)}, bf16[8,80,256]{2,1,0:T(8,128)(2,1)S(1)}, u32[]{:S(2)}, u32[]{:S(2)}) %collective-permute-start) | collective-permute-done | bytes 327712 | tf_op jit(solution)/shard_map/ppermute | solution.py:30
  7.7 0.6 %halo_plane.2 = (bf16[16,4096]{1,0:T(8,128)(2,1)S(1)}, bf16[16,4096]{1,0:T(8,128)(2,1)S(1)}, bf16[16,4096]{1,0:T(8,128)(2,1)S(1)}, bf16[16,4096]{1,0:T(8,128)(2,1)S(1)}) custom-call(bf16[8,80,256]{2,1,0:T(8,128)(2,1)S(1)} %collective-permute-done.refs_0_, bf16[64,96]{1,0:T(8,128)(2,1)S(1)} %get-tuple-element.37.refs_1_.refs_2_, ...), custom_call_target="tpu_custom_call" | custom-call | flops 50331648 | bytes 2097152 | tf_op jit(solution)/shard_map/halo_plane/pallas_call | solution.py:266
  8.4 0.0 copy-start.1
  8.4 0.0 copy-start.2
  8.4 0.2 collective-permute-start.4
  8.6 1.2 %collective-permute-done.2.refs_1_ = bf16[8,48,256]{2,1,0:T(8,128)(2,1)S(1)} collective-permute-done((bf16[8,48,256]{2,1,0:T(8,128)(2,1)S(1)}, bf16[8,48,256]{2,1,0:T(8,128)(2,1)S(1)}, u32[]{:S(2)}, u32[]{:S(2)}) %collective-permute-start.2) | collective-permute-done | bytes 196640 | tf_op jit(solution)/shard_map/ppermute | solution.py:30
  9.8 0.6 %halo_plane.3 = (bf16[16,4096]{1,0:T(8,128)(2,1)S(1)}, bf16[16,4096]{1,0:T(8,128)(2,1)S(1)}, bf16[16,4096]{1,0:T(8,128)(2,1)S(1)}, bf16[16,4096]{1,0:T(8,128)(2,1)S(1)}) custom-call(bf16[8,80,256]{2,1,0:T(8,128)(2,1)S(1)} %collective-permute-done.refs_0_, bf16[8,48,256]{2,1,0:T(8,128)(2,1)S(1)} %collective-permute-done.2.refs_1_, ...), custom_call_target="tpu_custom_call" | custom-call | flops 50331648 | bytes 2097152 | tf_op jit(solution)/shard_map/halo_plane/pallas_call | solution.py:266
  10.5 2.4 %collective-permute-start.3 = (bf16[16,4096]{1,0:T(8,128)(2,1)S(1)}, bf16[16,4096]{1,0:T(8,128)(2,1)S(1)}, u32[]{:S(2)}, u32[]{:S(2)}) collective-permute-start(bf16[16,4096]{1,0:T(8,128)(2,1)S(1)} %get-tuple-element.38), channel_id=1, source_target_pairs={{0,1},{2,0},{3,2},{1,3},{4,5},{6,4},{7,6},{5,7},{8,9},{10,8},{11,1... | collective-permute-start | bytes 393224 | tf_op jit(solution)/shard_map/ppermute | solution.py:30
  12.8 0.3 collective-permute-done.4
  13.2 0.1 collective-permute-start.5
  13.3 0.2 copy.12
  13.5 2.4 %collective-permute-start.1 = (bf16[16,4096]{1,0:T(8,128)(2,1)S(1)}, bf16[16,4096]{1,0:T(8,128)(2,1)S(1)}, u32[]{:S(2)}, u32[]{:S(2)}) collective-permute-start(bf16[16,4096]{1,0:T(8,128)(2,1)S(1)} %get-tuple-element.36), channel_id=1, source_target_pairs={{0,1},{2,0},{3,2},{1,3},{4,5},{6,4},{7,6},{5,7},{8,9},{10,8},{11,1... | collective-permute-start | bytes 393224 | tf_op jit(solution)/shard_map/ppermute | solution.py:30
  15.9 0.2 collective-permute-start.6
  16.1 0.4 collective-permute-done.3
  16.5 2.9 %collective-permute-done.5.refs_2_ = bf16[16,4096]{1,0:T(8,128)(2,1)S(1)} collective-permute-done((bf16[16,4096]{1,0:T(8,128)(2,1)S(1)}, bf16[16,4096]{1,0:T(8,128)(2,1)S(1)}, u32[]{:S(2)}, u32[]{:S(2)}) %collective-permute-start.5) | collective-permute-done | bytes 131104 | tf_op jit(solution)/shard_map/ppermute | solution.py:30
  19.4 1.1 %collective-permute-start.7 = (bf16[16,4096]{1,0:T(8,128)(2,1)S(1)}, bf16[16,4096]{1,0:T(8,128)(2,1)S(1)}, u32[]{:S(2)}, u32[]{:S(2)}) collective-permute-start(bf16[16,4096]{1,0:T(8,128)(2,1)S(1)} %add_convert_fusion), channel_id=1, source_target_pairs={{0,1},{2,0},{3,2},{1,3},{4,5},{6,4},{7,6},{5,7},{8,9},{10,8},{11,1... | collective-permute-start | bytes 393224 | tf_op jit(solution)/shard_map/ppermute | solution.py:30
  20.4 3.0 %collective-permute-done.1.refs_1_ = bf16[16,4096]{1,0:T(8,128)(2,1)S(1)} collective-permute-done((bf16[16,4096]{1,0:T(8,128)(2,1)S(1)}, bf16[16,4096]{1,0:T(8,128)(2,1)S(1)}, u32[]{:S(2)}, u32[]{:S(2)}) %collective-permute-start.1) | collective-permute-done | bytes 131104 | tf_op jit(solution)/shard_map/ppermute | solution.py:30
  23.4 0.1 broadcast_in_dim.2.refs_3_
  23.5 0.2 activation.2
  23.8 0.1 collective-permute-start.9
  23.8 3.3 %collective-permute-start.10 = (bf16[16,4096]{1,0:T(8,128)(2,1)S(1)}, bf16[16,4096]{1,0:T(8,128)(2,1)S(1)}, u32[]{:S(2)}, u32[]{:S(2)}) collective-permute-start(bf16[16,4096]{1,0:T(8,128)(2,1)S(1)} %get-tuple-element.54.refs_3_.refs_5_), channel_id=1, source_target_pairs={{0,1},{2,0},{3,2},{1,3},{4,5},{6,4},{7,6},{5,7},{8,9},{10,8},{11,1... | collective-permute-start | bytes 393224 | tf_op jit(solution)/shard_map/ppermute | solution.py:30
  27.1 0.0 collective-permute-done.6.refs_1_
  27.1 2.0 %collective-permute-done.7.refs_2_ = bf16[16,4096]{1,0:T(8,128)(2,1)S(1)} collective-permute-done((bf16[16,4096]{1,0:T(8,128)(2,1)S(1)}, bf16[16,4096]{1,0:T(8,128)(2,1)S(1)}, u32[]{:S(2)}, u32[]{:S(2)}) %collective-permute-start.7) | collective-permute-done | bytes 131104 | tf_op jit(solution)/shard_map/ppermute | solution.py:30
  29.1 0.2 activation.3
  29.3 3.3 %collective-permute-start.13 = (bf16[16,4096]{1,0:T(8,128)(2,1)S(1)}, bf16[16,4096]{1,0:T(8,128)(2,1)S(1)}, u32[]{:S(2)}, u32[]{:S(2)}) collective-permute-start(bf16[16,4096]{1,0:T(8,128)(2,1)S(1)} %get-tuple-element.51.refs_9_), channel_id=1, source_target_pairs={{0,1},{2,0},{3,2},{1,3},{4,5},{6,4},{7,6},{5,7},{8,9},{10,8},{11,1... | collective-permute-start | bytes 393224 | tf_op jit(solution)/shard_map/ppermute | solution.py:30
  32.6 0.0 collective-permute-start.12
  32.6 2.9 %collective-permute-start.8 = (bf16[16,8192]{1,0:T(8,128)(2,1)S(1)}, bf16[16,8192]{1,0:T(8,128)(2,1)S(1)}, u32[]{:S(2)}, u32[]{:S(2)}) collective-permute-start(bf16[16,8192]{1,0:T(8,128)(2,1)S(1)} %pad_maximum_fusion.1), channel_id=1, source_target_pairs={{0,28},{4,0},{8,4},{12,8},{16,12},{20,16},{24,20},{28,24},{1,29},{... | collective-permute-start | bytes 786440 | tf_op jit(solution)/shard_map/ppermute | solution.py:30
  35.6 0.0 collective-permute-done.9.refs_4_.refs_6_
  35.6 0.0 collective-permute-done.10.refs_6_.refs_8_
  35.6 1.2 %collective-permute-start.15 = (bf16[16,4096]{1,0:T(8,128)(2,1)S(1)}, bf16[16,4096]{1,0:T(8,128)(2,1)S(1)}, u32[]{:S(2)}, u32[]{:S(2)}) collective-permute-start(bf16[16,4096]{1,0:T(8,128)(2,1)S(1)} %collective-permute-done.9.refs_4_.refs_6_), channel_id=1, source_target_pairs={{0,2},{2,3},{3,1},{1,0},{4,6},{6,7},{7,5},{5,4},{8,10},{10,11},{11... | collective-permute-start | bytes 393224 | tf_op jit(solution)/shard_map/ppermute | solution.py:30
  36.8 1.8 %collective-permute-start.11 = (bf16[32,4096]{1,0:T(8,128)(2,1)S(1)}, bf16[32,4096]{1,0:T(8,128)(2,1)S(1)}, u32[]{:S(2)}, u32[]{:S(2)}) collective-permute-start(bf16[32,4096]{1,0:T(8,128)(2,1)S(1)} %pad_maximum_fusion.2), channel_id=1, source_target_pairs={{0,28},{4,0},{8,4},{12,8},{16,12},{20,16},{24,20},{28,24},{1,29},{... | collective-permute-start | bytes 786440 | tf_op jit(solution)/shard_map/ppermute | solution.py:30
  38.6 2.8 %collective-permute-start.17 = (bf16[16,4096]{1,0:T(8,128)(2,1)S(1)}, bf16[16,4096]{1,0:T(8,128)(2,1)S(1)}, u32[]{:S(2)}, u32[]{:S(2)}) collective-permute-start(bf16[16,4096]{1,0:T(8,128)(2,1)S(1)} %collective-permute-done.13.refs_12_), channel_id=1, source_target_pairs={{0,1},{2,0},{3,2},{1,3},{4,5},{6,4},{7,6},{5,7},{8,9},{10,8},{11,1... | collective-permute-start | bytes 393224 | tf_op jit(solution)/shard_map/ppermute | solution.py:30
  41.4 5.1 %collective-permute-start.14 = (bf16[32,4096]{1,0:T(8,128)(2,1)S(1)}, bf16[32,4096]{1,0:T(8,128)(2,1)S(1)}, u32[]{:S(2)}, u32[]{:S(2)}) collective-permute-start(bf16[32,4096]{1,0:T(8,128)(2,1)S(1)} %pad_maximum_fusion.3), channel_id=1, source_target_pairs={{0,28},{4,0},{8,4},{12,8},{16,12},{20,16},{24,20},{28,24},{1,29},{... | collective-permute-start | bytes 786440 | tf_op jit(solution)/shard_map/ppermute | solution.py:30
  46.5 0.1 collective-permute-start.16
  46.5 2.4 %collective-permute-start.18 = (bf16[16,4096]{1,0:T(8,128)(2,1)S(1)}, bf16[16,4096]{1,0:T(8,128)(2,1)S(1)}, u32[]{:S(2)}, u32[]{:S(2)}) collective-permute-start(bf16[16,4096]{1,0:T(8,128)(2,1)S(1)} %collective-permute-done.17.refs_11_), channel_id=1, source_target_pairs={{0,28},{4,0},{8,4},{12,8},{16,12},{20,16},{24,20},{28,24},{1,29},{... | collective-permute-start | bytes 393224 | tf_op jit(solution)/shard_map/ppermute | solution.py:30
  48.9 0.8 %copy.10 = bf16[2,8,64,128]{3,2,1,0:T(8,128)(2,1)} copy(bf16[2,8,64,128]{3,1,2,0:T(8,128)(2,1)S(1)} %maximum_bitcast_fusion) | data formatting | bytes 524288
  49.7 3.6 %collective-permute-done.16.refs_2_.refs_3_ = bf16[16,4096]{1,0:T(8,128)(2,1)S(1)} collective-permute-done((bf16[16,4096]{1,0:T(8,128)(2,1)S(1)}, bf16[16,4096]{1,0:T(8,128)(2,1)S(1)}, u32[]{:S(2)}, u32[]{:S(2)}) %collective-permute-start.16) | collective-permute-done | bytes 131104 | tf_op jit(solution)/shard_map/ppermute | solution.py:30
  53.3 0.0 collective-permute-done.11.refs_1_
  53.3 0.8 %lower_grad.1.refs_14_ = bf16[8,2,48,256]{3,2,1,0:T(8,128)(2,1)S(1)} custom-call(bf16[16,8192]{1,0:T(8,128)(2,1)S(1)} %collective-permute-done.8.refs_0_, bf16[32,4096]{1,0:T(8,128)(2,1)S(1)} %collective-permute-done.11.refs_1_, bf16[16,4096]{1,0:T(8,128)(2,1)S(1)} %collective-permute-done.16.refs_2_.refs_3_, ...), custom_call_target="tpu_custom_call" | custom-call | flops 150994944 | bytes 1048576 | tf_op jit(solution)/shard_map/lower_grad/pallas_call | solution.py:266
  54.1 0.6 %collective-permute-done.18.refs_4_ = bf16[16,4096]{1,0:T(8,128)(2,1)S(1)} collective-permute-done((bf16[16,4096]{1,0:T(8,128)(2,1)S(1)}, bf16[16,4096]{1,0:T(8,128)(2,1)S(1)}, u32[]{:S(2)}, u32[]{:S(2)}) %collective-permute-start.18) | collective-permute-done | bytes 131104 | tf_op jit(solution)/shard_map/ppermute | solution.py:30
  54.7 0.0 collective-permute-done.14.refs_2_
  54.7 1.8 %upper_grad.1 = bf16[8,2,128,256]{3,2,1,0:T(8,128)(2,1)} custom-call(bf16[16,8192]{1,0:T(8,128)(2,1)S(1)} %collective-permute-done.8.refs_0_, bf16[32,4096]{1,0:T(8,128)(2,1)S(1)} %collective-permute-done.11.refs_1_, bf16[32,4096]{1,0:T(8,128)(2,1)S(1)} %collective-permute-done.14.refs_2_, bf16[16,4096]{1,0:T(8,128)(2,1)S(1)} %collective-permute-done.16.refs_2_.refs_3_, ...), custom_call_target="tpu_custom_call" | custom-call | flops 251658240 | bytes 1048576 | tf_op jit(solution)/shard_map/upper_grad/pallas_call | solution.py:425
  (20 shorter events, 0.2 us)
Async XLA Ops:
  0.6 4.2 %copy-start = (bf16[8,2,128,256]{3,2,1,0:T(8,128)(2,1)S(1)}, bf16[8,2,128,256]{3,2,1,0:T(8,128)(2,1)}, u32[]{:S(2)}) copy-start(bf16[8,2,128,256]{3,2,1,0:T(8,128)(2,1)} %field_ref.1) | copy-start | bytes 3145732
  1.9 5.8 %collective-permute-start = (bf16[8,80,256]{2,1,0:T(8,128)(2,1)S(1)}, bf16[8,80,256]{2,1,0:T(8,128)(2,1)S(1)}, u32[]{:S(2)}, u32[]{:S(2)}) collective-permute-start(bf16[8,80,256]{2,1,0:T(8,128)(2,1)S(1)} %pad_maximum_fusion), channel_id=1, source_target_pairs={{0,4},{4,8},{8,12},{12,16},{16,20},{20,24},{24,28},{28,0},{1,5},{5... | collective-permute-start | bytes 983048 | tf_op jit(solution)/shard_map/ppermute | solution.py:30
  3.7 6.1 %collective-permute-start.2 = (bf16[8,48,256]{2,1,0:T(8,128)(2,1)S(1)}, bf16[8,48,256]{2,1,0:T(8,128)(2,1)S(1)}, u32[]{:S(2)}, u32[]{:S(2)}) collective-permute-start(bf16[8,48,256]{2,1,0:T(8,128)(2,1)S(1)} %slice.26), channel_id=1, source_target_pairs={{0,4},{4,8},{8,12},{12,16},{16,20},{20,24},{24,28},{28,0},{1,5},{5... | collective-permute-start | bytes 589832 | tf_op jit(solution)/shard_map/ppermute | solution.py:30
  8.4 4.9 %copy-start.1 = (bf16[16,1,64,128]{3,2,1,0:T(8,128)(2,1)S(1)}, bf16[16,1,64,128]{3,2,1,0:T(8,128)(2,1)}, u32[]{:S(2)}) copy-start(bf16[16,1,64,128]{3,2,1,0:T(8,128)(2,1)} %param.7) | copy-start | bytes 786436
  8.4 15.0 %copy-start.2 = (f32[16]{0:T(128)S(1)}, f32[16]{0:T(128)}, u32[]{:S(2)}) copy-start(f32[16]{0:T(128)} %param.6) | copy-start | bytes 196
  8.4 4.8 %collective-permute-start.4 = (bf16[16,4096]{1,0:T(8,128)(2,1)S(1)}, bf16[16,4096]{1,0:T(8,128)(2,1)S(1)}, u32[]{:S(2)}, u32[]{:S(2)}) collective-permute-start(bf16[16,4096]{1,0:T(8,128)(2,1)S(1)} %get-tuple-element.40), channel_id=1, source_target_pairs={{0,2},{2,3},{3,1},{1,0},{4,6},{6,7},{7,5},{5,4},{8,10},{10,11},{11... | collective-permute-start | bytes 393224 | tf_op jit(solution)/shard_map/ppermute | solution.py:30
  10.5 6.0 %collective-permute-start.3 = (bf16[16,4096]{1,0:T(8,128)(2,1)S(1)}, bf16[16,4096]{1,0:T(8,128)(2,1)S(1)}, u32[]{:S(2)}, u32[]{:S(2)}) collective-permute-start(bf16[16,4096]{1,0:T(8,128)(2,1)S(1)} %get-tuple-element.38), channel_id=1, source_target_pairs={{0,1},{2,0},{3,2},{1,3},{4,5},{6,4},{7,6},{5,7},{8,9},{10,8},{11,1... | collective-permute-start | bytes 393224 | tf_op jit(solution)/shard_map/ppermute | solution.py:30
  13.2 6.1 %collective-permute-start.5 = (bf16[16,4096]{1,0:T(8,128)(2,1)S(1)}, bf16[16,4096]{1,0:T(8,128)(2,1)S(1)}, u32[]{:S(2)}, u32[]{:S(2)}) collective-permute-start(bf16[16,4096]{1,0:T(8,128)(2,1)S(1)} %add_convert_fusion.1), channel_id=1, source_target_pairs={{0,2},{2,3},{3,1},{1,0},{4,6},{6,7},{7,5},{5,4},{8,10},{10,11},{11... | collective-permute-start | bytes 393224 | tf_op jit(solution)/shard_map/ppermute | solution.py:30
  13.5 10.0 %collective-permute-start.1 = (bf16[16,4096]{1,0:T(8,128)(2,1)S(1)}, bf16[16,4096]{1,0:T(8,128)(2,1)S(1)}, u32[]{:S(2)}, u32[]{:S(2)}) collective-permute-start(bf16[16,4096]{1,0:T(8,128)(2,1)S(1)} %get-tuple-element.36), channel_id=1, source_target_pairs={{0,1},{2,0},{3,2},{1,3},{4,5},{6,4},{7,6},{5,7},{8,9},{10,8},{11,1... | collective-permute-start | bytes 393224 | tf_op jit(solution)/shard_map/ppermute | solution.py:30
  15.9 11.3 %collective-permute-start.6 = (bf16[16,4096]{1,0:T(8,128)(2,1)S(1)}, bf16[16,4096]{1,0:T(8,128)(2,1)S(1)}, u32[]{:S(2)}, u32[]{:S(2)}) collective-permute-start(bf16[16,4096]{1,0:T(8,128)(2,1)S(1)} %get-tuple-element.46), channel_id=1, source_target_pairs={{0,2},{2,3},{3,1},{1,0},{4,6},{6,7},{7,5},{5,4},{8,10},{10,11},{11... | collective-permute-start | bytes 393224 | tf_op jit(solution)/shard_map/ppermute | solution.py:30
  19.4 9.7 %collective-permute-start.7 = (bf16[16,4096]{1,0:T(8,128)(2,1)S(1)}, bf16[16,4096]{1,0:T(8,128)(2,1)S(1)}, u32[]{:S(2)}, u32[]{:S(2)}) collective-permute-start(bf16[16,4096]{1,0:T(8,128)(2,1)S(1)} %add_convert_fusion), channel_id=1, source_target_pairs={{0,1},{2,0},{3,2},{1,3},{4,5},{6,4},{7,6},{5,7},{8,9},{10,8},{11,1... | collective-permute-start | bytes 393224 | tf_op jit(solution)/shard_map/ppermute | solution.py:30
  23.8 11.8 %collective-permute-start.9 = (bf16[16,4096]{1,0:T(8,128)(2,1)S(1)}, bf16[16,4096]{1,0:T(8,128)(2,1)S(1)}, u32[]{:S(2)}, u32[]{:S(2)}) collective-permute-start(bf16[16,4096]{1,0:T(8,128)(2,1)S(1)} %get-tuple-element.54.refs_3_.refs_5_), channel_id=1, source_target_pairs={{0,2},{2,3},{3,1},{1,0},{4,6},{6,7},{7,5},{5,4},{8,10},{10,11},{11... | collective-permute-start | bytes 393224 | tf_op jit(solution)/shard_map/ppermute | solution.py:30
  23.8 11.8 %collective-permute-start.10 = (bf16[16,4096]{1,0:T(8,128)(2,1)S(1)}, bf16[16,4096]{1,0:T(8,128)(2,1)S(1)}, u32[]{:S(2)}, u32[]{:S(2)}) collective-permute-start(bf16[16,4096]{1,0:T(8,128)(2,1)S(1)} %get-tuple-element.54.refs_3_.refs_5_), channel_id=1, source_target_pairs={{0,1},{2,0},{3,2},{1,3},{4,5},{6,4},{7,6},{5,7},{8,9},{10,8},{11,1... | collective-permute-start | bytes 393224 | tf_op jit(solution)/shard_map/ppermute | solution.py:30
  29.3 9.3 %collective-permute-start.13 = (bf16[16,4096]{1,0:T(8,128)(2,1)S(1)}, bf16[16,4096]{1,0:T(8,128)(2,1)S(1)}, u32[]{:S(2)}, u32[]{:S(2)}) collective-permute-start(bf16[16,4096]{1,0:T(8,128)(2,1)S(1)} %get-tuple-element.51.refs_9_), channel_id=1, source_target_pairs={{0,1},{2,0},{3,2},{1,3},{4,5},{6,4},{7,6},{5,7},{8,9},{10,8},{11,1... | collective-permute-start | bytes 393224 | tf_op jit(solution)/shard_map/ppermute | solution.py:30
  32.6 8.7 %collective-permute-start.12 = (bf16[16,4096]{1,0:T(8,128)(2,1)S(1)}, bf16[16,4096]{1,0:T(8,128)(2,1)S(1)}, u32[]{:S(2)}, u32[]{:S(2)}) collective-permute-start(bf16[16,4096]{1,0:T(8,128)(2,1)S(1)} %get-tuple-element.51.refs_9_), channel_id=1, source_target_pairs={{0,2},{2,3},{3,1},{1,0},{4,6},{6,7},{7,5},{5,4},{8,10},{10,11},{11... | collective-permute-start | bytes 393224 | tf_op jit(solution)/shard_map/ppermute | solution.py:30
  32.6 20.7 %collective-permute-start.8 = (bf16[16,8192]{1,0:T(8,128)(2,1)S(1)}, bf16[16,8192]{1,0:T(8,128)(2,1)S(1)}, u32[]{:S(2)}, u32[]{:S(2)}) collective-permute-start(bf16[16,8192]{1,0:T(8,128)(2,1)S(1)} %pad_maximum_fusion.1), channel_id=1, source_target_pairs={{0,28},{4,0},{8,4},{12,8},{16,12},{20,16},{24,20},{28,24},{1,29},{... | collective-permute-start | bytes 786440 | tf_op jit(solution)/shard_map/ppermute | solution.py:30
  35.6 10.9 %collective-permute-start.15 = (bf16[16,4096]{1,0:T(8,128)(2,1)S(1)}, bf16[16,4096]{1,0:T(8,128)(2,1)S(1)}, u32[]{:S(2)}, u32[]{:S(2)}) collective-permute-start(bf16[16,4096]{1,0:T(8,128)(2,1)S(1)} %collective-permute-done.9.refs_4_.refs_6_), channel_id=1, source_target_pairs={{0,2},{2,3},{3,1},{1,0},{4,6},{6,7},{7,5},{5,4},{8,10},{10,11},{11... | collective-permute-start | bytes 393224 | tf_op jit(solution)/shard_map/ppermute | solution.py:30
  36.8 16.6 %collective-permute-start.11 = (bf16[32,4096]{1,0:T(8,128)(2,1)S(1)}, bf16[32,4096]{1,0:T(8,128)(2,1)S(1)}, u32[]{:S(2)}, u32[]{:S(2)}) collective-permute-start(bf16[32,4096]{1,0:T(8,128)(2,1)S(1)} %pad_maximum_fusion.2), channel_id=1, source_target_pairs={{0,28},{4,0},{8,4},{12,8},{16,12},{20,16},{24,20},{28,24},{1,29},{... | collective-permute-start | bytes 786440 | tf_op jit(solution)/shard_map/ppermute | solution.py:30
  38.6 7.9 %collective-permute-start.17 = (bf16[16,4096]{1,0:T(8,128)(2,1)S(1)}, bf16[16,4096]{1,0:T(8,128)(2,1)S(1)}, u32[]{:S(2)}, u32[]{:S(2)}) collective-permute-start(bf16[16,4096]{1,0:T(8,128)(2,1)S(1)} %collective-permute-done.13.refs_12_), channel_id=1, source_target_pairs={{0,1},{2,0},{3,2},{1,3},{4,5},{6,4},{7,6},{5,7},{8,9},{10,8},{11,1... | collective-permute-start | bytes 393224 | tf_op jit(solution)/shard_map/ppermute | solution.py:30
  41.4 13.4 %collective-permute-start.14 = (bf16[32,4096]{1,0:T(8,128)(2,1)S(1)}, bf16[32,4096]{1,0:T(8,128)(2,1)S(1)}, u32[]{:S(2)}, u32[]{:S(2)}) collective-permute-start(bf16[32,4096]{1,0:T(8,128)(2,1)S(1)} %pad_maximum_fusion.3), channel_id=1, source_target_pairs={{0,28},{4,0},{8,4},{12,8},{16,12},{20,16},{24,20},{28,24},{1,29},{... | collective-permute-start | bytes 786440 | tf_op jit(solution)/shard_map/ppermute | solution.py:30
  46.5 6.9 %collective-permute-start.16 = (bf16[16,4096]{1,0:T(8,128)(2,1)S(1)}, bf16[16,4096]{1,0:T(8,128)(2,1)S(1)}, u32[]{:S(2)}, u32[]{:S(2)}) collective-permute-start(bf16[16,4096]{1,0:T(8,128)(2,1)S(1)} %collective-permute-done.15.refs_5_.refs_7_), channel_id=1, source_target_pairs={{0,28},{4,0},{8,4},{12,8},{16,12},{20,16},{24,20},{28,24},{1,29},{... | collective-permute-start | bytes 393224 | tf_op jit(solution)/shard_map/ppermute | solution.py:30
  46.5 8.2 %collective-permute-start.18 = (bf16[16,4096]{1,0:T(8,128)(2,1)S(1)}, bf16[16,4096]{1,0:T(8,128)(2,1)S(1)}, u32[]{:S(2)}, u32[]{:S(2)}) collective-permute-start(bf16[16,4096]{1,0:T(8,128)(2,1)S(1)} %collective-permute-done.17.refs_11_), channel_id=1, source_target_pairs={{0,28},{4,0},{8,4},{12,8},{16,12},{20,16},{24,20},{28,24},{1,29},{... | collective-permute-start | bytes 393224 | tf_op jit(solution)/shard_map/ppermute | solution.py:30
